TPU v7x, 128 devices: a whole 4x4x4 slice. The times are simulated.
128 devices in a mesh: shard: 8 (over x, y_lo), ctx: 2 (over y_hi), tp: 8 (over z, core).
Axes of the slice: x: 4, y: 4 (y_hi: 2, y_lo: 2; y = y_hi * 2 + y_lo), z: 4, core: 2. Of those that a mesh axis runs over, the one named last changes fastest.
Arguments:
- tokens: bfloat16 [8, 1024, 2048], P('shard', 'ctx'), may hold values from -6 to 6
- out_grad: bfloat16 [8, 1024, 2048], P('shard', 'ctx'), may hold values from -6 to 6
- segments: int32 [8, 1024], P('shard'), may hold values from 0 to 4, as said below
- routes: int32 [8, 1024, 8], P('shard', 'ctx'), may hold values from 0 to 15, all different within a row; in each aligned block of 512 rows (0 to 511, 512 to 1023, ..., all dimensions but the last counted through in order) at most 288 rows name the same one
- query_weight: bfloat16 [2048, 2048], P('shard', 'tp'), may hold values from -0.125 to 0.125
- key_weight: bfloat16 [2048, 2048], P('shard', 'tp'), may hold values from -0.125 to 0.125
- value_weight: bfloat16 [2048, 2048], P('shard', 'tp'), may hold values from -0.125 to 0.125
- out_weight: bfloat16 [2048, 2048], P('tp', 'shard'), may hold values from -0.5 to 0.5
- router_weight: bfloat16 [2048, 16], P('shard'), may hold values from -0.0625 to 0.0625
- attn_gain: bfloat16 [2048], P('shard'), may hold values from 0.099609375 to 1.8984375
- moe_gain: bfloat16 [2048], P('shard'), may hold values from 0.099609375 to 1.8984375
- query_gain: bfloat16 [16, 128], P('tp', 'shard'), may hold values from 0.099609375 to 1.8984375
- key_gain: bfloat16 [16, 128], P('tp', 'shard'), may hold values from 0.099609375 to 1.8984375
- gate_weight: bfloat16 [16, 2048, 1024], P(None, 'shard', 'tp'), may hold values from -0.125 to 0.125
- up_weight: bfloat16 [16, 2048, 1024], P(None, 'shard', 'tp'), may hold values from -0.125 to 0.125
- down_weight: bfloat16 [16, 1024, 2048], P(None, 'tp', 'shard'), may hold values from -0.75 to 0.75
Outputs:
- layer_out: bfloat16 [8, 1024, 2048], P('shard', 'ctx')
- input_grad: bfloat16 [8, 1024, 2048], P('shard', 'ctx')
- query_weight_grad: float32 [2048, 2048], P('shard', 'tp')
- key_weight_grad: float32 [2048, 2048], P('shard', 'tp')
- value_weight_grad: float32 [2048, 2048], P('shard', 'tp')
- out_weight_grad: float32 [2048, 2048], P('tp', 'shard')
- router_weight_grad: float32 [2048, 16], P('shard')
- attn_gain_grad: float32 [2048], P('shard')
- moe_gain_grad: float32 [2048], P('shard')
- query_gain_grad: float32 [16, 128], P('tp', 'shard')
- key_gain_grad: float32 [16, 128], P('tp', 'shard')
- gate_weight_grad: float32 [16, 2048, 1024], P(None, 'shard', 'tp')
- up_weight_grad: float32 [16, 2048, 1024], P(None, 'shard', 'tp')
- down_weight_grad: float32 [16, 1024, 2048], P(None, 'tp', 'shard')
Inputs may be any that keep to these rules, and one draw needn't show every extreme that they name: `segments`: segment numbers start at 0, never fall along a sequence and rise by one from document to document; every sequence holds exactly five documents, one of them exactly 768 positions long, the other four sharing the remaining 1024 - 768 positions, each at least one eighth of them. `routes`: each token names 8 different experts; within the 512 positions of one block of one sequence no expert is named by more than 288 tokens, and in some blocks one expert is named by exactly 288.
All inputs are finite; a program needn't handle non-finite values.
Results may differ from a plain program's by a relative error of at most 0.035.
Values may be sent and summed in bfloat16 or wider, within the bound.
A program may use at most 384 MiB of HBM per device.

v0:
```python
import jax
import jax.numpy as jnp
from jax import lax
from jax.sharding import PartitionSpec as P

EPSILON = 1e-05
ROPE_BASE = 10000.0
MASKED_SCORE = -1e30


def rms_scale(values):
    return lax.rsqrt(jnp.mean(values * values, axis=-1, keepdims=True) + EPSILON)


def norm_back(grad_normed, source, scale_row, gain_row):
    unit_values = source * scale_row
    grad_unit = grad_normed * gain_row
    grad_source = scale_row * (
        grad_unit - unit_values * jnp.mean(grad_unit * unit_values, axis=-1, keepdims=True)
    )
    return (grad_source, grad_normed * unit_values)


def rope_tables(positions, head_width):
    frequency = ROPE_BASE ** (-(jnp.arange(0, head_width, 2, dtype=jnp.float32) / head_width))
    angles = positions.astype(jnp.float32)[:, None] * frequency[None, :]
    return (jnp.cos(angles), jnp.sin(angles))


def rotate(values, cosine, sine_table):
    half_width = values.shape[-1] // 2
    first_half = values[..., :half_width]
    second_half = values[..., half_width:]
    return jnp.concatenate(
        [
            first_half * cosine - second_half * sine_table,
            second_half * cosine + first_half * sine_table,
        ],
        axis=-1,
    )


def rounded(values):
    return lax.optimization_barrier(values.astype(jnp.bfloat16)).astype(jnp.float32)


def silu_parts(preact):
    logistic = jax.nn.sigmoid(preact)
    return (preact * logistic, logistic * (1.0 + preact * (1.0 - logistic)))


def body(
    tokens,
    out_grad,
    segments,
    routes,
    query_weight,
    key_weight,
    value_weight,
    out_weight,
    router_weight,
    attn_gain,
    moe_gain,
    query_gain,
    key_gain,
    gate_weight,
    up_weight,
    down_weight,
):
    seq_count, local_rows, model_width = tokens.shape
    heads_local = query_gain.shape[0]
    experts = gate_weight.shape[0]
    top_count = routes.shape[2]
    capacity = local_rows * 9 // 16
    row_count = seq_count * local_rows
    slot_count = seq_count * experts * capacity
    full_length = segments.shape[1]
    w_query, w_key, w_value, w_out, w_router, gain_one, gain_two, gain_query, gain_key = (
        lax.all_gather(query_weight, "shard", axis=0, tiled=True),
        lax.all_gather(key_weight, "shard", axis=0, tiled=True),
        lax.all_gather(value_weight, "shard", axis=0, tiled=True),
        lax.all_gather(out_weight, "shard", axis=1, tiled=True),
        lax.all_gather(router_weight, "shard", axis=0, tiled=True),
        lax.all_gather(attn_gain, "shard", axis=0, tiled=True),
        lax.all_gather(moe_gain, "shard", axis=0, tiled=True),
        lax.all_gather(query_gain, "shard", axis=1, tiled=True),
        lax.all_gather(key_gain, "shard", axis=1, tiled=True),
    )
    gate_full, up_full, down_full = (
        lax.all_gather(gate_weight, "shard", axis=1, tiled=True),
        lax.all_gather(up_weight, "shard", axis=1, tiled=True),
        lax.all_gather(down_weight, "shard", axis=2, tiled=True),
    )
    head_dim = gain_query.shape[1]
    local_width = heads_local * head_dim
    score_scale = head_dim ** (-0.5)
    inputs = tokens.reshape(row_count, model_width).astype(jnp.float32)
    scale_one = rms_scale(inputs)
    attn_gains = gain_one.astype(jnp.float32)
    normed = (inputs * scale_one * attn_gains).astype(jnp.bfloat16)
    w_stacked = jnp.concatenate([w_query, w_key, w_value], axis=1)
    projected = jnp.dot(normed, w_stacked, preferred_element_type=jnp.float32)
    head_shape = (seq_count, local_rows, heads_local, head_dim)
    query_pre = projected[:, :local_width].reshape(head_shape)
    key_pre = projected[:, local_width : 2 * local_width].reshape(head_shape)
    value_low = projected[:, 2 * local_width :].reshape(head_shape).astype(jnp.bfloat16)
    query_gains = gain_query.astype(jnp.float32)
    key_gains = gain_key.astype(jnp.float32)
    scale_query = rms_scale(query_pre)
    scale_key = rms_scale(key_pre)
    first_row = lax.axis_index("ctx") * local_rows
    query_places = first_row + jnp.arange(local_rows, dtype=jnp.int32)
    cosine, sine_table = rope_tables(query_places, head_dim)
    cosine = cosine[None, :, None, :]
    sine_table = sine_table[None, :, None, :]
    query_low = rotate(query_pre * scale_query * query_gains, cosine, sine_table).astype(
        jnp.bfloat16
    )
    key_low = rotate(key_pre * scale_key * key_gains, cosine, sine_table).astype(jnp.bfloat16)
    keys_all, values_all = (
        lax.all_gather(key_low, "ctx", axis=1, tiled=True),
        lax.all_gather(value_low, "ctx", axis=1, tiled=True),
    )
    key_places = jnp.arange(full_length, dtype=jnp.int32)
    query_segments = lax.dynamic_slice_in_dim(segments, first_row, local_rows, 1)
    allowed = (query_places[None, :, None] >= key_places[None, None, :]) & (
        query_segments[:, :, None] == segments[:, None, :]
    )
    allowed = allowed[:, None]

    def masked_scores():
        raw_scores = (
            jnp.einsum("sqhd,skhd->shqk", query_low, keys_all, preferred_element_type=jnp.float32)
            * score_scale
        )
        return jnp.where(allowed, raw_scores, MASKED_SCORE)

    scores = masked_scores()
    row_peak = jnp.max(scores, axis=-1, keepdims=True)
    exponents = jnp.exp(scores - row_peak)
    row_total = jnp.sum(exponents, axis=-1, keepdims=True)
    attn_probs = exponents / row_total
    log_total = row_peak + jnp.log(row_total)
    mixed_low = (
        jnp.einsum(
            "shqk,skhd->sqhd",
            attn_probs.astype(jnp.bfloat16),
            values_all,
            preferred_element_type=jnp.float32,
        )
        .astype(jnp.bfloat16)
        .reshape(row_count, local_width)
    )
    attn_part = jnp.dot(mixed_low, w_out, preferred_element_type=jnp.float32)
    hidden = inputs + lax.psum(attn_part.astype(jnp.bfloat16), "tp").astype(jnp.float32)
    scale_two = rms_scale(hidden)
    moe_gains = gain_two.astype(jnp.float32)
    moe_in = (hidden * scale_two * moe_gains).astype(jnp.bfloat16)
    logits = jnp.dot(moe_in, w_router, preferred_element_type=jnp.float32)
    route_rows = routes.reshape(row_count, top_count)
    picked = route_rows[:, :, None] == jnp.arange(experts, dtype=jnp.int32)[None, None, :]
    chosen = jnp.sum(jnp.where(picked, logits[:, None, :], 0.0), axis=-1)
    gate_probs = jax.nn.softmax(chosen, axis=-1)
    pick_counts = picked.astype(jnp.int32).reshape(seq_count, local_rows * top_count, experts)
    before = jnp.cumsum(pick_counts, axis=1) - pick_counts
    slot_index = jnp.sum(before * pick_counts, axis=-1).reshape(row_count, top_count)
    row_sequence = jnp.arange(row_count, dtype=jnp.int32) // local_rows
    destination = (row_sequence[:, None] * experts + route_rows) * capacity + slot_index
    flat_destination = destination.reshape(-1)
    pair_ids = jnp.arange(row_count * top_count, dtype=jnp.int32)
    source_pair = jnp.zeros((slot_count,), jnp.int32).at[flat_destination].set(pair_ids)
    filled = jnp.zeros((slot_count,), jnp.float32).at[flat_destination].set(1.0)
    source_row = source_pair // top_count
    dispatched = (moe_in[source_row] * filled[:, None].astype(jnp.bfloat16)).reshape(
        seq_count, experts, capacity, model_width
    )
    gate_pre = jnp.einsum(
        "secd,edf->secf", dispatched, gate_full, preferred_element_type=jnp.float32
    )
    up_pre = jnp.einsum("secd,edf->secf", dispatched, up_full, preferred_element_type=jnp.float32)
    silu_gate, silu_slope = silu_parts(gate_pre)
    act_low = (silu_gate * up_pre).astype(jnp.bfloat16)
    expert_out = jnp.einsum(
        "secf,efd->secd", act_low, down_full, preferred_element_type=jnp.float32
    ).reshape(slot_count, model_width)
    picked_out = expert_out[destination]
    moe_part = jnp.sum(gate_probs[:, :, None] * picked_out, axis=1)
    grad_rows = out_grad.reshape(row_count, model_width).astype(jnp.float32)
    gate_grad_part = jnp.sum(grad_rows[:, None, :] * picked_out, axis=-1)
    moe_total = lax.psum(moe_part.astype(jnp.bfloat16), "tp").astype(jnp.float32)
    layer_out = (
        (hidden + moe_total).astype(jnp.bfloat16).reshape(seq_count, local_rows, model_width)
    )
    gate_back, up_back, down_back = (gate_full, up_full, down_full)
    slot_gates = gate_probs.reshape(-1)[source_pair] * filled
    slot_grad = (
        (slot_gates[:, None] * grad_rows[source_row])
        .astype(jnp.bfloat16)
        .reshape(seq_count, experts, capacity, model_width)
    )
    act_grad = jnp.einsum(
        "secd,efd->secf", slot_grad, down_back, preferred_element_type=jnp.float32
    )
    gate_pre_grad = (act_grad * up_pre * silu_slope).astype(jnp.bfloat16)
    up_pre_grad = (act_grad * silu_gate).astype(jnp.bfloat16)
    joined_grad = jnp.concatenate([gate_pre_grad, up_pre_grad], axis=3)
    joined_weight = jnp.concatenate([gate_back, up_back], axis=2)
    slot_in_grad = jnp.einsum(
        "secf,edf->secd", joined_grad, joined_weight, preferred_element_type=jnp.float32
    )
    moe_in_part = jnp.sum(slot_in_grad.reshape(slot_count, model_width)[destination], axis=1)
    grad_gate_weight = jnp.einsum(
        "secd,secf->edf", dispatched, gate_pre_grad, preferred_element_type=jnp.float32
    )
    grad_up_weight = jnp.einsum(
        "secd,secf->edf", dispatched, up_pre_grad, preferred_element_type=jnp.float32
    )
    grad_down_weight = jnp.einsum(
        "secf,secd->efd", act_low, slot_grad, preferred_element_type=jnp.float32
    )
    moe_in_grad, gate_grad = (
        lax.psum(moe_in_part.astype(jnp.bfloat16), "tp").astype(jnp.float32),
        lax.psum(gate_grad_part.astype(jnp.bfloat16), "tp").astype(jnp.float32),
    )
    chosen_grad = gate_probs * (gate_grad - jnp.sum(gate_probs * gate_grad, axis=-1, keepdims=True))
    logit_grad = jnp.sum(jnp.where(picked, chosen_grad[:, :, None], 0.0), axis=1).astype(
        jnp.bfloat16
    )
    moe_in_grad = moe_in_grad + jnp.dot(logit_grad, w_router.T, preferred_element_type=jnp.float32)
    grad_router = jnp.dot(moe_in.T, logit_grad, preferred_element_type=jnp.float32)
    hidden_norm_grad, moe_gain_rows = norm_back(moe_in_grad, hidden, scale_two, moe_gains)
    grad_moe_gain = jnp.sum(moe_gain_rows, axis=0)
    hidden_grad = grad_rows + hidden_norm_grad
    hidden_low = hidden_grad.astype(jnp.bfloat16)
    mixed_grad = (
        jnp.dot(hidden_low, w_out.T, preferred_element_type=jnp.float32)
        .astype(jnp.bfloat16)
        .reshape(head_shape)
    )
    grad_out_weight = jnp.dot(mixed_low.T, hidden_low, preferred_element_type=jnp.float32)
    again_probs = jnp.exp(masked_scores() - log_total)
    probs_low = again_probs.astype(jnp.bfloat16)
    prob_grad = jnp.einsum(
        "sqhd,skhd->shqk", mixed_grad, values_all, preferred_element_type=jnp.float32
    )
    row_delta = jnp.sum(again_probs * prob_grad, axis=-1, keepdims=True)
    score_grad = (again_probs * (prob_grad - row_delta)).astype(jnp.bfloat16)
    query_rot_grad = rounded(
        jnp.einsum("shqk,skhd->sqhd", score_grad, keys_all, preferred_element_type=jnp.float32)
        * score_scale
    )
    key_terms = (
        jnp.einsum("shqk,sqhd->skhd", score_grad, query_low, preferred_element_type=jnp.float32)
        * score_scale
    )
    value_terms = jnp.einsum(
        "shqk,sqhd->skhd", probs_low, mixed_grad, preferred_element_type=jnp.float32
    )
    key_sum, value_sum = (
        lax.psum_scatter(
            key_terms.astype(jnp.bfloat16), "ctx", scatter_dimension=1, tiled=True
        ).astype(jnp.float32),
        lax.psum_scatter(
            value_terms.astype(jnp.bfloat16), "ctx", scatter_dimension=1, tiled=True
        ).astype(jnp.float32),
    )
    key_rot_grad = rounded(key_sum)
    value_grad = value_sum.astype(jnp.bfloat16).reshape(row_count, local_width)
    query_unit_grad = rotate(query_rot_grad, cosine, -sine_table)
    key_unit_grad = rotate(key_rot_grad, cosine, -sine_table)
    query_pre_grad, query_gain_rows = norm_back(
        query_unit_grad, query_pre, scale_query, query_gains
    )
    key_pre_grad, key_gain_rows = norm_back(key_unit_grad, key_pre, scale_key, key_gains)
    grad_query_gain = jnp.sum(query_gain_rows, axis=(0, 1))
    grad_key_gain = jnp.sum(key_gain_rows, axis=(0, 1))
    stacked_grad = jnp.concatenate(
        [
            query_pre_grad.reshape(row_count, local_width).astype(jnp.bfloat16),
            key_pre_grad.reshape(row_count, local_width).astype(jnp.bfloat16),
            value_grad,
        ],
        axis=1,
    )
    normed_part = jnp.dot(stacked_grad, w_stacked.T, preferred_element_type=jnp.float32)
    grad_stacked = jnp.dot(normed.T, stacked_grad, preferred_element_type=jnp.float32)
    normed_grad = lax.psum(normed_part.astype(jnp.bfloat16), "tp").astype(jnp.float32)
    input_norm_grad, attn_gain_rows = norm_back(normed_grad, inputs, scale_one, attn_gains)
    grad_attn_gain = jnp.sum(attn_gain_rows, axis=0)
    input_grad = (
        (hidden_grad + input_norm_grad)
        .astype(jnp.bfloat16)
        .reshape(seq_count, local_rows, model_width)
    )
    grad_query_weight = grad_stacked[:, :local_width]
    grad_key_weight = grad_stacked[:, local_width : 2 * local_width]
    grad_value_weight = grad_stacked[:, 2 * local_width :]
    pieces = (
        lax.psum_scatter(
            grad_query_weight.astype(jnp.bfloat16),
            ("shard", "ctx"),
            scatter_dimension=0,
            tiled=True,
        ).astype(jnp.float32),
        lax.psum_scatter(
            grad_key_weight.astype(jnp.bfloat16), ("shard", "ctx"), scatter_dimension=0, tiled=True
        ).astype(jnp.float32),
        lax.psum_scatter(
            grad_value_weight.astype(jnp.bfloat16),
            ("shard", "ctx"),
            scatter_dimension=0,
            tiled=True,
        ).astype(jnp.float32),
        lax.psum_scatter(
            grad_out_weight.astype(jnp.bfloat16), ("shard", "ctx"), scatter_dimension=1, tiled=True
        ).astype(jnp.float32),
        lax.psum_scatter(
            grad_router.astype(jnp.bfloat16), ("shard", "ctx"), scatter_dimension=0, tiled=True
        ).astype(jnp.float32),
        lax.psum_scatter(
            grad_attn_gain.astype(jnp.bfloat16), ("shard", "ctx"), scatter_dimension=0, tiled=True
        ).astype(jnp.float32),
        lax.psum_scatter(
            grad_moe_gain.astype(jnp.bfloat16), ("shard", "ctx"), scatter_dimension=0, tiled=True
        ).astype(jnp.float32),
        lax.psum_scatter(
            grad_query_gain.astype(jnp.bfloat16), ("shard", "ctx"), scatter_dimension=1, tiled=True
        ).astype(jnp.float32),
        lax.psum_scatter(
            grad_key_gain.astype(jnp.bfloat16), ("shard", "ctx"), scatter_dimension=1, tiled=True
        ).astype(jnp.float32),
        lax.psum_scatter(
            grad_gate_weight.astype(jnp.bfloat16), ("shard", "ctx"), scatter_dimension=1, tiled=True
        ).astype(jnp.float32),
        lax.psum_scatter(
            grad_up_weight.astype(jnp.bfloat16), ("shard", "ctx"), scatter_dimension=1, tiled=True
        ).astype(jnp.float32),
        lax.psum_scatter(
            grad_down_weight.astype(jnp.bfloat16), ("shard", "ctx"), scatter_dimension=2, tiled=True
        ).astype(jnp.float32),
    )
    summed = (
        lax.all_gather(pieces[0].astype(jnp.bfloat16), "ctx", axis=0, tiled=True).astype(
            jnp.float32
        ),
        lax.all_gather(pieces[1].astype(jnp.bfloat16), "ctx", axis=0, tiled=True).astype(
            jnp.float32
        ),
        lax.all_gather(pieces[2].astype(jnp.bfloat16), "ctx", axis=0, tiled=True).astype(
            jnp.float32
        ),
        lax.all_gather(pieces[3].astype(jnp.bfloat16), "ctx", axis=1, tiled=True).astype(
            jnp.float32
        ),
        lax.all_gather(pieces[4].astype(jnp.bfloat16), "ctx", axis=0, tiled=True).astype(
            jnp.float32
        ),
        lax.all_gather(pieces[5].astype(jnp.bfloat16), "ctx", axis=0, tiled=True).astype(
            jnp.float32
        ),
        lax.all_gather(pieces[6].astype(jnp.bfloat16), "ctx", axis=0, tiled=True).astype(
            jnp.float32
        ),
        lax.all_gather(pieces[7].astype(jnp.bfloat16), "ctx", axis=1, tiled=True).astype(
            jnp.float32
        ),
        lax.all_gather(pieces[8].astype(jnp.bfloat16), "ctx", axis=1, tiled=True).astype(
            jnp.float32
        ),
        lax.all_gather(pieces[9].astype(jnp.bfloat16), "ctx", axis=1, tiled=True).astype(
            jnp.float32
        ),
        lax.all_gather(pieces[10].astype(jnp.bfloat16), "ctx", axis=1, tiled=True).astype(
            jnp.float32
        ),
        lax.all_gather(pieces[11].astype(jnp.bfloat16), "ctx", axis=2, tiled=True).astype(
            jnp.float32
        ),
    )
    return (
        layer_out,
        input_grad,
        summed[0],
        summed[1],
        summed[2],
        summed[3],
        summed[4],
        summed[5],
        summed[6],
        summed[7],
        summed[8],
        summed[9],
        summed[10],
        summed[11],
    )


def solution(mesh):
    return jax.shard_map(
        body,
        mesh=mesh,
        in_specs=(
            P("shard", "ctx", None),
            P("shard", "ctx", None),
            P("shard", None),
            P("shard", "ctx", None),
            P("shard", "tp"),
            P("shard", "tp"),
            P("shard", "tp"),
            P("tp", "shard"),
            P("shard", None),
            P("shard"),
            P("shard"),
            P("tp", "shard"),
            P("tp", "shard"),
            P(None, "shard", "tp"),
            P(None, "shard", "tp"),
            P(None, "tp", "shard"),
        ),
        out_specs=(
            P("shard", "ctx", None),
            P("shard", "ctx", None),
            P("shard", "tp"),
            P("shard", "tp"),
            P("shard", "tp"),
            P("tp", "shard"),
            P("shard", None),
            P("shard"),
            P("shard"),
            P("tp", "shard"),
            P("tp", "shard"),
            P(None, "shard", "tp"),
            P(None, "shard", "tp"),
            P(None, "tp", "shard"),
        ),
        check_vma=False,
    )
```

profile of v0, /device:TPU:14, one launch (start us, length us, event | category | flops | bytes accessed | tf_op | source)
XLA Modules:
  0.0 2132.4 jit_solution(8556119468771221688)
XLA Ops:
  12.8 15.1 all-gather.1
  28.0 17.4 all-gather.2
  45.5 15.2 all-gather
  67.6 21.9 %all-gather.21.cloned.1.call-done = bf16[2048,256]{1,0:T(8,128)(2,1)} async-done(((bf16[256,256]{1,0:T(8,128)(2,1)}), bf16[2048,256]{1,0:T(8,128)(2,1)}) %all-gather.21.cloned.1.call-update) | async-done | bytes 1048592 | tf_op jit(solution)/shard_map/all_gather | solution.py:80
  91.8 38.2 %all-gather.23.cloned.1.call-done = bf16[2048,256]{1,0:T(8,128)(2,1)} async-done(((bf16[256,256]{1,0:T(8,128)(2,1)}), bf16[2048,256]{1,0:T(8,128)(2,1)}) %all-gather.23.cloned.1.call-update) | async-done | bytes 1048592 | tf_op jit(solution)/shard_map/all_gather | solution.py:81
  132.4 3.7 fusion.77
  147.6 14.9 all_gather.82
  162.5 14.3 all_gather.85
  182.5 3.4 convolution_convert_fusion.1
  188.6 15.1 all-gather.3
  203.7 4.6 reduce-window.6
  210.2 15.5 scatter_custom_fusion
  225.7 16.1 scatter_custom_fusion.1
  241.9 4.2 bitcast_convert_fusion
  246.1 36.2 %gather_fusion.3 = f32[4608,2048]{1,0:T(8,128)} fusion(f32[512,2048]{1,0:T(8,128)} %bitcast_convert_fusion, s32[5120]{0:T(1024)S(1)} %pad_clamp_fusion.1), kind=kCustom, calls=%fused_computation.3 | custom fusion | bytes 75515904 | tf_op jit(solution)/shard_map/gather | solution.py:197
  282.3 34.5 %all_gather.88 = bf16[2048,16]{0,1:T(8,128)(2,1)S(1)} all-gather(bf16[256,16]{0,1:T(8,128)(2,1)S(1)} %copy-done.68), channel_id=1, replica_groups=mesh['shard'=8,'ctx'=2,'tp'=8] {'shard'}, dimensions={0}, use_global_device_ids=true | all-gather | bytes 73728 | tf_op jit(solution)/shard_map/all_gather | solution.py:83
  321.5 18.5 gather_fusion
  341.7 24.1 %gather_fusion.2 = f32[4608]{0:T(1024)S(1)} fusion(f32[4096]{0:T(1024)S(1)} %div.97, s32[5120]{0:T(1024)S(1)} %pad_clamp_fusion), kind=kCustom, calls=%fused_computation.2 | custom fusion | bytes 55296 | tf_op jit(solution)/shard_map/gather | solution.py:195
  366.0 56.7 %all-gather.29.cloned.1.call-done = bf16[16,2048,128]{2,1,0:T(8,128)(2,1)} async-done(((bf16[16,256,128]{2,1,0:T(8,128)(2,1)}), bf16[16,2048,128]{2,1,0:T(8,128)(2,1)}) %all-gather.29.cloned.1.call-update) | async-done | bytes 8388624 | tf_op jit(solution)/shard_map/all_gather | solution.py:91
  422.8 12.6 fusion.10
  435.4 160.6 %all-gather.27.cloned.1.call-done = bf16[16,2048,128]{2,1,0:T(8,128)(2,1)} async-done(((bf16[16,256,128]{2,1,0:T(8,128)(2,1)}), bf16[16,2048,128]{2,1,0:T(8,128)(2,1)}) %all-gather.27.cloned.1.call-update) | async-done | bytes 8388624 | tf_op jit(solution)/shard_map/all_gather | solution.py:90
  596.0 12.7 fusion.12
  608.7 163.0 %all-gather.31.cloned.1.call-done = bf16[16,128,2048]{2,1,0:T(8,128)(2,1)} async-done(((bf16[16,128,256]{2,1,0:T(8,128)(2,1)}), bf16[16,128,2048]{2,1,0:T(8,128)(2,1)}) %all-gather.31.cloned.1.call-update) | async-done | bytes 8388624 | tf_op jit(solution)/shard_map/all_gather | solution.py:92
  771.7 19.9 fusion.45
  791.6 19.6 fusion.2
  811.2 43.6 %gather_fusion.4 = f32[4096,2048]{1,0:T(8,128)} fusion(f32[4608,2048]{1,0:T(8,128)} %bitcast.314, s32[4096]{0:T(1024)S(1)} %broadcast_clamp_fusion), kind=kCustom, calls=%fused_computation.4 | custom fusion | bytes 67125248 | tf_op jit(solution)/shard_map/gather | solution.py:211
  854.8 16.6 bitcast_reduce_fusion
  871.5 18.5 fusion.130
  890.0 43.7 %gather_fusion.1 = f32[4096,2048]{1,0:T(8,128)} fusion(f32[4608,2048]{1,0:T(8,128)} %bitcast.313, s32[4096]{0:T(1024)S(1)} %broadcast_clamp_fusion), kind=kCustom, calls=%fused_computation.1 | custom fusion | bytes 67125248 | tf_op jit(solution)/shard_map/gather | solution.py:186
  933.6 16.4 fusion
  951.0 15.7 psum.38
  969.0 4.2 multiply_reduce_fusion
  980.7 3.5 multiply_reduce_fusion.1
  988.9 18.4 fusion.24
  1007.3 12.5 copy.224
  1019.8 10.9 copy.258
  1031.9 13.9 fusion.25
  1049.9 3.1 convolution_convert_fusion.3
  1070.7 3.1 convolution_convert_fusion.2
  1080.8 14.0 fusion.28
  1094.8 116.7 %reduce-scatter.37.cloned.1.call-done = bf16[128,2048]{1,0:T(8,128)(2,1)} async-done(((bf16[2048,2048]{1,0:T(8,128)(2,1)}), bf16[128,2048]{1,0:T(8,128)(2,1)}) %reduce-scatter.37.cloned.1.call-update) | async-done | bytes 524304
  1214.0 180.7 %reduce-scatter.29.cloned.1.call-done = bf16[16,128,128]{2,1,0:T(8,128)(2,1)} async-done(((bf16[16,2048,128]{2,1,0:T(8,128)(2,1)}), bf16[16,128,128]{2,1,0:T(8,128)(2,1)}) %reduce-scatter.29.cloned.1.call-update) | async-done | bytes 524304 | tf_op jit(solution)/shard_map/reduce_scatter | solution.py:332
  1396.7 75.0 %reduce-scatter.35.cloned.1.call-done = bf16[128,16]{1,0:T(8,128)(2,1)} async-done(((bf16[2048,16]{1,0:T(8,128)(2,1)}), bf16[128,16]{1,0:T(8,128)(2,1)}) %reduce-scatter.35.cloned.1.call-update) | async-done | bytes 4112
  1472.5 5.9 all_gather.96
  1478.9 70.5 %reduce-scatter.33.cloned.1.call-done = bf16[128,256]{1,0:T(8,128)(2,1)} async-done(((bf16[2048,256]{1,0:T(8,128)(2,1)}), bf16[128,256]{1,0:T(8,128)(2,1)}) %reduce-scatter.33.cloned.1.call-update) | async-done | bytes 65552
  1550.4 6.5 all_gather.95
  1556.9 68.5 %all-reduce.14.cloned.1.call-done = (bf16[512,2048]{1,0:T(8,128)(2,1)}, bf16[512,2048]{1,0:T(8,128)(2,1)}) async-done(((bf16[512,2048]{1,0:T(8,128)(2,1)}, bf16[512,2048]{1,0:T(8,128)(2,1)}), (bf16[512,2048]{1,0:T(8,128)(2,1)}, bf16[512,2048]{1,0:T(8,128)(2,1)})) %all-reduce.14.cloned.1.call-update) | async-done | bytes 4194320 | tf_op jit(solution)/shard_map/psum | solution.py:190
  1625.4 2.9 fusion.37
  1628.3 35.8 %all-reduce.4 = (bf16[2048]{0:T(1024)(128)(2,1)S(1)}, bf16[2048]{0:T(1024)(128)(2,1)S(1)}, bf16[2,128]{1,0:T(2,128)(2,1)S(1)}, bf16[2,128]{1,0:T(2,128)(2,1)S(1)}) all-reduce(bf16[2048]{0:T(1024)(128)(2,1)S(1)} %get-tuple-element.18, ...), channel_id=9, replica_groups=mesh['shard'=8,'ctx'=2,'tp'=8] {'shard','ctx'}, use_global_device_ids=true, to_apply=%region_37.38.clone | all-reduce | flops 4608 | bytes 18432
  1664.9 5.7 all-gather.7
  1670.7 5.7 all-gather.6
  1676.4 5.7 all-gather.5
  1682.8 5.7 all-gather.4
  1690.4 13.5 reduce-scatter.27.cloned.1.call-done
  1703.9 6.6 all_gather.94
  1711.3 70.7 %reduce-scatter.25.cloned.1.call-done = bf16[128,256]{1,0:T(8,128)(2,1)} async-done(((bf16[2048,256]{1,0:T(8,128)(2,1)}), bf16[128,256]{1,0:T(8,128)(2,1)}) %reduce-scatter.25.cloned.1.call-update) | async-done | bytes 65552 | tf_op jit(solution)/shard_map/reduce_scatter | solution.py:305
  1782.0 6.6 all_gather.93
  1789.3 71.0 %reduce-scatter.23.cloned.1.call-done = bf16[128,256]{1,0:T(8,128)(2,1)} async-done(((bf16[2048,256]{1,0:T(8,128)(2,1)}), bf16[128,256]{1,0:T(8,128)(2,1)}) %reduce-scatter.23.cloned.1.call-update) | async-done | bytes 65552 | tf_op jit(solution)/shard_map/reduce_scatter | solution.py:299
  1860.3 6.6 all_gather.92
  1867.7 175.2 %reduce-scatter.31.cloned.1.call-done = bf16[16,128,128]{2,1,0:T(8,128)(2,1)} async-done(((bf16[16,2048,128]{2,1,0:T(8,128)(2,1)}), bf16[16,128,128]{2,1,0:T(8,128)(2,1)}) %reduce-scatter.31.cloned.1.call-update) | async-done | bytes 524304 | tf_op jit(solution)/shard_map/reduce_scatter | solution.py:335
  2043.0 6.6 fusion.56
  2049.6 20.2 all-gather.37.cloned.1.call-done
  2072.5 23.8 %all-gather.33.cloned.1.call-done = bf16[16,256,128]{2,1,0:T(8,128)(2,1)} async-done(((bf16[16,128,128]{2,1,0:T(8,128)(2,1)}), bf16[16,256,128]{2,1,0:T(8,128)(2,1)}) %all-gather.33.cloned.1.call-update) | async-done | bytes 1048592 | tf_op jit(solution)/shard_map/all_gather | solution.py:370
  2099.1 23.8 %all-gather.35.cloned.1.call-done = bf16[16,256,128]{2,1,0:T(8,128)(2,1)} async-done(((bf16[16,128,128]{2,1,0:T(8,128)(2,1)}), bf16[16,256,128]{2,1,0:T(8,128)(2,1)}) %all-gather.35.cloned.1.call-update) | async-done | bytes 1048592 | tf_op jit(solution)/shard_map/all_gather | solution.py:373
  (328 shorter events, 109.5 us)
Async XLA Ops:
  7.2 58.1 %all-gather.19.cloned.1.call-start = ((), (), s32[]{:S(2)}) async-start(), calls=%async_computation.10 | async-start | bytes 1179648 | tf_op jit(solution)/shard_map/all_gather | solution.py:79
  7.9 81.6 %all-gather.21.cloned.1.call-start = ((), (), s32[]{:S(2)}) async-start(), calls=%async_computation.11 | async-start | bytes 1179648 | tf_op jit(solution)/shard_map/all_gather | solution.py:80
  8.7 121.4 %all-gather.23.cloned.1.call-start = ((), (), s32[]{:S(2)}) async-start(), calls=%async_computation.12 | async-start | bytes 1179648 | tf_op jit(solution)/shard_map/all_gather | solution.py:81
  9.4 173.1 %all-gather.25.cloned.1.call-start = ((), (), s32[]{:S(2)}) async-start(), calls=%async_computation.13 | async-start | bytes 1179648 | tf_op jit(solution)/shard_map/all_gather | solution.py:82
  10.0 307.5 %all-reduce.10.cloned.1.call-start = ((), (), s32[]{:S(2)}) async-start(), calls=%async_computation.14 | async-start | bytes 4194304 | tf_op jit(solution)/shard_map/psum | solution.py:155
  12.8 119.6 %copy-start.5 = (bf16[1,512,2048]{2,1,0:T(8,128)(2,1)S(1)}, bf16[1,512,2048]{2,1,0:T(8,128)(2,1)}, u32[]{:S(2)}) copy-start(bf16[1,512,2048]{2,1,0:T(8,128)(2,1)} %param.16) | copy-start | bytes 6291460
  12.8 123.3 %copy-start.58 = (f32[512]{0:T(512)}, f32[512]{0:T(512)S(1)}, u32[]{:S(2)}) copy-start(f32[512]{0:T(512)S(1)} %add_rsqrt_fusion.3) | copy-start | bytes 6148
  28.0 112.6 %copy-start.62 = (f32[128,2]{0,1:T(2,128)}, f32[128,2]{0,1:T(2,128)S(1)}, u32[]{:S(2)}) copy-start(f32[128,2]{0,1:T(2,128)S(1)} %reshape.1052) | copy-start | bytes 3076
  45.5 95.1 %copy-start.64 = (f32[128,2]{0,1:T(2,128)}, f32[128,2]{0,1:T(2,128)S(1)}, u32[]{:S(2)}) copy-start(f32[128,2]{0,1:T(2,128)S(1)} %reshape.1053) | copy-start | bytes 3076
  60.7 75.4 %copy-start.47 = (f32[8,1,256]{2,1,0:T(1,128)}, f32[8,1,256]{2,1,0:T(1,128)S(1)}, u32[]{:S(2)}) copy-start(f32[8,1,256]{2,1,0:T(1,128)S(1)} %convert_element_type.378) | copy-start | bytes 24580
  137.7 5.8 copy-start.12
  138.5 6.9 copy-start.51
  139.8 7.8 copy-start.14
  143.5 35.9 %copy-start.27 = (bf16[512,2,64]{2,0,1:T(8,128)(2,1)}, bf16[512,2,64]{2,0,1:T(8,128)(2,1)S(1)}, u32[]{:S(2)}) copy-start(bf16[512,2,64]{2,0,1:T(8,128)(2,1)S(1)} %get-tuple-element.48) | copy-start | bytes 393220
  162.5 17.9 copy-start.32
  182.5 4.8 copy-start.34
  182.5 5.5 copy-start.45
  182.5 6.0 copy-start.69
  185.9 236.8 %all-gather.29.cloned.1.call-start = ((), (), s32[]{:S(2)}) async-start(), calls=%async_computation.16 | async-start | bytes 9437184 | tf_op jit(solution)/shard_map/all_gather | solution.py:91
  186.5 409.5 %all-gather.27.cloned.1.call-start = ((), (), s32[]{:S(2)}) async-start(), calls=%async_computation.15 | async-start | bytes 9437184 | tf_op jit(solution)/shard_map/all_gather | solution.py:90
  187.3 584.4 %all-gather.31.cloned.1.call-start = ((), (), s32[]{:S(2)}) async-start(), calls=%async_computation.17 | async-start | bytes 9437184 | tf_op jit(solution)/shard_map/all_gather | solution.py:92
  188.0 780.9 %all-reduce.12.cloned.1.call-start = ((), (), s32[]{:S(2)}) async-start(), calls=%async_computation.18 | async-start | bytes 4194304 | tf_op jit(solution)/shard_map/psum | solution.py:222
  203.6 116.4 %copy-start.49 = (f32[8,1,256]{2,1,0:T(1,128)}, f32[8,1,256]{2,1,0:T(1,128)S(1)}, u32[]{:S(2)}) copy-start(f32[8,1,256]{2,1,0:T(1,128)S(1)} %convert_element_type.381) | copy-start | bytes 24580
  246.1 36.2 %copy-start.68 = (bf16[256,16]{0,1:T(8,128)(2,1)S(1)}, bf16[256,16]{0,1:T(8,128)(2,1)}, u32[]{:S(2)}) copy-start(bf16[256,16]{0,1:T(8,128)(2,1)} %param.24) | copy-start | bytes 24580
  316.8 23.3 %copy-start.43 = (bf16[2048,16]{0,1:T(8,128)(2,1)}, bf16[2048,16]{0,1:T(8,128)(2,1)S(1)}, u32[]{:S(2)}) copy-start(bf16[2048,16]{0,1:T(8,128)(2,1)S(1)} %all_gather.88) | copy-start | bytes 196612
  321.5 18.6 copy-start
  341.6 24.3 %copy-start.25 = (f32[512,8]{1,0:T(8,128)}, f32[512,8]{1,0:T(8,128)S(1)}, u32[]{:S(2)}) copy-start(f32[512,8]{1,0:T(8,128)S(1)} %copy.187) | copy-start | bytes 49156
  341.7 24.1 %copy-start.46 = (f32[4608]{0:T(1024)S(1)}, f32[4608]{0:T(1024)}, u32[]{:S(2)}) copy-start(f32[4608]{0:T(1024)} %scatter_custom_fusion.1) | copy-start | bytes 55300
  365.9 405.8 %copy-start.38 = (f32[16,288]{1,0:T(8,128)}, f32[16,288]{1,0:T(8,128)S(1)}, u32[]{:S(2)}) copy-start(f32[16,288]{1,0:T(8,128)S(1)} %mul.667) | copy-start | bytes 55300
  366.0 230.0 %copy-start.66 = (bf16[16,288]{1,0:T(8,128)(2,1)}, bf16[16,288]{1,0:T(8,128)(2,1)S(1)}, u32[]{:S(2)}) copy-start(bf16[16,288]{1,0:T(8,128)(2,1)S(1)} %mul.658) | copy-start | bytes 27652
  791.6 19.6 copy-start.19
  871.4 184.8 %reduce-scatter.21.cloned.1.call-start = ((), (), s32[]{:S(2)}) async-start(), calls=%async_computation.20 | async-start | bytes 786432 | tf_op jit(solution)/shard_map/reduce_scatter | solution.py:263
  890.0 43.7 %copy-start.26 = (f32[512,8]{1,0:T(8,128)S(1)}, f32[512,8]{1,0:T(8,128)}, u32[]{:S(2)}) copy-start(f32[512,8]{1,0:T(8,128)} %copy-done.25) | copy-start | bytes 49156
  933.6 33.1 %copy-start.41 = (f32[512,8]{0,1:T(8,128)S(1)}, f32[512,8]{0,1:T(8,128)}, u32[]{:S(2)}) copy-start(f32[512,8]{0,1:T(8,128)} %copy-done.40) | copy-start | bytes 49156
  933.6 35.3 %copy-start.7 = (bf16[1,512,2048]{2,1,0:T(8,128)(2,1)S(1)}, bf16[1,512,2048]{2,1,0:T(8,128)(2,1)}, u32[]{:S(2)}) copy-start(bf16[1,512,2048]{2,1,0:T(8,128)(2,1)} %param.16) | copy-start | bytes 6291460
  968.9 4.3 copy-start.50
  968.9 4.3 copy-start.61
  969.0 4.2 copy-start.11
  969.0 4.2 copy-start.18
  980.7 77.5 %reduce-scatter.19.cloned.1.call-start = ((), (), s32[]{:S(2)}) async-start(), calls=%async_computation.19 | async-start | bytes 786432 | tf_op jit(solution)/shard_map/reduce_scatter | solution.py:260
  984.3 4.6 copy-start.39
  988.4 223.1 %reduce-scatter.37.cloned.1.call-start = ((), (), s32[]{:S(2)}) async-start(), calls=%async_computation.31 | async-start | bytes 8912896
  1030.7 364.0 %reduce-scatter.29.cloned.1.call-start = ((), (), s32[]{:S(2)}) async-start(), calls=%async_computation.24 | async-start | bytes 8912896 | tf_op jit(solution)/shard_map/reduce_scatter | solution.py:332
  1045.8 4.1 copy-start.35
  1045.9 425.8 %reduce-scatter.35.cloned.1.call-start = ((), (), s32[]{:S(2)}) async-start(), calls=%async_computation.30 | async-start | bytes 557056
  1049.7 4.7 copy-start.17
  1049.7 499.8 %reduce-scatter.33.cloned.1.call-start = ((), (), s32[]{:S(2)}) async-start(), calls=%async_computation.29 | async-start | bytes 1114112
  1053.0 6.2 copy-start.30
  1054.3 571.1 %all-reduce.14.cloned.1.call-start = ((), (), s32[]{:S(2)}) async-start(), calls=%async_computation.32 | async-start | bytes 8388608 | tf_op jit(solution)/shard_map/psum | solution.py:190
  1056.1 4.3 copy-start.15
  1056.1 4.3 copy-start.65
  1056.2 6.3 copy-start.13
  1056.2 6.3 copy-start.63
  1060.4 8.0 copy-start.36
  1061.6 8.6 copy-start.24
  1063.6 6.0 copy-start.37
  1073.9 630.0 %reduce-scatter.27.cloned.1.call-start = ((), (), s32[]{:S(2)}) async-start(), calls=%async_computation.23 | async-start | bytes 1114112 | tf_op jit(solution)/shard_map/reduce_scatter | solution.py:308
  1079.2 702.8 %reduce-scatter.25.cloned.1.call-start = ((), (), s32[]{:S(2)}) async-start(), calls=%async_computation.22 | async-start | bytes 1114112 | tf_op jit(solution)/shard_map/reduce_scatter | solution.py:305
  1079.8 780.5 %reduce-scatter.23.cloned.1.call-start = ((), (), s32[]{:S(2)}) async-start(), calls=%async_computation.21 | async-start | bytes 1114112 | tf_op jit(solution)/shard_map/reduce_scatter | solution.py:299
  1080.5 962.4 %reduce-scatter.31.cloned.1.call-start = ((), (), s32[]{:S(2)}) async-start(), calls=%async_computation.26 | async-start | bytes 8912896 | tf_op jit(solution)/shard_map/reduce_scatter | solution.py:335
  1094.8 300.0 %copy-start.70 = (u32[128]{0:T(128)S(1)}, u32[128]{0:T(128)}, u32[]{:S(2)}) copy-start(u32[128]{0:T(128)} %constant.103) | copy-start | bytes 1540
  1094.8 975.0 %all-gather.37.cloned.1.call-start = ((), (), s32[]{:S(2)}) async-start(), calls=%async_computation.28 | async-start | bytes 1572864 | tf_op jit(solution)/shard_map/all_gather | solution.py:376
  1213.9 882.4 %all-gather.33.cloned.1.call-start = ((), (), s32[]{:S(2)}) async-start(), calls=%async_computation.25 | async-start | bytes 1572864 | tf_op jit(solution)/shard_map/all_gather | solution.py:370
  1394.7 728.2 %all-gather.35.cloned.1.call-start = ((), (), s32[]{:S(2)}) async-start(), calls=%async_computation.27 | async-start | bytes 1572864 | tf_op jit(solution)/shard_map/all_gather | solution.py:373
  (30 other events, 63.0 us)
Sparse Core Ops, SparseCore 0:
  9.7 39.6 all-gather.18
  51.0 38.4 all-gather.20
  91.2 38.8 all-gather.22
  131.5 45.1 all-gather.24
  186.1 67.3 all-reduce.9
  254.9 167.8 all-gather.28
  424.4 171.5 all-gather.26
  597.6 174.0 all-gather.30
  871.5 69.3 all-reduce.11
  980.8 18.3 reduce-scatter.20
  1001.7 17.9 reduce-scatter.18
  1030.8 180.6 reduce-scatter.36
  1213.9 180.7 reduce-scatter.28
  1396.9 74.7 reduce-scatter.34
  1474.0 75.4 reduce-scatter.32
  1552.3 73.0 all-reduce.13
  1628.2 75.6 reduce-scatter.26
  1706.8 75.0 reduce-scatter.24
  1784.9 75.3 reduce-scatter.22
  1862.7 180.1 reduce-scatter.30
  2044.7 25.0 all-gather.36
  2071.5 24.7 all-gather.32
  2098.1 24.7 all-gather.34
where the time goes:
time: 2140 us; the launch traced here: 2130 us
  waiting for transfers between devices  1360 us (64%)
  local copies, waits for them, and re-layouts  271 us (13%)
  blocking collectives  233 us (11%)
  matrix products  163 us (8%)
  other arithmetic  90.9 us (4%)
    unnamed x26, waiting for transfers between devices  268 us
    reduce_scatter x1, waiting for transfers between devices, body(): lax.psum_scatter(grad_gate_weight.astype(jnp.bfloat16), ('shard', 'ctx'),...  181 us
    reduce_scatter x1, waiting for transfers between devices, body(): lax.psum_scatter(grad_up_weight.astype(jnp.bfloat16), ('shard', 'ctx'), s...  175 us
    all_gather x1, waiting for transfers between devices, body(): lax.all_gather(down_weight, 'shard', axis=2, tiled=True)  163 us
    all_gather x1, waiting for transfers between devices, body(): lax.all_gather(gate_weight, 'shard', axis=1, tiled=True)  161 us
    reduce_scatter x1, waiting for transfers between devices, body(): lax.psum_scatter(grad_query_weight.astype(jnp.bfloat16), ('shard', 'ctx')...  71 us
    reduce_scatter x1, waiting for transfers between devices, body(): lax.psum_scatter(grad_key_weight.astype(jnp.bfloat16), ('shard', 'ctx'),...  70.7 us
    psum x1, waiting for transfers between devices, body(): lax.psum(moe_part.astype(jnp.bfloat16), 'tp').astype(jnp.float32)  68.5 us
  transfers between devices with their start and end apart: 23, of which 17 were waited for; matrix products, arithmetic and copies ran while one was open for 19% of the time, Pallas kernels for 0%

commit v1 on v0

v1 whole, which is shorter than its diff:
```python
import jax
import jax.numpy as jnp
from jax import lax
from jax.sharding import PartitionSpec as P

EPSILON = 1e-05
ROPE_BASE = 10000.0
MASKED_SCORE = -1e30
AXES = ("shard", "ctx", "tp")
BF = jnp.bfloat16
F32 = jnp.float32


def place_of(index):
    shard, rest = divmod(index, 16)
    ctx, tp = divmod(rest, 8)
    return shard // 2, ctx * 2 + shard % 2, tp // 2, tp % 2


def index_of(x, y, z, c):
    x, y, z, c = x % 4, y % 4, z % 4, c % 2
    return (x * 2 + y % 2) * 16 + (y // 2) * 8 + z * 2 + c


def hop(value, dx=0, dy=0, dz=0, dc=0, only=None):
    pairs = []
    for index in range(128):
        x, y, z, c = place_of(index)
        if only is None or only(x, y, z, c):
            pairs.append((index, index_of(x + dx, y + dy, z + dz, c + dc)))
    return lax.ppermute(value, AXES, pairs)


def step_of(axis, amount):
    return {"d" + axis: amount}


def halves(value):
    middle = value.shape[0] // 2
    return value[:middle], value[middle:]


def ring_gather(block, axis):
    from_before = hop(block, **step_of(axis, 1))
    from_after = hop(block, **step_of(axis, -1))
    first = hop(halves(from_before)[0], **step_of(axis, 1))
    second = hop(halves(from_after)[1], **step_of(axis, -1))
    return [block, from_after, jnp.concatenate([first, second], axis=0), from_before]


def direct_gather(block, axis):
    return [
        block,
        hop(block, **step_of(axis, -1)),
        hop(block, **step_of(axis, 2)),
        hop(block, **step_of(axis, 1)),
    ]


def in_order(blocks, start):
    whole = jnp.zeros((4,) + blocks[0].shape, blocks[0].dtype)
    for distance, block in enumerate(blocks):
        whole = lax.dynamic_update_index_in_dim(whole, block, (start + distance) % 4, 0)
    return whole


def by_distance(whole, start):
    return [
        lax.dynamic_index_in_dim(whole, (start + distance) % 4, 0, keepdims=False)
        for distance in range(4)
    ]


def added(*values):
    total = values[0].astype(F32)
    for value in values[1:]:
        total = total + value.astype(F32)
    return total


def ring_scatter(chunks, axis):
    far_first, far_second = halves(chunks[2])
    got_first = hop(far_first, **step_of(axis, 1))
    got_second = hop(far_second, **step_of(axis, -1))
    after_first, after_second = halves(chunks[1])
    before_first, before_second = halves(chunks[3])
    to_after = jnp.concatenate([added(after_first, got_first).astype(BF), after_second], axis=0)
    to_before = jnp.concatenate([before_first, added(before_second, got_second).astype(BF)], axis=0)
    from_before = hop(to_after, **step_of(axis, 1))
    from_after = hop(to_before, **step_of(axis, -1))
    return added(chunks[0], from_before, from_after)


def direct_scatter(chunks, axis):
    return added(
        chunks[0],
        hop(chunks[1], **step_of(axis, 1)),
        hop(chunks[2], **step_of(axis, 2)),
        hop(chunks[3], **step_of(axis, -1)),
    )


def with_partner(own, other, number):
    return jnp.where(
        number == 0, jnp.concatenate([own, other], 0), jnp.concatenate([other, own], 0)
    )


def rms_scale(values):
    return lax.rsqrt(jnp.mean(values * values, axis=-1, keepdims=True) + EPSILON)


def norm_back(grad_normed, source, scale_row, gain_row):
    unit_values = source * scale_row
    grad_unit = grad_normed * gain_row
    grad_source = scale_row * (
        grad_unit - unit_values * jnp.mean(grad_unit * unit_values, axis=-1, keepdims=True)
    )
    return (grad_source, grad_normed * unit_values)


def rope_tables(positions, head_width):
    frequency = ROPE_BASE ** (-(jnp.arange(0, head_width, 2, dtype=F32) / head_width))
    angles = positions.astype(F32)[:, None] * frequency[None, :]
    return (jnp.cos(angles), jnp.sin(angles))


def rotate(values, cosine, sine_table):
    half_width = values.shape[-1] // 2
    first_half = values[..., :half_width]
    second_half = values[..., half_width:]
    return jnp.concatenate(
        [
            first_half * cosine - second_half * sine_table,
            second_half * cosine + first_half * sine_table,
        ],
        axis=-1,
    )


def dot(left, right):
    return jnp.dot(left, right, preferred_element_type=F32)


def dot_nt(left, right):
    return lax.dot_general(left, right, (((1,), (1,)), ((), ())), preferred_element_type=F32)


def dot_tn(left, right):
    return lax.dot_general(left, right, (((0,), (0,)), ((), ())), preferred_element_type=F32)


def body(
    tokens,
    out_grad,
    segments,
    routes,
    query_weight,
    key_weight,
    value_weight,
    out_weight,
    router_weight,
    attn_gain,
    moe_gain,
    query_gain,
    key_gain,
    gate_weight,
    up_weight,
    down_weight,
):
    rows, width = tokens.shape[1], tokens.shape[2]
    experts = gate_weight.shape[0]
    own_experts = experts // 4
    hidden_units = gate_weight.shape[2]
    span = own_experts * hidden_units
    shard, ctx, tp = lax.axis_index("shard"), lax.axis_index("ctx"), lax.axis_index("tp")
    x, y_low, z, core = shard // 2, shard % 2, tp // 2, tp % 2
    y = ctx * 2 + y_low
    home = rows // 8
    head_dim = 128
    local_width = 256
    score_scale = head_dim ** (-0.5)

    def spread_rows(part):
        lane = in_order(direct_gather(part, "z"), z).reshape(4 * part.shape[0], -1)
        return with_partner(lane, hop(lane, dc=1), core)

    def gather_tokens(part):
        lane = jnp.concatenate(direct_gather(part, "z"), axis=0)
        near = ring_gather(lane, "y")
        mine = jnp.concatenate(near, axis=0)
        return jnp.concatenate([mine, hop(mine, dc=1)], axis=0)

    def home_sum(terms):
        keep = lax.dynamic_slice_in_dim(terms, core * 256, 256, 0)
        give = lax.dynamic_slice_in_dim(terms, (1 - core) * 256, 256, 0)
        lane = added(keep, hop(give, dc=1)).astype(BF).reshape(4, home, -1)
        return direct_scatter(by_distance(lane, z), "z")

    def tokens_sum(terms):
        half = 2 * rows
        lane = added(terms[:half], hop(terms[half:], dc=1)).astype(BF)
        mine = ring_scatter([lane[256 * k : 256 * k + 256] for k in range(4)], "y").astype(BF)
        return direct_scatter([mine[home * k : home * k + home] for k in range(4)], "z")

    small = jnp.zeros((256, 128), BF)
    small = small.at[:, 0].set(attn_gain).at[:, 1].set(moe_gain)
    head_gains = jnp.stack([query_gain, key_gain]).reshape(-1)
    small = small.at[: head_gains.shape[0], 2].set(head_gains)
    attn_own = jnp.concatenate([query_weight, key_weight, value_weight, small, out_weight.T], axis=1)
    attn_pair = with_partner(
        attn_own,
        jnp.concatenate([hop(attn_own[:128], dy=1), hop(attn_own[128:], dy=-1)], axis=0),
        y_low,
    )
    attn_all = in_order(ring_gather(attn_pair, "x"), x).reshape(width, -1)
    w_stacked = attn_all[:, : 3 * local_width]
    small_all = attn_all[:, 3 * local_width : 3 * local_width + 128]
    w_out_t = attn_all[:, 3 * local_width + 128 :]
    attn_gains = small_all[:, 0].astype(F32)
    moe_gains = small_all[:, 1].astype(F32)
    gains = small_all[:, 2].reshape(8, 256)[:, :64].reshape(8, 2, 2, 16)
    gains = gains.transpose(1, 2, 0, 3).reshape(2, 2 * head_dim).astype(F32)
    query_gains, key_gains = gains[0][None], gains[1][None]

    def grouped(weight):
        parted = weight.reshape(4, own_experts, 256, hidden_units)
        return parted.transpose(0, 2, 1, 3).reshape(4, 256, span)

    router_pad = jnp.pad(router_weight, ((0, 0), (0, 128 - experts)))
    moe_groups = jnp.concatenate(
        [
            grouped(gate_weight),
            grouped(up_weight),
            jnp.broadcast_to(router_pad[None], (4, 256, 128)),
            grouped(down_weight.transpose(0, 2, 1)),
        ],
        axis=2,
    )
    moe_groups, _ = lax.optimization_barrier((moe_groups, attn_pair))
    moe_own, to_after, _, to_before = by_distance(moe_groups, y)
    moe_pair = with_partner(
        moe_own,
        jnp.concatenate([hop(to_after[:128], dy=1), hop(to_before[128:], dy=-1)], axis=0),
        y_low,
    )
    moe_pair, _ = lax.optimization_barrier((moe_pair, attn_all))
    moe_all = in_order(ring_gather(moe_pair, "x"), x).reshape(width, -1)
    w_in = moe_all[:, : 2 * span + 128]
    w_down_t = moe_all[:, 2 * span + 128 :]

    own_grad = out_grad.reshape(rows, width)
    route_rows = routes.reshape(rows, -1)
    own_picked = jnp.any(
        route_rows[:, :, None] == jnp.arange(128, dtype=jnp.int32)[None, None, :], axis=1
    ).astype(BF)

    def lane_rows(whole):
        half = lax.dynamic_slice_in_dim(whole, core * (rows // 2), rows // 2, 0)
        twice = jnp.concatenate([half, half], axis=0)
        return lax.dynamic_slice_in_dim(twice, z * home, rows // 2, 0)

    grad_half, _ = lax.optimization_barrier((lane_rows(own_grad), attn_pair))
    grad_lane = jnp.concatenate(ring_gather(grad_half, "y"), axis=0)
    grad_all = jnp.concatenate([grad_lane, hop(grad_lane, dc=1)], axis=0)
    picked_lane = jnp.concatenate(direct_gather(lane_rows(own_picked), "y"), axis=0)
    picked = jnp.concatenate([picked_lane, hop(picked_lane, dc=1)], axis=0)[:, :experts] > 0

    inputs = tokens.reshape(rows, width).astype(F32)
    scale_one = rms_scale(inputs)
    normed = (inputs * scale_one * attn_gains).astype(BF)
    projected = dot(normed, w_stacked)
    query_pre = [projected[:, h * 128 : h * 128 + 128] for h in range(2)]
    key_pre = [projected[:, 256 + h * 128 : 384 + h * 128] for h in range(2)]
    value_low = projected[:, 512:].astype(BF)
    first_row = ctx * rows
    places = first_row + jnp.arange(rows, dtype=jnp.int32)
    cosine, sine_table = rope_tables(places, head_dim)
    scale_query = [rms_scale(v) for v in query_pre]
    scale_key = [rms_scale(v) for v in key_pre]
    gain_q = [query_gains[:, h * 128 : h * 128 + 128] for h in range(2)]
    gain_k = [key_gains[:, h * 128 : h * 128 + 128] for h in range(2)]
    query_low = [
        rotate(query_pre[h] * scale_query[h] * gain_q[h], cosine, sine_table).astype(BF)
        for h in range(2)
    ]
    key_low = [
        rotate(key_pre[h] * scale_key[h] * gain_k[h], cosine, sine_table).astype(BF)
        for h in range(2)
    ]
    keys_values = jnp.concatenate(key_low + [value_low], axis=1)
    earlier = hop(keys_values, dy=2, only=lambda x, y, z, c: y < 2)
    both = jnp.concatenate([earlier, keys_values], axis=0)
    keys = [both[:, h * 128 : h * 128 + 128] for h in range(2)]
    values = [both[:, 256 + h * 128 : 384 + h * 128] for h in range(2)]
    key_places = first_row - rows + jnp.arange(2 * rows, dtype=jnp.int32)
    own_segments = lax.dynamic_slice_in_dim(segments[0], first_row, rows, 0)
    key_segments = jnp.concatenate([segments[0, :rows], own_segments])
    allowed = (
        (places[:, None] >= key_places[None, :])
        & (key_places[None, :] >= 0)
        & (own_segments[:, None] == key_segments[None, :])
    )
    probs, mixed = [], []
    for h in range(2):
        scores = jnp.where(allowed, dot_nt(query_low[h], keys[h]) * score_scale, MASKED_SCORE)
        exponents = jnp.exp(scores - jnp.max(scores, axis=-1, keepdims=True))
        probs.append(exponents / jnp.sum(exponents, axis=-1, keepdims=True))
        mixed.append(dot(probs[h].astype(BF), values[h]))
    mixed_low = jnp.concatenate(mixed, axis=1).astype(BF)
    attn_part = dot_nt(mixed_low, w_out_t).astype(BF)

    home_row = (core * 4 + z) * home
    home_inputs = lax.dynamic_slice_in_dim(tokens.reshape(rows, width), home_row, home, 0).astype(F32)
    home_scale_one = lax.dynamic_slice_in_dim(scale_one, home_row, home, 0)
    home_grad = lax.dynamic_slice_in_dim(own_grad, home_row, home, 0).astype(F32)
    hidden = home_inputs + home_sum(attn_part)
    scale_two = rms_scale(hidden)
    moe_in = gather_tokens((hidden * scale_two * moe_gains).astype(BF))

    joined = dot(moe_in, w_in)
    logits = jnp.where(picked, joined[:, 2 * span : 2 * span + experts], -jnp.inf)
    gates = jax.nn.softmax(logits, axis=-1)
    own_gates = lax.dynamic_slice_in_dim(gates, y * own_experts, own_experts, 1)
    wide_gates = jnp.repeat(own_gates, hidden_units, axis=1)
    gate_pre, up_pre = joined[:, :span], joined[:, span : 2 * span]
    logistic = jax.nn.sigmoid(gate_pre)
    silu_gate = gate_pre * logistic
    silu_slope = logistic * (1.0 + gate_pre * (1.0 - logistic))
    act = silu_gate * up_pre
    act_back = dot(grad_all, w_down_t)
    gate_terms = jnp.sum(
        (act.astype(BF).astype(F32) * act_back).reshape(-1, own_experts, hidden_units), axis=-1
    )
    gate_grad = lax.dynamic_update_slice_in_dim(
        jnp.zeros_like(gates), gate_terms, y * own_experts, 1
    )
    logit_grad = gates * (gate_grad - jnp.sum(gates * gate_grad, axis=-1, keepdims=True))
    act_grad = act_back * wide_gates
    pre_grad = jnp.concatenate(
        [
            (act_grad * up_pre * silu_slope).astype(BF),
            (act_grad * silu_gate).astype(BF),
            jnp.pad(logit_grad.astype(BF), ((0, 0), (0, 128 - experts))),
        ],
        axis=1,
    )
    gated_act = (act * wide_gates).astype(BF)
    moe_in_part = dot_nt(pre_grad, w_in).astype(BF)
    moe_in_grad = tokens_sum(moe_in_part)
    moe_part = dot_nt(gated_act, w_down_t).astype(BF)
    moe_part, _ = lax.optimization_barrier((moe_part, moe_in_grad))
    layer_rows = (hidden + tokens_sum(moe_part)).astype(BF)
    layer_out = spread_rows(layer_rows).reshape(tokens.shape)
    grad_in = dot_tn(moe_in, pre_grad).astype(BF)
    grad_down_t = dot_tn(grad_all, gated_act).astype(BF)
    grad_in, grad_down_t, _ = lax.optimization_barrier((grad_in, grad_down_t, moe_in_grad))
    grad_moe = ring_scatter(
        [
            jnp.concatenate([a[:, : 2 * span], b], axis=1)
            for a, b in zip(
                by_distance(grad_in.reshape(4, 512, -1), x),
                by_distance(grad_down_t.reshape(4, 512, -1), x),
            )
        ],
        "x",
    ).astype(BF)
    grad_moe = grad_moe.reshape(2, 256, -1)
    keep = lax.dynamic_index_in_dim(grad_moe, y_low, 0, keepdims=False)
    give = lax.dynamic_index_in_dim(grad_moe, 1 - y_low, 0, keepdims=False)
    grad_groups = in_order(
        [keep, hop(give, dy=-1), hop(keep, dy=2), hop(give, dy=1)], y
    )

    def ungrouped(part):
        parted = part.reshape(4, 256, own_experts, hidden_units)
        return parted.transpose(0, 2, 1, 3).reshape(experts, 256, hidden_units).astype(F32)

    grad_gate_weight = ungrouped(grad_groups[:, :, :span])
    grad_up_weight = ungrouped(grad_groups[:, :, span : 2 * span])
    grad_down_weight = (
        grad_groups[:, :, 2 * span :]
        .reshape(4, 256, own_experts, hidden_units)
        .transpose(0, 2, 3, 1)
        .reshape(experts, hidden_units, 256)
        .astype(F32)
    )

    hidden_norm_grad, moe_gain_rows = norm_back(moe_in_grad, hidden, scale_two, moe_gains)
    hidden_grad = home_grad + hidden_norm_grad
    hidden_low = spread_rows(hidden_grad.astype(BF))
    grad_router = grad_in[:, 2 * span : 2 * span + experts]
    early = jnp.concatenate([grad_router.T.astype(F32), jnp.sum(moe_gain_rows, axis=0)[None]], axis=0)
    early = early.reshape(-1, 128)
    early = early + hop(early, dc=1)
    for axis in "zyx":
        early = direct_scatter([early] * 4, axis)
    early = early.reshape(experts + 1, width)
    early = lax.dynamic_slice_in_dim(early, shard * 256, 256, 1)

    mixed_grad = dot(hidden_low, w_out_t).astype(BF)
    grad_out_t = dot_tn(hidden_low, mixed_low)
    query_grads, key_terms, value_terms = [], [], []
    for h in range(2):
        grad_h = mixed_grad[:, h * 128 : h * 128 + 128]
        prob_grad = dot_nt(grad_h, values[h])
        row_delta = jnp.sum(probs[h] * prob_grad, axis=-1, keepdims=True)
        score_grad = (probs[h] * (prob_grad - row_delta)).astype(BF)
        query_grads.append((dot(score_grad, keys[h]) * score_scale).astype(BF).astype(F32))
        key_terms.append(dot_tn(score_grad, query_low[h]) * score_scale)
        value_terms.append(dot_tn(probs[h].astype(BF), grad_h))
    terms = jnp.concatenate(key_terms + value_terms, axis=1)
    later = hop(terms[:rows].astype(BF), dy=2, only=lambda x, y, z, c: y >= 2)
    key_value_grad = added(terms[rows:], later).astype(BF)
    stacked, gain_sums = [], []
    for pre, scale, gain, grads in (
        (query_pre, scale_query, gain_q, query_grads),
        (key_pre, scale_key, gain_k, [key_value_grad[:, :128], key_value_grad[:, 128:256]]),
    ):
        for h in range(2):
            unit_grad = rotate(grads[h].astype(F32), cosine, -sine_table)
            pre_back, gain_rows = norm_back(unit_grad, pre[h], scale[h], gain[h])
            stacked.append(pre_back.astype(BF))
            gain_sums.append(jnp.sum(gain_rows, axis=0))
    stacked = jnp.concatenate(stacked + [key_value_grad[:, 256:]], axis=1)
    normed_part = dot_nt(stacked, w_stacked).astype(BF)
    grad_stacked = dot_tn(normed, stacked)
    normed_grad = home_sum(normed_part)
    input_norm_grad, attn_gain_rows = norm_back(
        normed_grad, home_inputs, home_scale_one, attn_gains
    )
    input_grad = spread_rows((hidden_grad + input_norm_grad).astype(BF)).reshape(tokens.shape)
    grad_attn = jnp.concatenate([grad_stacked, grad_out_t], axis=1).astype(BF)
    grad_attn = ring_scatter(by_distance(grad_attn.reshape(4, 512, -1), x), "x").astype(BF)
    grad_attn = grad_attn.reshape(2, 256, -1)
    keep = lax.dynamic_index_in_dim(grad_attn, y_low, 0, keepdims=False)
    give = lax.dynamic_index_in_dim(grad_attn, 1 - y_low, 0, keepdims=False)
    got = jnp.concatenate([hop(give[:128], dy=1), hop(give[128:], dy=-1)], axis=0)
    keep = added(keep, got).astype(BF)
    grad_attn = added(keep, hop(keep, dy=2))
    head_gain_sums = jnp.stack(gain_sums).reshape(2, 1, 2, 128)
    mine = (jnp.arange(8) == tp).astype(F32)[None, :, None, None]
    late = jnp.concatenate(
        [jnp.sum(attn_gain_rows, axis=0), (mine * head_gain_sums).reshape(-1)]
    ).reshape(48, 128)
    late = late + hop(late, dc=1)
    for axis in "zyx":
        late = direct_scatter([late] * 4, axis)
    grad_attn_gain = lax.dynamic_slice_in_dim(late[:16].reshape(-1), shard * 256, 256, 0)
    late_heads = late[16:].reshape(2, 8, 2, 128)
    late_heads = lax.dynamic_index_in_dim(late_heads, tp, 1, keepdims=False)
    late_heads = lax.dynamic_slice_in_dim(late_heads, shard * 16, 16, 2)
    return (
        layer_out,
        input_grad,
        grad_attn[:, :256],
        grad_attn[:, 256:512],
        grad_attn[:, 512:768],
        grad_attn[:, 768:].T,
        early[:experts].T,
        grad_attn_gain,
        early[experts],
        late_heads[0],
        late_heads[1],
        grad_gate_weight,
        grad_up_weight,
        grad_down_weight,
    )


def solution(mesh):
    return jax.shard_map(
        body,
        mesh=mesh,
        in_specs=(
            P("shard", "ctx", None),
            P("shard", "ctx", None),
            P("shard", None),
            P("shard", "ctx", None),
            P("shard", "tp"),
            P("shard", "tp"),
            P("shard", "tp"),
            P("tp", "shard"),
            P("shard", None),
            P("shard"),
            P("shard"),
            P("tp", "shard"),
            P("tp", "shard"),
            P(None, "shard", "tp"),
            P(None, "shard", "tp"),
            P(None, "tp", "shard"),
        ),
        out_specs=(
            P("shard", "ctx", None),
            P("shard", "ctx", None),
            P("shard", "tp"),
            P("shard", "tp"),
            P("shard", "tp"),
            P("tp", "shard"),
            P("shard", None),
            P("shard"),
            P("shard"),
            P("tp", "shard"),
            P("tp", "shard"),
            P(None, "shard", "tp"),
            P(None, "shard", "tp"),
            P(None, "tp", "shard"),
        ),
        check_vma=False,
    )
```

time: 2140 us -> 742 us (0.35)
  waiting for transfers between devices: 1360 us -> 291 us
  blocking collectives: 233 us -> 0 us
  local copies, waits for them, and re-layouts: 271 us -> 119 us
  starting transfers between devices: 1.71 us -> 137 us
  matrix products: 163 us -> 91.8 us
    reduce_scatter x7 -> x0, waiting for transfers between devices: 511 us -> none  [the longest x1 181 us: body(): lax.psum_scatter(grad_gate_weight.astype(jnp.bfloat16), ('shard', 'ctx'),...]
    all_gather x10 -> x0, waiting for transfers between devices: 508 us -> none  [the longest x1 163 us: body(): lax.all_gather(down_weight, 'shard', axis=2, tiled=True)]
    ppermute x0 -> x101, waiting for transfers between devices: none -> 291 us  [hop(): return lax.ppermute(value, AXES, pairs)]
    unnamed x26 -> x0, waiting for transfers between devices: 268 us -> none
    all_gather x16 -> x0, blocking collectives: 182 us -> none  [the longest x1 34.5 us: body(): lax.all_gather(router_weight, 'shard', axis=0, tiled=True)]
    gather x5 -> x0, local copies, waits for them, and re-layouts: 166 us -> none  [the longest x1 43.7 us: body(): picked_out = expert_out[destination]]
    ppermute x0 -> x101, starting transfers between devices: none -> 137 us  [hop(): return lax.ppermute(value, AXES, pairs)]
    dot_general x23 -> x24, matrix products: 163 us -> 91.8 us  [the longest x8 32.5 us: dot(): return jnp.dot(left, right, preferred_element_type=F32)]
  transfers between devices with their start and end apart: 23 -> 101, of which waited for: 17 -> 51; matrix products, arithmetic and copies ran while one was open for 19% -> 26% of each run, Pallas kernels for 0% -> 0%
where the time goes in v1:
time: 742 us; the launch traced here: 733 us
  waiting for transfers between devices  291 us (39%)
  starting transfers between devices  137 us (18%)
  local copies, waits for them, and re-layouts  119 us (16%)
  matrix products  91.8 us (12%)
  other arithmetic  90.4 us (12%)
    ppermute x101, waiting for transfers between devices, hop(): return lax.ppermute(value, AXES, pairs)  291 us
    ppermute x101, starting transfers between devices, hop(): return lax.ppermute(value, AXES, pairs)  137 us
    unnamed x222, local copies, waits for them, and re-layouts  35.4 us
    dot_general x8, matrix products, dot(): return jnp.dot(left, right, preferred_element_type=F32)  32.5 us
    dot_general x8, matrix products, dot_nt(): lax.dot_general(left, right, (((1,), (1,)), ((), ())), preferred_element_...  29.8 us
    dot_general x8, matrix products, dot_tn(): lax.dot_general(left, right, (((0,), (0,)), ((), ())), preferred_element_...  29.5 us
    dynamic_update_slice x17, local copies, waits for them, and re-layouts, in_order(): lax.dynamic_update_index_in_dim(whole, block, (start + distance) % 4, 0)  16.9 us
  transfers between devices with their start and end apart: 101, of which 51 were waited for; matrix products, arithmetic and copies ran while one was open for 26% of the time, Pallas kernels for 0%

profile of v1, /device:TPU:14, one launch (start us, length us, event | category | flops | bytes accessed | tf_op | source)
XLA Modules:
  0.0 733.2 jit_solution(3383265587914325578)
XLA Ops:
  17.1 6.9 collective-permute-done
  29.4 24.2 %collective-permute-done.3 = bf16[512,1152]{1,0:T(8,128)(2,1)} collective-permute-done((bf16[512,1152]{1,0:T(8,128)(2,1)}, bf16[512,1152]{1,0:T(8,128)(2,1)}, u32[]{:S(2)}, u32[]{:S(2)}) %collective-permute-start.3) | collective-permute-done | bytes 1179680 | tf_op jit(solution)/shard_map/ppermute | solution.py:31
  60.3 7.4 %collective-permute-done.4 = bf16[256,1152]{1,0:T(8,128)(2,1)S(1)} collective-permute-done((bf16[256,1152]{1,0:T(8,128)(2,1)S(1)}, bf16[256,1152]{1,0:T(8,128)(2,1)S(1)}, u32[]{:S(2)}, u32[]{:S(2)}) %collective-permute-start.4) | collective-permute-done | bytes 589856 | tf_op jit(solution)/shard_map/ppermute | solution.py:31
  67.8 3.8 collective-permute-done.5
  79.4 5.1 collective-permute-start.6
  113.4 3.8 collective-permute-start.10
  117.1 24.2 %collective-permute-done.19 = bf16[128,1664]{0,1:T(8,128)(2,1)S(1)} collective-permute-done((bf16[128,1664]{0,1:T(8,128)(2,1)}, bf16[128,1664]{0,1:T(8,128)(2,1)S(1)}, u32[]{:S(2)}, u32[]{:S(2)}) %collective-permute-start.19) | collective-permute-done | bytes 426016 | tf_op jit(solution)/shard_map/ppermute | solution.py:31
  143.0 3.6 collective-permute-start.9
  146.6 2.8 constant_dynamic-update-slice_fusion.30
  153.3 3.2 collective-permute-start.32
  162.5 2.8 constant_dynamic-update-slice_fusion.29
  165.3 4.4 collective-permute-done.11
  171.3 3.4 collective-permute-done.13
  179.3 2.8 constant_dynamic-update-slice_fusion.26
  183.0 17.3 %collective-permute-done.15 = bf16[256,2048]{1,0:T(8,128)(2,1)S(1)} collective-permute-done((bf16[256,2048]{1,0:T(8,128)(2,1)S(1)}, bf16[256,2048]{1,0:T(8,128)(2,1)S(1)}, u32[]{:S(2)}, u32[]{:S(2)}) %collective-permute-start.15) | collective-permute-done | bytes 1048608 | tf_op jit(solution)/shard_map/ppermute | solution.py:31
  202.2 2.7 collective-permute-start.17
  206.2 8.1 %collective-permute-done.16 = bf16[128,2048]{1,0:T(8,128)(2,1)S(1)} collective-permute-done((bf16[128,2048]{1,0:T(8,128)(2,1)S(1)}, bf16[128,2048]{1,0:T(8,128)(2,1)S(1)}, u32[]{:S(2)}, u32[]{:S(2)}) %collective-permute-start.16) | collective-permute-done | bytes 524320 | tf_op jit(solution)/shard_map/ppermute | solution.py:31
  222.5 2.9 fusion.17
  230.6 5.6 collective-permute-start.26
  239.3 3.4 collective-permute-done.27
  244.4 15.4 %collective-permute-done.22 = bf16[512,1664]{1,0:T(8,128)(2,1)} collective-permute-done((bf16[512,1664]{1,0:T(8,128)(2,1)}, bf16[512,1664]{1,0:T(8,128)(2,1)}, u32[]{:S(2)}, u32[]{:S(2)}) %collective-permute-start.22) | collective-permute-done | bytes 1703968 | tf_op jit(solution)/shard_map/ppermute | solution.py:31
  268.7 12.5 %collective-permute-done.23 = bf16[256,1664]{1,0:T(8,128)(2,1)S(1)} collective-permute-done((bf16[256,1664]{1,0:T(8,128)(2,1)S(1)}, bf16[256,1664]{1,0:T(8,128)(2,1)S(1)}, u32[]{:S(2)}, u32[]{:S(2)}) %collective-permute-start.23) | collective-permute-done | bytes 852000 | tf_op jit(solution)/shard_map/ppermute | solution.py:31
  281.1 4.0 collective-permute-done.24
  287.2 4.9 constant_dynamic-update-slice_fusion.31
  292.1 7.8 %constant_dynamic-update-slice_fusion.12 = bf16[2048,2048]{1,0:T(8,128)(2,1)} fusion(bf16[2048,2048]{1,0:T(8,128)(2,1)} %copy-done.89, bf16[1024,2048]{1,0:T(8,128)(2,1)} %collective-permute-done.18), kind=kLoop, calls=%fused_computation.368 | loop fusion | bytes 8388608 | tf_op jit(solution)/shard_map/concatenate | solution.py:192
  299.9 14.0 %fusion.8 = f32[2048,1152]{0,1:T(8,128)S(1)} fusion(bf16[2048,2048]{1,0:T(8,128)(2,1)} %constant_dynamic-update-slice_fusion.12, bf16[2048,1664]{1,0:T(8,128)(2,1)} %bitcast.278), kind=kOutput, calls=%fused_computation.31 | convolution fusion | flops 9663676416 | bytes 22544384 | tf_op jit(solution)/shard_map/dot_general | solution.py:142
  314.0 11.4 %bitcast_reduce_fusion = (f32[2048,4]{0,1:T(4,128)S(1)}, f32[2048,512]{0,1:T(8,128)}) fusion(f32[2048,1152]{0,1:T(8,128)S(1)} %fusion.8, bf16[2048,2048]{1,0:T(8,128)(2,1)} %copy-done.60, bf16[2048,1664]{1,0:T(8,128)(2,1)} %bitcast.279), kind=kOutput, calls=%fused_computation.24 | convolution fusion | flops 4304396288 | bytes 23101440 | tf_op jit(solution)/shard_map/dot_general | solution.py:142
  325.6 6.7 multiply_convert_fusion.1
  332.3 14.4 %convolution_convert_fusion.1 = bf16[2048,2048]{1,0:T(8,128)(2,1)S(1)} fusion(bf16[2048,1664]{1,0:T(8,128)(2,1)} %bitcast.280, bf16[2048,16]{0,1:T(8,128)(2,1)S(1)} %multiply_convert_fusion.9, bf16[2048,512]{0,1:T(8,128)(2,1)} %get-tuple-element.171, bf16[2048,512]{0,1:T(8,128)(2,1)} %get-tuple-element.170), kind=kOutput, calls=%fused_computation.5 | convolution fusion | flops 9686745088 | bytes 17367040 | tf_op jit(solution)/shard_map/dot_general | solution.py:146
  353.2 3.9 copy.154
  358.8 5.4 add_convert_fusion.1
  368.0 13.8 %convolution_convert_fusion = bf16[2048,1152]{1,0:T(8,128)(2,1)S(1)} fusion(bf16[2048,2048]{1,0:T(8,128)(2,1)} %constant_dynamic-update-slice_fusion.12, bf16[2048,16]{0,1:T(8,128)(2,1)S(1)} %multiply_convert_fusion.9, bf16[2048,512]{0,1:T(8,128)(2,1)S(1)} %copy-done.44, bf16[2048,512]{0,1:T(8,128)(2,1)S(1)} %copy-done.43), kind=kOutput, calls=%fused_computation.4 | convolution fusion | flops 9684910080 | bytes 17367040 | tf_op jit(solution)/shard_map/dot_general | solution.py:150
  387.2 8.6 %convolution_convert_fusion.4 = bf16[2048,512]{1,0:T(8,128)(2,1)S(1)} fusion(bf16[2048,2048]{1,0:T(8,128)(2,1)} %copy-done.60, bf16[2048,512]{0,1:T(8,128)(2,1)S(1)} %copy-done.42), kind=kOutput, calls=%fused_computation.40 | convolution fusion | flops 4296015872 | bytes 12582912 | tf_op jit(solution)/shard_map/dot_general | solution.py:150
  395.7 14.4 %collective-permute-done.36 = bf16[256,2048]{1,0:T(8,128)(2,1)S(1)} collective-permute-done((bf16[256,2048]{1,0:T(8,128)(2,1)S(1)}, bf16[256,2048]{1,0:T(8,128)(2,1)S(1)}, u32[]{:S(2)}, u32[]{:S(2)}) %collective-permute-start.36) | collective-permute-done | bytes 1048608 | tf_op jit(solution)/shard_map/ppermute | solution.py:31
  412.0 3.1 collective-permute-start.41
  415.1 8.7 %convolution_convert_fusion.2 = bf16[2048,2048]{1,0:T(8,128)(2,1)} fusion(bf16[2048,512]{0,1:T(8,128)(2,1)S(1)} %copy-done.42, bf16[2048,1664]{1,0:T(8,128)(2,1)} %bitcast.281), kind=kOutput, calls=%fused_computation.6 | convolution fusion | flops 4299161600 | bytes 12582912 | tf_op jit(solution)/shard_map/dot_general | solution.py:146
  439.5 2.7 fusion.49
  445.8 4.9 slice.558
  451.7 2.7 collective-permute-start.75
  459.1 3.5 collective-permute-done.76
  464.3 2.9 collective-permute-start.79
  477.6 5.2 collective-permute-done.81
  482.7 10.4 %collective-permute-done.82 = f32[272,128]{1,0:T(8,128)S(1)} collective-permute-done((f32[272,128]{1,0:T(8,128)S(1)}, f32[272,128]{1,0:T(8,128)S(1)}, u32[]{:S(2)}, u32[]{:S(2)}) %collective-permute-start.82) | collective-permute-done | bytes 139296 | tf_op jit(solution)/shard_map/ppermute | solution.py:31
  493.1 3.6 collective-permute-done.83
  503.8 3.3 convolution_convert_fusion.8
  517.5 3.4 convolution_convert_fusion.6
  520.9 9.0 %collective-permute-done.58 = bf16[512,512]{1,0:T(8,128)(2,1)S(1)} collective-permute-done((bf16[512,512]{1,0:T(8,128)(2,1)S(1)}, bf16[512,512]{1,0:T(8,128)(2,1)S(1)}, u32[]{:S(2)}, u32[]{:S(2)}) %collective-permute-start.58) | collective-permute-done | bytes 524320 | tf_op jit(solution)/shard_map/ppermute | solution.py:31
  544.1 10.4 %collective-permute-done.67 = bf16[256,1024]{1,0:T(8,128)(2,1)S(1)} collective-permute-done((bf16[256,1024]{1,0:T(8,128)(2,1)S(1)}, bf16[256,1024]{1,0:T(8,128)(2,1)S(1)}, u32[]{:S(2)}, u32[]{:S(2)}) %collective-permute-start.67) | collective-permute-done | bytes 524320 | tf_op jit(solution)/shard_map/ppermute | solution.py:31
  554.7 3.5 collective-permute-done.69
  568.2 6.2 collective-permute-done.61
  575.6 18.3 %collective-permute-done.99 = bf16[256,1536]{1,0:T(8,128)(2,1)S(1)} collective-permute-done((bf16[256,1536]{1,0:T(8,128)(2,1)S(1)}, bf16[256,1536]{1,0:T(8,128)(2,1)S(1)}, u32[]{:S(2)}, u32[]{:S(2)}) %collective-permute-start.99) | collective-permute-done | bytes 786464 | tf_op jit(solution)/shard_map/ppermute | solution.py:31
  605.7 10.9 %collective-permute-start.88 = (f32[48,128]{1,0:T(8,128)S(1)}, f32[48,128]{1,0:T(8,128)S(1)}, u32[]{:S(2)}, u32[]{:S(2)}) collective-permute-start(f32[48,128]{1,0:T(8,128)S(1)} %add_add_fusion.5), channel_id=1, source_target_pairs={{0,16},{1,17},{2,18},{3,19},{4,20},{5,21},{6,22},{7,23},{8,24},{9,... | collective-permute-start | bytes 73736 | tf_op jit(solution)/shard_map/ppermute | solution.py:31
  624.8 3.3 collective-permute-start.91
  629.0 5.4 add_convert_fusion
  636.9 9.3 %collective-permute-done.92 = f32[48,128]{1,0:T(8,128)S(1)} collective-permute-done((f32[48,128]{1,0:T(8,128)S(1)}, f32[48,128]{1,0:T(8,128)S(1)}, u32[]{:S(2)}, u32[]{:S(2)}) %collective-permute-start.92) | collective-permute-done | bytes 24608 | tf_op jit(solution)/shard_map/ppermute | solution.py:31
  654.1 3.7 collective-permute-done.43
  660.8 3.1 collective-permute-start.46
  670.3 10.7 %collective-permute-done.44 = bf16[256,2048]{1,0:T(8,128)(2,1)} collective-permute-done((bf16[256,2048]{1,0:T(8,128)(2,1)}, bf16[256,2048]{1,0:T(8,128)(2,1)}, u32[]{:S(2)}, u32[]{:S(2)}) %collective-permute-start.44) | collective-permute-done | bytes 1048608 | tf_op jit(solution)/shard_map/ppermute | solution.py:31
  691.9 4.1 collective-permute-done.48
  700.2 4.8 collective-permute-start.73
  706.8 8.8 %collective-permute-done.51 = bf16[64,2048]{1,0:T(8,128)(2,1)S(1)} collective-permute-done((bf16[64,2048]{1,0:T(8,128)(2,1)S(1)}, bf16[64,2048]{1,0:T(8,128)(2,1)S(1)}, u32[]{:S(2)}, u32[]{:S(2)}) %collective-permute-start.51) | collective-permute-done | bytes 262176 | tf_op jit(solution)/shard_map/ppermute | solution.py:31
  715.7 4.6 collective-permute-done.52
  725.2 3.8 maximum_select_fusion.2
  729.0 3.8 maximum_select_fusion
  (612 shorter events, 275.8 us)
Async XLA Ops:
  26.8 26.8 %collective-permute-start.3 = (bf16[512,1152]{1,0:T(8,128)(2,1)}, bf16[512,1152]{1,0:T(8,128)(2,1)}, u32[]{:S(2)}, u32[]{:S(2)}) collective-permute-start(bf16[512,1152]{1,0:T(8,128)(2,1)} %maximum_select_fusion.5), channel_id=1, source_target_pairs={{0,32},{1,33},{2,34},{3,35},{4,36},{5,37},{6,38},{7,39},{8,40},{9,... | collective-permute-start | bytes 3538952 | tf_op jit(solution)/shard_map/ppermute | solution.py:31
  27.3 29.2 %collective-permute-start.2 = (bf16[512,1152]{1,0:T(8,128)(2,1)}, bf16[512,1152]{1,0:T(8,128)(2,1)}, u32[]{:S(2)}, u32[]{:S(2)}) collective-permute-start(bf16[512,1152]{1,0:T(8,128)(2,1)} %maximum_select_fusion.5), channel_id=1, source_target_pairs={{0,96},{1,97},{2,98},{3,99},{4,100},{5,101},{6,102},{7,103},{8,104... | collective-permute-start | bytes 3538952 | tf_op jit(solution)/shard_map/ppermute | solution.py:31
  57.6 14.0 %collective-permute-start.5 = (bf16[256,1152]{1,0:T(8,128)(2,1)S(1)}, bf16[256,1152]{1,0:T(8,128)(2,1)S(1)}, u32[]{:S(2)}, u32[]{:S(2)}) collective-permute-start(bf16[256,1152]{1,0:T(8,128)(2,1)S(1)} %slice.632), channel_id=1, source_target_pairs={{0,96},{1,97},{2,98},{3,99},{4,100},{5,101},{6,102},{7,103},{8,104... | collective-permute-start | bytes 1769480 | tf_op jit(solution)/shard_map/ppermute | solution.py:31
  103.2 49.0 %collective-permute-start.29 = (bf16[256,2048]{1,0:T(8,128)(2,1)}, bf16[256,2048]{1,0:T(8,128)(2,1)}, u32[]{:S(2)}, u32[]{:S(2)}) collective-permute-start(bf16[256,2048]{1,0:T(8,128)(2,1)} %fusion.34), channel_id=1, source_target_pairs={{0,24},{1,25},{2,26},{3,27},{4,28},{5,29},{6,30},{7,31},{8,16},{9,... | collective-permute-start | bytes 3145736 | tf_op jit(solution)/shard_map/ppermute | solution.py:31
  103.9 47.1 %collective-permute-start.30 = (bf16[256,2048]{1,0:T(8,128)(2,1)}, bf16[256,2048]{1,0:T(8,128)(2,1)}, u32[]{:S(2)}, u32[]{:S(2)}) collective-permute-start(bf16[256,2048]{1,0:T(8,128)(2,1)} %fusion.34), channel_id=1, source_target_pairs={{0,16},{1,17},{2,18},{3,19},{4,20},{5,21},{6,22},{7,23},{8,24},{9,... | collective-permute-start | bytes 3145736 | tf_op jit(solution)/shard_map/ppermute | solution.py:31
  106.9 34.4 %collective-permute-start.19 = (bf16[128,1664]{0,1:T(8,128)(2,1)}, bf16[128,1664]{0,1:T(8,128)(2,1)S(1)}, u32[]{:S(2)}, u32[]{:S(2)}) collective-permute-start(bf16[128,1664]{0,1:T(8,128)(2,1)} %get-tuple-element.192), channel_id=1, source_target_pairs={{0,16},{1,17},{2,18},{3,19},{4,20},{5,21},{6,22},{7,23},{8,24},{9,... | collective-permute-start | bytes 1277960 | tf_op jit(solution)/shard_map/ppermute | solution.py:31
  108.9 34.1 %collective-permute-start.20 = (bf16[128,1664]{0,1:T(8,128)(2,1)}, bf16[128,1664]{0,1:T(8,128)(2,1)}, u32[]{:S(2)}, u32[]{:S(2)}) collective-permute-start(bf16[128,1664]{0,1:T(8,128)(2,1)} %get-tuple-element.193), channel_id=1, source_target_pairs={{0,24},{1,25},{2,26},{3,27},{4,28},{5,29},{6,30},{7,31},{8,16},{9,... | collective-permute-start | bytes 1277960 | tf_op jit(solution)/shard_map/ppermute | solution.py:31
  113.4 43.1 %collective-permute-start.10 = (bf16[64,2048]{1,0:T(8,128)(2,1)}, bf16[64,2048]{1,0:T(8,128)(2,1)}, u32[]{:S(2)}, u32[]{:S(2)}) collective-permute-start(bf16[64,2048]{1,0:T(8,128)(2,1)} %get-tuple-element.243), channel_id=1, source_target_pairs={{0,6},{1,7},{2,0},{3,1},{4,2},{5,3},{6,4},{7,5},{8,14},{9,15},{10,... | collective-permute-start | bytes 786440 | tf_op jit(solution)/shard_map/ppermute | solution.py:31
  141.3 15.1 %collective-permute-start.8 = (bf16[64,2048]{1,0:T(8,128)(2,1)S(1)}, bf16[64,2048]{1,0:T(8,128)(2,1)}, u32[]{:S(2)}, u32[]{:S(2)}) collective-permute-start(bf16[64,2048]{1,0:T(8,128)(2,1)S(1)} %get-tuple-element.242), channel_id=1, source_target_pairs={{0,2},{1,3},{2,4},{3,5},{4,6},{5,7},{6,0},{7,1},{8,10},{9,11},{10,... | collective-permute-start | bytes 786440 | tf_op jit(solution)/shard_map/ppermute | solution.py:31
  143.0 15.2 %collective-permute-start.9 = (bf16[64,2048]{1,0:T(8,128)(2,1)S(1)}, bf16[64,2048]{1,0:T(8,128)(2,1)}, u32[]{:S(2)}, u32[]{:S(2)}) collective-permute-start(bf16[64,2048]{1,0:T(8,128)(2,1)S(1)} %get-tuple-element.244), channel_id=1, source_target_pairs={{0,4},{1,5},{2,6},{3,7},{4,0},{5,1},{6,2},{7,3},{8,12},{9,13},{10,... | collective-permute-start | bytes 786440 | tf_op jit(solution)/shard_map/ppermute | solution.py:31
  152.1 22.8 %collective-permute-start.31 = (bf16[128,2048]{1,0:T(8,128)(2,1)S(1)}, bf16[128,2048]{1,0:T(8,128)(2,1)S(1)}, u32[]{:S(2)}, u32[]{:S(2)}) collective-permute-start(bf16[128,2048]{1,0:T(8,128)(2,1)S(1)} %slice.672), channel_id=1, source_target_pairs={{0,16},{1,17},{2,18},{3,19},{4,20},{5,21},{6,22},{7,23},{8,24},{9,... | collective-permute-start | bytes 1572872 | tf_op jit(solution)/shard_map/ppermute | solution.py:31
  153.3 22.7 %collective-permute-start.32 = (bf16[128,2048]{1,0:T(8,128)(2,1)S(1)}, bf16[128,2048]{1,0:T(8,128)(2,1)S(1)}, u32[]{:S(2)}, u32[]{:S(2)}) collective-permute-start(bf16[128,2048]{1,0:T(8,128)(2,1)S(1)} %slice.673), channel_id=1, source_target_pairs={{0,24},{1,25},{2,26},{3,27},{4,28},{5,29},{6,30},{7,31},{8,16},{9,... | collective-permute-start | bytes 1572872 | tf_op jit(solution)/shard_map/ppermute | solution.py:31
  160.9 13.8 %collective-permute-start.13 = (bf16[64,2048]{1,0:T(8,128)(2,1)S(1)}, bf16[64,2048]{1,0:T(8,128)(2,1)S(1)}, u32[]{:S(2)}, u32[]{:S(2)}) collective-permute-start(bf16[64,2048]{1,0:T(8,128)(2,1)S(1)} %get-tuple-element.167), channel_id=1, source_target_pairs={{0,2},{1,3},{2,4},{3,5},{4,6},{5,7},{6,0},{7,1},{8,10},{9,11},{10,... | collective-permute-start | bytes 786440 | tf_op jit(solution)/shard_map/ppermute | solution.py:31
  174.8 25.4 %collective-permute-start.15 = (bf16[256,2048]{1,0:T(8,128)(2,1)S(1)}, bf16[256,2048]{1,0:T(8,128)(2,1)S(1)}, u32[]{:S(2)}, u32[]{:S(2)}) collective-permute-start(bf16[256,2048]{1,0:T(8,128)(2,1)S(1)} %pad_maximum_fusion.3), channel_id=1, source_target_pairs={{0,16},{1,17},{2,18},{3,19},{4,20},{5,21},{6,22},{7,23},{8,24},{9,... | collective-permute-start | bytes 3145736 | tf_op jit(solution)/shard_map/ppermute | solution.py:31
  177.1 25.1 %collective-permute-start.14 = (bf16[256,2048]{1,0:T(8,128)(2,1)S(1)}, bf16[256,2048]{1,0:T(8,128)(2,1)S(1)}, u32[]{:S(2)}, u32[]{:S(2)}) collective-permute-start(bf16[256,2048]{1,0:T(8,128)(2,1)S(1)} %pad_maximum_fusion.3), channel_id=1, source_target_pairs={{0,24},{1,25},{2,26},{3,27},{4,28},{5,29},{6,30},{7,31},{8,16},{9,... | collective-permute-start | bytes 3145736 | tf_op jit(solution)/shard_map/ppermute | solution.py:31
  182.2 105.0 %collective-permute-start.33 = (bf16[1024,2048]{1,0:T(8,128)(2,1)}, bf16[1024,2048]{1,0:T(8,128)(2,1)}, u32[]{:S(2)}, u32[]{:S(2)}) collective-permute-start(bf16[1024,2048]{1,0:T(8,128)(2,1)} %get-tuple-element.236), channel_id=1, source_target_pairs={{0,1},{1,0},{2,3},{3,2},{4,5},{5,4},{6,7},{7,6},{8,9},{9,8},{10,11... | collective-permute-start | bytes 12582920 | tf_op jit(solution)/shard_map/ppermute | solution.py:31
  200.3 14.0 %collective-permute-start.16 = (bf16[128,2048]{1,0:T(8,128)(2,1)S(1)}, bf16[128,2048]{1,0:T(8,128)(2,1)S(1)}, u32[]{:S(2)}, u32[]{:S(2)}) collective-permute-start(bf16[128,2048]{1,0:T(8,128)(2,1)S(1)} %slice.662), channel_id=1, source_target_pairs={{0,16},{1,17},{2,18},{3,19},{4,20},{5,21},{6,22},{7,23},{8,24},{9,... | collective-permute-start | bytes 1572872 | tf_op jit(solution)/shard_map/ppermute | solution.py:31
  202.2 13.7 %collective-permute-start.17 = (bf16[128,2048]{1,0:T(8,128)(2,1)S(1)}, bf16[128,2048]{1,0:T(8,128)(2,1)S(1)}, u32[]{:S(2)}, u32[]{:S(2)}) collective-permute-start(bf16[128,2048]{1,0:T(8,128)(2,1)S(1)} %slice.663), channel_id=1, source_target_pairs={{0,24},{1,25},{2,26},{3,27},{4,28},{5,29},{6,30},{7,31},{8,16},{9,... | collective-permute-start | bytes 1572872 | tf_op jit(solution)/shard_map/ppermute | solution.py:31
  218.0 74.2 %collective-permute-start.18 = (bf16[1024,2048]{1,0:T(8,128)(2,1)}, bf16[1024,2048]{1,0:T(8,128)(2,1)}, u32[]{:S(2)}, u32[]{:S(2)}) collective-permute-start(bf16[1024,2048]{1,0:T(8,128)(2,1)} %get-tuple-element.232), channel_id=1, source_target_pairs={{0,1},{1,0},{2,3},{3,2},{4,5},{5,4},{6,7},{7,6},{8,9},{9,8},{10,11... | collective-permute-start | bytes 12582920 | tf_op jit(solution)/shard_map/ppermute | solution.py:31
  220.3 39.5 %collective-permute-start.22 = (bf16[512,1664]{1,0:T(8,128)(2,1)}, bf16[512,1664]{1,0:T(8,128)(2,1)}, u32[]{:S(2)}, u32[]{:S(2)}) collective-permute-start(bf16[512,1664]{1,0:T(8,128)(2,1)} %maximum_select_fusion.3), channel_id=1, source_target_pairs={{0,32},{1,33},{2,34},{3,35},{4,36},{5,37},{6,38},{7,39},{8,40},{9,... | collective-permute-start | bytes 5111816 | tf_op jit(solution)/shard_map/ppermute | solution.py:31
  220.3 42.3 %collective-permute-start.21 = (bf16[512,1664]{1,0:T(8,128)(2,1)}, bf16[512,1664]{1,0:T(8,128)(2,1)}, u32[]{:S(2)}, u32[]{:S(2)}) collective-permute-start(bf16[512,1664]{1,0:T(8,128)(2,1)} %maximum_select_fusion.3), channel_id=1, source_target_pairs={{0,96},{1,97},{2,98},{3,99},{4,100},{5,101},{6,102},{7,103},{8,104... | collective-permute-start | bytes 5111816 | tf_op jit(solution)/shard_map/ppermute | solution.py:31
  261.0 20.1 %collective-permute-start.23 = (bf16[256,1664]{1,0:T(8,128)(2,1)S(1)}, bf16[256,1664]{1,0:T(8,128)(2,1)S(1)}, u32[]{:S(2)}, u32[]{:S(2)}) collective-permute-start(bf16[256,1664]{1,0:T(8,128)(2,1)S(1)} %slice.664), channel_id=1, source_target_pairs={{0,32},{1,33},{2,34},{3,35},{4,36},{5,37},{6,38},{7,39},{8,40},{9,... | collective-permute-start | bytes 2555912 | tf_op jit(solution)/shard_map/ppermute | solution.py:31
  263.8 21.4 %collective-permute-start.24 = (bf16[256,1664]{1,0:T(8,128)(2,1)S(1)}, bf16[256,1664]{1,0:T(8,128)(2,1)S(1)}, u32[]{:S(2)}, u32[]{:S(2)}) collective-permute-start(bf16[256,1664]{1,0:T(8,128)(2,1)S(1)} %slice.665), channel_id=1, source_target_pairs={{0,96},{1,97},{2,98},{3,99},{4,100},{5,101},{6,102},{7,103},{8,104... | collective-permute-start | bytes 2555912 | tf_op jit(solution)/shard_map/ppermute | solution.py:31
  365.4 16.4 %collective-permute-start.35 = (bf16[128,2048]{1,0:T(8,128)(2,1)}, bf16[128,2048]{1,0:T(8,128)(2,1)S(1)}, u32[]{:S(2)}, u32[]{:S(2)}) collective-permute-start(bf16[128,2048]{1,0:T(8,128)(2,1)} %get-tuple-element.188), channel_id=1, source_target_pairs={{0,16},{1,17},{2,18},{3,19},{4,20},{5,21},{6,22},{7,23},{8,24},{9,... | collective-permute-start | bytes 1572872 | tf_op jit(solution)/shard_map/ppermute | solution.py:31
  368.0 15.2 %collective-permute-start.37 = (bf16[128,2048]{1,0:T(8,128)(2,1)}, bf16[128,2048]{1,0:T(8,128)(2,1)}, u32[]{:S(2)}, u32[]{:S(2)}) collective-permute-start(bf16[128,2048]{1,0:T(8,128)(2,1)} %get-tuple-element.189), channel_id=1, source_target_pairs={{0,24},{1,25},{2,26},{3,27},{4,28},{5,29},{6,30},{7,31},{8,16},{9,... | collective-permute-start | bytes 1572872 | tf_op jit(solution)/shard_map/ppermute | solution.py:31
  384.8 25.4 %collective-permute-start.36 = (bf16[256,2048]{1,0:T(8,128)(2,1)S(1)}, bf16[256,2048]{1,0:T(8,128)(2,1)S(1)}, u32[]{:S(2)}, u32[]{:S(2)}) collective-permute-start(bf16[256,2048]{1,0:T(8,128)(2,1)S(1)} %pad_maximum_fusion.4), channel_id=1, source_target_pairs={{0,16},{1,17},{2,18},{3,19},{4,20},{5,21},{6,22},{7,23},{8,24},{9,... | collective-permute-start | bytes 3145736 | tf_op jit(solution)/shard_map/ppermute | solution.py:31
  386.7 24.5 %collective-permute-start.38 = (bf16[256,2048]{1,0:T(8,128)(2,1)S(1)}, bf16[256,2048]{1,0:T(8,128)(2,1)S(1)}, u32[]{:S(2)}, u32[]{:S(2)}) collective-permute-start(bf16[256,2048]{1,0:T(8,128)(2,1)S(1)} %pad_maximum_fusion.5), channel_id=1, source_target_pairs={{0,24},{1,25},{2,26},{3,27},{4,28},{5,29},{6,30},{7,31},{8,16},{9,... | collective-permute-start | bytes 3145736 | tf_op jit(solution)/shard_map/ppermute | solution.py:31
  411.8 13.6 %collective-permute-start.39 = (bf16[64,2048]{1,0:T(8,128)(2,1)S(1)}, bf16[64,2048]{1,0:T(8,128)(2,1)S(1)}, u32[]{:S(2)}, u32[]{:S(2)}) collective-permute-start(bf16[64,2048]{1,0:T(8,128)(2,1)S(1)} %get-tuple-element.229), channel_id=1, source_target_pairs={{0,2},{1,3},{2,4},{3,5},{4,6},{5,7},{6,0},{7,1},{8,10},{9,11},{10,... | collective-permute-start | bytes 786440 | tf_op jit(solution)/shard_map/ppermute | solution.py:31
  411.9 13.5 %collective-permute-start.40 = (bf16[64,2048]{1,0:T(8,128)(2,1)S(1)}, bf16[64,2048]{1,0:T(8,128)(2,1)S(1)}, u32[]{:S(2)}, u32[]{:S(2)}) collective-permute-start(bf16[64,2048]{1,0:T(8,128)(2,1)S(1)} %get-tuple-element.231), channel_id=1, source_target_pairs={{0,4},{1,5},{2,6},{3,7},{4,0},{5,1},{6,2},{7,3},{8,12},{9,13},{10,... | collective-permute-start | bytes 786440 | tf_op jit(solution)/shard_map/ppermute | solution.py:31
  412.0 14.0 %collective-permute-start.41 = (bf16[64,2048]{1,0:T(8,128)(2,1)S(1)}, bf16[64,2048]{1,0:T(8,128)(2,1)S(1)}, u32[]{:S(2)}, u32[]{:S(2)}) collective-permute-start(bf16[64,2048]{1,0:T(8,128)(2,1)S(1)} %get-tuple-element.230), channel_id=1, source_target_pairs={{0,6},{1,7},{2,0},{3,1},{4,2},{5,3},{6,4},{7,5},{8,14},{9,15},{10,... | collective-permute-start | bytes 786440 | tf_op jit(solution)/shard_map/ppermute | solution.py:31
  429.4 26.3 %collective-permute-start.54 = (bf16[64,2048]{1,0:T(8,128)(2,1)}, bf16[64,2048]{1,0:T(8,128)(2,1)}, u32[]{:S(2)}, u32[]{:S(2)}) collective-permute-start(bf16[64,2048]{1,0:T(8,128)(2,1)} %get-tuple-element.158), channel_id=1, source_target_pairs={{0,6},{1,7},{2,0},{3,1},{4,2},{5,3},{6,4},{7,5},{8,14},{9,15},{10,... | collective-permute-start | bytes 786440 | tf_op jit(solution)/shard_map/ppermute | solution.py:31
  431.7 35.5 %collective-permute-start.55 = (bf16[64,2048]{1,0:T(8,128)(2,1)}, bf16[64,2048]{1,0:T(8,128)(2,1)}, u32[]{:S(2)}, u32[]{:S(2)}) collective-permute-start(bf16[64,2048]{1,0:T(8,128)(2,1)} %get-tuple-element.158), channel_id=1, source_target_pairs={{0,4},{1,5},{2,6},{3,7},{4,0},{5,1},{6,2},{7,3},{8,12},{9,13},{10,... | collective-permute-start | bytes 786440 | tf_op jit(solution)/shard_map/ppermute | solution.py:31
  431.7 43.3 %collective-permute-start.56 = (bf16[64,2048]{1,0:T(8,128)(2,1)}, bf16[64,2048]{1,0:T(8,128)(2,1)}, u32[]{:S(2)}, u32[]{:S(2)}) collective-permute-start(bf16[64,2048]{1,0:T(8,128)(2,1)} %get-tuple-element.158), channel_id=1, source_target_pairs={{0,2},{1,3},{2,4},{3,5},{4,6},{5,7},{6,0},{7,1},{8,10},{9,11},{10,... | collective-permute-start | bytes 786440 | tf_op jit(solution)/shard_map/ppermute | solution.py:31
  459.1 38.9 %collective-permute-start.94 = (bf16[256,1536]{1,0:T(8,128)(2,1)}, bf16[256,1536]{1,0:T(8,128)(2,1)}, u32[]{:S(2)}, u32[]{:S(2)}) collective-permute-start(bf16[256,1536]{1,0:T(8,128)(2,1)} %get-tuple-element.209), channel_id=1, source_target_pairs={{0,32},{1,33},{2,34},{3,35},{4,36},{5,37},{6,38},{7,39},{8,40},{9,... | collective-permute-start | bytes 2359304 | tf_op jit(solution)/shard_map/ppermute | solution.py:31
  471.1 28.7 %collective-permute-start.96 = (bf16[256,1536]{1,0:T(8,128)(2,1)}, bf16[256,1536]{1,0:T(8,128)(2,1)}, u32[]{:S(2)}, u32[]{:S(2)}) collective-permute-start(bf16[256,1536]{1,0:T(8,128)(2,1)} %get-tuple-element.210), channel_id=1, source_target_pairs={{0,96},{1,97},{2,98},{3,99},{4,100},{5,101},{6,102},{7,103},{8,104... | collective-permute-start | bytes 2359304 | tf_op jit(solution)/shard_map/ppermute | solution.py:31
  474.4 18.7 %collective-permute-start.82 = (f32[272,128]{1,0:T(8,128)S(1)}, f32[272,128]{1,0:T(8,128)S(1)}, u32[]{:S(2)}, u32[]{:S(2)}) collective-permute-start(f32[272,128]{1,0:T(8,128)S(1)} %add_add_fusion.1), channel_id=1, source_target_pairs={{0,64},{1,65},{2,66},{3,67},{4,68},{5,69},{6,70},{7,71},{8,72},{9,... | collective-permute-start | bytes 417800 | tf_op jit(solution)/shard_map/ppermute | solution.py:31
  475.0 21.7 %collective-permute-start.83 = (f32[272,128]{1,0:T(8,128)S(1)}, f32[272,128]{1,0:T(8,128)S(1)}, u32[]{:S(2)}, u32[]{:S(2)}) collective-permute-start(f32[272,128]{1,0:T(8,128)S(1)} %add_add_fusion.1), channel_id=1, source_target_pairs={{0,96},{1,97},{2,98},{3,99},{4,100},{5,101},{6,102},{7,103},{8,104... | collective-permute-start | bytes 417800 | tf_op jit(solution)/shard_map/ppermute | solution.py:31
  482.7 145.3 %collective-permute-start.42 = (bf16[1024,2048]{1,0:T(8,128)(2,1)}, bf16[1024,2048]{1,0:T(8,128)(2,1)}, u32[]{:S(2)}, u32[]{:S(2)}) collective-permute-start(bf16[1024,2048]{1,0:T(8,128)(2,1)} %slice.558), channel_id=1, source_target_pairs={{0,1},{1,0},{2,3},{3,2},{4,5},{5,4},{6,7},{7,6},{8,9},{9,8},{10,11... | collective-permute-start | bytes 12582920 | tf_op jit(solution)/shard_map/ppermute | solution.py:31
  499.7 43.1 %collective-permute-start.95 = (bf16[512,1536]{1,0:T(8,128)(2,1)S(1)}, bf16[512,1536]{1,0:T(8,128)(2,1)S(1)}, u32[]{:S(2)}, u32[]{:S(2)}) collective-permute-start(bf16[512,1536]{1,0:T(8,128)(2,1)S(1)} %fusion.27), channel_id=1, source_target_pairs={{0,32},{1,33},{2,34},{3,35},{4,36},{5,37},{6,38},{7,39},{8,40},{9,... | collective-permute-start | bytes 4718600 | tf_op jit(solution)/shard_map/ppermute | solution.py:31
  502.4 40.5 %collective-permute-start.97 = (bf16[512,1536]{1,0:T(8,128)(2,1)S(1)}, bf16[512,1536]{1,0:T(8,128)(2,1)S(1)}, u32[]{:S(2)}, u32[]{:S(2)}) collective-permute-start(bf16[512,1536]{1,0:T(8,128)(2,1)S(1)} %pad_maximum_fusion.2), channel_id=1, source_target_pairs={{0,96},{1,97},{2,98},{3,99},{4,100},{5,101},{6,102},{7,103},{8,104... | collective-permute-start | bytes 4718600 | tf_op jit(solution)/shard_map/ppermute | solution.py:31
  515.0 14.9 %collective-permute-start.58 = (bf16[512,512]{1,0:T(8,128)(2,1)S(1)}, bf16[512,512]{1,0:T(8,128)(2,1)S(1)}, u32[]{:S(2)}, u32[]{:S(2)}) collective-permute-start(bf16[512,512]{1,0:T(8,128)(2,1)S(1)} %slice.966), channel_id=1, source_target_pairs={{8,0},{9,1},{10,2},{11,3},{12,4},{13,5},{14,6},{15,7},{24,16},{25,... | collective-permute-start | bytes 1572872 | tf_op jit(solution)/shard_map/ppermute | solution.py:31
  536.1 22.3 %collective-permute-start.59 = (bf16[256,2048]{1,0:T(8,128)(2,1)S(1)}, bf16[256,2048]{1,0:T(8,128)(2,1)S(1)}, u32[]{:S(2)}, u32[]{:S(2)}) collective-permute-start(bf16[256,2048]{1,0:T(8,128)(2,1)S(1)} %constant_dynamic-slice_fusion.5), channel_id=1, source_target_pairs={{0,1},{1,0},{2,3},{3,2},{4,5},{5,4},{6,7},{7,6},{8,9},{9,8},{10,11... | collective-permute-start | bytes 3145736 | tf_op jit(solution)/shard_map/ppermute | solution.py:31
  539.9 14.5 %collective-permute-start.67 = (bf16[256,1024]{1,0:T(8,128)(2,1)S(1)}, bf16[256,1024]{1,0:T(8,128)(2,1)S(1)}, u32[]{:S(2)}, u32[]{:S(2)}) collective-permute-start(bf16[256,1024]{1,0:T(8,128)(2,1)S(1)} %get-tuple-element.221), channel_id=1, source_target_pairs={{0,32},{1,33},{2,34},{3,35},{4,36},{5,37},{6,38},{7,39},{8,40},{9,... | collective-permute-start | bytes 1572872 | tf_op jit(solution)/shard_map/ppermute | solution.py:31
  542.8 15.3 %collective-permute-start.69 = (bf16[256,1024]{1,0:T(8,128)(2,1)S(1)}, bf16[256,1024]{1,0:T(8,128)(2,1)S(1)}, u32[]{:S(2)}, u32[]{:S(2)}) collective-permute-start(bf16[256,1024]{1,0:T(8,128)(2,1)S(1)} %get-tuple-element.222), channel_id=1, source_target_pairs={{0,96},{1,97},{2,98},{3,99},{4,100},{5,101},{6,102},{7,103},{8,104... | collective-permute-start | bytes 1572872 | tf_op jit(solution)/shard_map/ppermute | solution.py:31
  544.0 31.3 %collective-permute-start.98 = (bf16[256,1536]{1,0:T(8,128)(2,1)S(1)}, bf16[256,1536]{1,0:T(8,128)(2,1)S(1)}, u32[]{:S(2)}, u32[]{:S(2)}) collective-permute-start(bf16[256,1536]{1,0:T(8,128)(2,1)S(1)} %get-tuple-element.207), channel_id=1, source_target_pairs={{0,24},{1,25},{2,26},{3,27},{4,28},{5,29},{6,30},{7,31},{8,16},{9,... | collective-permute-start | bytes 2359304 | tf_op jit(solution)/shard_map/ppermute | solution.py:31
  560.9 13.5 %collective-permute-start.61 = (bf16[64,2048]{1,0:T(8,128)(2,1)S(1)}, bf16[64,2048]{1,0:T(8,128)(2,1)S(1)}, u32[]{:S(2)}, u32[]{:S(2)}) collective-permute-start(bf16[64,2048]{1,0:T(8,128)(2,1)S(1)} %get-tuple-element.225), channel_id=1, source_target_pairs={{0,4},{1,5},{2,6},{3,7},{4,0},{5,1},{6,2},{7,3},{8,12},{9,13},{10,... | collective-permute-start | bytes 786440 | tf_op jit(solution)/shard_map/ppermute | solution.py:31
  568.2 25.7 %collective-permute-start.100 = (bf16[256,1536]{1,0:T(8,128)(2,1)S(1)}, bf16[256,1536]{1,0:T(8,128)(2,1)S(1)}, u32[]{:S(2)}, u32[]{:S(2)}) collective-permute-start(bf16[256,1536]{1,0:T(8,128)(2,1)S(1)} %get-tuple-element.207), channel_id=1, source_target_pairs={{0,16},{1,17},{2,18},{3,19},{4,20},{5,21},{6,22},{7,23},{8,24},{9,... | collective-permute-start | bytes 2359304 | tf_op jit(solution)/shard_map/ppermute | solution.py:31
  574.5 19.4 %collective-permute-start.99 = (bf16[256,1536]{1,0:T(8,128)(2,1)S(1)}, bf16[256,1536]{1,0:T(8,128)(2,1)S(1)}, u32[]{:S(2)}, u32[]{:S(2)}) collective-permute-start(bf16[256,1536]{1,0:T(8,128)(2,1)S(1)} %get-tuple-element.206), channel_id=1, source_target_pairs={{0,8},{1,9},{2,10},{3,11},{4,12},{5,13},{6,14},{7,15},{8,0},{9,1},... | collective-permute-start | bytes 2359304 | tf_op jit(solution)/shard_map/ppermute | solution.py:31
  574.5 74.3 %collective-permute-start.68 = (bf16[512,1024]{1,0:T(8,128)(2,1)}, bf16[512,1024]{1,0:T(8,128)(2,1)}, u32[]{:S(2)}, u32[]{:S(2)}) collective-permute-start(bf16[512,1024]{1,0:T(8,128)(2,1)} %pad_maximum_fusion.8), channel_id=1, source_target_pairs={{0,32},{1,33},{2,34},{3,35},{4,36},{5,37},{6,38},{7,39},{8,40},{9,... | collective-permute-start | bytes 3145736 | tf_op jit(solution)/shard_map/ppermute | solution.py:31
  575.4 24.0 %collective-permute-start.84 = (f32[48,128]{1,0:T(8,128)S(1)}, f32[48,128]{1,0:T(8,128)S(1)}, u32[]{:S(2)}, u32[]{:S(2)}) collective-permute-start(f32[48,128]{1,0:T(8,128)S(1)} %maximum_bitcast_fusion.2), channel_id=1, source_target_pairs={{0,1},{1,0},{2,3},{3,2},{4,5},{5,4},{6,7},{7,6},{8,9},{9,8},{10,11... | collective-permute-start | bytes 73736 | tf_op jit(solution)/shard_map/ppermute | solution.py:31
  605.7 19.1 %collective-permute-start.88 = (f32[48,128]{1,0:T(8,128)S(1)}, f32[48,128]{1,0:T(8,128)S(1)}, u32[]{:S(2)}, u32[]{:S(2)}) collective-permute-start(f32[48,128]{1,0:T(8,128)S(1)} %add_add_fusion.5), channel_id=1, source_target_pairs={{0,16},{1,17},{2,18},{3,19},{4,20},{5,21},{6,22},{7,23},{8,24},{9,... | collective-permute-start | bytes 73736 | tf_op jit(solution)/shard_map/ppermute | solution.py:31
  624.7 25.7 %collective-permute-start.70 = (bf16[512,1024]{1,0:T(8,128)(2,1)}, bf16[512,1024]{1,0:T(8,128)(2,1)S(1)}, u32[]{:S(2)}, u32[]{:S(2)}) collective-permute-start(bf16[512,1024]{1,0:T(8,128)(2,1)} %pad_maximum_fusion.9), channel_id=1, source_target_pairs={{0,96},{1,97},{2,98},{3,99},{4,100},{5,101},{6,102},{7,103},{8,104... | collective-permute-start | bytes 3145736 | tf_op jit(solution)/shard_map/ppermute | solution.py:31
  628.1 18.1 %collective-permute-start.92 = (f32[48,128]{1,0:T(8,128)S(1)}, f32[48,128]{1,0:T(8,128)S(1)}, u32[]{:S(2)}, u32[]{:S(2)}) collective-permute-start(f32[48,128]{1,0:T(8,128)S(1)} %add_add_fusion.4), channel_id=1, source_target_pairs={{0,64},{1,65},{2,66},{3,67},{4,68},{5,69},{6,70},{7,71},{8,72},{9,... | collective-permute-start | bytes 73736 | tf_op jit(solution)/shard_map/ppermute | solution.py:31
  628.1 18.5 %collective-permute-start.93 = (f32[48,128]{1,0:T(8,128)S(1)}, f32[48,128]{1,0:T(8,128)S(1)}, u32[]{:S(2)}, u32[]{:S(2)}) collective-permute-start(f32[48,128]{1,0:T(8,128)S(1)} %add_add_fusion.4), channel_id=1, source_target_pairs={{0,96},{1,97},{2,98},{3,99},{4,100},{5,101},{6,102},{7,103},{8,104... | collective-permute-start | bytes 73736 | tf_op jit(solution)/shard_map/ppermute | solution.py:31
  634.7 30.9 %collective-permute-start.63 = (bf16[64,2048]{1,0:T(8,128)(2,1)}, bf16[64,2048]{1,0:T(8,128)(2,1)S(1)}, u32[]{:S(2)}, u32[]{:S(2)}) collective-permute-start(bf16[64,2048]{1,0:T(8,128)(2,1)} %get-tuple-element.155), channel_id=1, source_target_pairs={{0,6},{1,7},{2,0},{3,1},{4,2},{5,3},{6,4},{7,5},{8,14},{9,15},{10,... | collective-permute-start | bytes 786440 | tf_op jit(solution)/shard_map/ppermute | solution.py:31
  648.8 19.4 %collective-permute-start.64 = (bf16[64,2048]{1,0:T(8,128)(2,1)}, bf16[64,2048]{1,0:T(8,128)(2,1)S(1)}, u32[]{:S(2)}, u32[]{:S(2)}) collective-permute-start(bf16[64,2048]{1,0:T(8,128)(2,1)} %get-tuple-element.155), channel_id=1, source_target_pairs={{0,4},{1,5},{2,6},{3,7},{4,0},{5,1},{6,2},{7,3},{8,12},{9,13},{10,... | collective-permute-start | bytes 786440 | tf_op jit(solution)/shard_map/ppermute | solution.py:31
  650.4 38.5 %collective-permute-start.65 = (bf16[64,2048]{1,0:T(8,128)(2,1)}, bf16[64,2048]{1,0:T(8,128)(2,1)S(1)}, u32[]{:S(2)}, u32[]{:S(2)}) collective-permute-start(bf16[64,2048]{1,0:T(8,128)(2,1)} %get-tuple-element.155), channel_id=1, source_target_pairs={{0,2},{1,3},{2,4},{3,5},{4,6},{5,7},{6,0},{7,1},{8,10},{9,11},{10,... | collective-permute-start | bytes 786440 | tf_op jit(solution)/shard_map/ppermute | solution.py:31
  659.3 21.7 %collective-permute-start.44 = (bf16[256,2048]{1,0:T(8,128)(2,1)}, bf16[256,2048]{1,0:T(8,128)(2,1)}, u32[]{:S(2)}, u32[]{:S(2)}) collective-permute-start(bf16[256,2048]{1,0:T(8,128)(2,1)} %pad_maximum_fusion.6), channel_id=1, source_target_pairs={{0,16},{1,17},{2,18},{3,19},{4,20},{5,21},{6,22},{7,23},{8,24},{9,... | collective-permute-start | bytes 3145736 | tf_op jit(solution)/shard_map/ppermute | solution.py:31
  660.8 21.1 %collective-permute-start.46 = (bf16[256,2048]{1,0:T(8,128)(2,1)}, bf16[256,2048]{1,0:T(8,128)(2,1)}, u32[]{:S(2)}, u32[]{:S(2)}) collective-permute-start(bf16[256,2048]{1,0:T(8,128)(2,1)} %pad_maximum_fusion.7), channel_id=1, source_target_pairs={{0,24},{1,25},{2,26},{3,27},{4,28},{5,29},{6,30},{7,31},{8,16},{9,... | collective-permute-start | bytes 3145736 | tf_op jit(solution)/shard_map/ppermute | solution.py:31
  665.6 33.4 %collective-permute-start.71 = (bf16[128,1024]{0,1:T(8,128)(2,1)}, bf16[128,1024]{0,1:T(8,128)(2,1)}, u32[]{:S(2)}, u32[]{:S(2)}) collective-permute-start(bf16[128,1024]{0,1:T(8,128)(2,1)} %bitcast.88), channel_id=1, source_target_pairs={{0,16},{1,17},{2,18},{3,19},{4,20},{5,21},{6,22},{7,23},{8,24},{9,... | collective-permute-start | bytes 786440 | tf_op jit(solution)/shard_map/ppermute | solution.py:31
  668.2 30.8 %collective-permute-start.72 = (bf16[128,1024]{0,1:T(8,128)(2,1)}, bf16[128,1024]{0,1:T(8,128)(2,1)}, u32[]{:S(2)}, u32[]{:S(2)}) collective-permute-start(bf16[128,1024]{0,1:T(8,128)(2,1)} %bitcast.89), channel_id=1, source_target_pairs={{0,24},{1,25},{2,26},{3,27},{4,28},{5,29},{6,30},{7,31},{8,16},{9,... | collective-permute-start | bytes 786440 | tf_op jit(solution)/shard_map/ppermute | solution.py:31
  698.9 26.3 %collective-permute-start.66 = (bf16[256,2048]{1,0:T(8,128)(2,1)}, bf16[256,2048]{1,0:T(8,128)(2,1)S(1)}, u32[]{:S(2)}, u32[]{:S(2)}) collective-permute-start(bf16[256,2048]{1,0:T(8,128)(2,1)} %bitcast.73), channel_id=1, source_target_pairs={{0,1},{1,0},{2,3},{3,2},{4,5},{5,4},{6,7},{7,6},{8,9},{9,8},{10,11... | collective-permute-start | bytes 3145736 | tf_op jit(solution)/shard_map/ppermute | solution.py:31
  700.2 21.6 %collective-permute-start.73 = (bf16[256,1024]{0,1:T(8,128)(2,1)S(1)}, bf16[256,1024]{0,1:T(8,128)(2,1)S(1)}, u32[]{:S(2)}, u32[]{:S(2)}) collective-permute-start(bf16[256,1024]{0,1:T(8,128)(2,1)S(1)} %fusion.41), channel_id=1, source_target_pairs={{0,8},{1,9},{2,10},{3,11},{4,12},{5,13},{6,14},{7,15},{8,0},{9,1},... | collective-permute-start | bytes 1572872 | tf_op jit(solution)/shard_map/ppermute | solution.py:31
  705.4 15.0 %collective-permute-start.52 = (bf16[64,2048]{1,0:T(8,128)(2,1)S(1)}, bf16[64,2048]{1,0:T(8,128)(2,1)S(1)}, u32[]{:S(2)}, u32[]{:S(2)}) collective-permute-start(bf16[64,2048]{1,0:T(8,128)(2,1)S(1)} %get-tuple-element.161), channel_id=1, source_target_pairs={{0,2},{1,3},{2,4},{3,5},{4,6},{5,7},{6,0},{7,1},{8,10},{9,11},{10,... | collective-permute-start | bytes 786440 | tf_op jit(solution)/shard_map/ppermute | solution.py:31
  (134 other events, 905.8 us)

commit v2 on v1

--- a/solution.py
+++ b/solution.py
@@ -1,6 +1,9 @@
 import jax
 import jax.numpy as jnp
+import numpy as np
 from jax import lax
+from jax.experimental import pallas as pl
+from jax.experimental.pallas import tpu as pltpu
 from jax.sharding import PartitionSpec as P
 
 EPSILON = 1e-05
@@ -148,6 +151,427 @@
 
 def dot_tn(left, right):
     return lax.dot_general(left, right, (((0,), (0,)), ((), ())), preferred_element_type=F32)
+
+
+ANY = pl.BlockSpec(memory_space=pl.ANY)
+VMEM = pl.BlockSpec(memory_space=pltpu.VMEM)
+MIB = 1024 * 1024
+ROWS, WIDTH, HOME, HALF = 512, 2048, 64, 256
+WROWS, WCOLS = 272, 1152
+
+
+def places():
+    shard, ctx, tp = lax.axis_index("shard"), lax.axis_index("ctx"), lax.axis_index("tp")
+    return shard // 2, ctx * 2 + shard % 2, tp // 2, tp % 2
+
+
+def device(x, y, z, c):
+    x, y, z, c = lax.rem(x + 4, 4), lax.rem(y + 4, 4), lax.rem(z + 4, 4), lax.rem(c + 2, 2)
+    return {"shard": x * 2 + lax.rem(y, 2), "ctx": y // 2, "tp": z * 2 + c}
+
+
+class Links:
+    def __init__(self, send_sems, recv_sems):
+        self.here = places()
+        self.send_sems, self.recv_sems, self.made = send_sems, recv_sems, []
+
+    def send(self, source, target, dx=0, dy=0, dz=0, dc=0, start=True):
+        x, y, z, c = self.here
+        number = len(self.made)
+        copy = pltpu.make_async_remote_copy(
+            src_ref=source,
+            dst_ref=target,
+            send_sem=self.send_sems.at[number],
+            recv_sem=self.recv_sems.at[number],
+            device_id=device(x + dx, y + dy, z + dz, c + dc),
+            device_id_type=pl.DeviceIdType.MESH,
+        )
+        self.made.append(copy)
+        if start:
+            copy.start()
+        return copy
+
+    def finish(self):
+        for copy in self.made:
+            copy.wait_send()
+
+    def greet(self, steps):
+        x, y, z, c = self.here
+        barrier = pltpu.get_barrier_semaphore()
+        for dx, dy, dz, dc in steps:
+            pl.semaphore_signal(
+                barrier,
+                inc=1,
+                device_id=device(x + dx, y + dy, z + dz, c + dc),
+                device_id_type=pl.DeviceIdType.MESH,
+            )
+        pl.semaphore_wait(barrier, len(steps))
+
+
+STEPS_X = [(1, 0, 0, 0), (-1, 0, 0, 0)]
+STEPS_Y = [(0, 1, 0, 0), (0, -1, 0, 0), (0, 2, 0, 0)]
+STEPS_Z = [(0, 0, 1, 0), (0, 0, -1, 0), (0, 0, 2, 0)]
+STEPS_C = [(0, 0, 0, 1)]
+
+
+def arrived(copies):
+    for copy in copies:
+        copy.wait_recv()
+
+
+def turned(values, cosine, sine):
+    return values * cosine + pltpu.roll(values, 64, 1) * sine
+
+
+def spread(links, array, home_ref, y, z, c):
+    first, second = pl.ds(0, 32), pl.ds(32, 32)
+    y_after, y_before, y_far = lax.rem(y + 1, 4), lax.rem(y + 3, 4), lax.rem(y + 2, 4)
+    z_after, z_before, z_far = lax.rem(z + 1, 4), lax.rem(z + 3, 4), lax.rem(z + 2, 4)
+    p_one = [
+        links.send(home_ref.at[first], array.at[y, c, z, first], dz=d) for d in (1, -1, 2)
+    ]
+    q_one = [
+        links.send(home_ref.at[second], array.at[y, c, z, second], dy=d) for d in (1, -1, 2)
+    ]
+
+    def p_block(place):
+        return array.at[place, c, :, first]
+
+    def q_block(place):
+        return array.at[:, c, place, second]
+
+    arrived(p_one)
+    p_two = [links.send(p_block(y), p_block(y), dy=d) for d in (1, -1)]
+    sibling = [links.send(p_block(y), p_block(y), dc=1)]
+    arrived(q_one)
+    q_two = [links.send(q_block(z), q_block(z), dz=d) for d in (1, -1)]
+    sibling.append(links.send(q_block(z), q_block(z), dc=1))
+    p_two[0].wait_recv()
+    low, high = pl.ds(0, 2), pl.ds(2, 2)
+    ahead = array.at[y_before, c, low, first]
+    p_far = [links.send(ahead, ahead, dy=1)]
+    sibling.append(links.send(p_block(y_before), p_block(y_before), dc=1))
+    q_two[0].wait_recv()
+    ahead = array.at[low, c, z_before, second]
+    q_far = [links.send(ahead, ahead, dz=1)]
+    sibling.append(links.send(q_block(z_before), q_block(z_before), dc=1))
+    p_two[1].wait_recv()
+    behind = array.at[y_after, c, high, first]
+    p_far.append(links.send(behind, behind, dy=-1))
+    sibling.append(links.send(p_block(y_after), p_block(y_after), dc=1))
+    q_two[1].wait_recv()
+    behind = array.at[high, c, z_after, second]
+    q_far.append(links.send(behind, behind, dz=-1))
+    sibling.append(links.send(q_block(z_after), q_block(z_after), dc=1))
+    arrived(p_far)
+    sibling.append(links.send(p_block(y_far), p_block(y_far), dc=1))
+    arrived(q_far)
+    sibling.append(links.send(q_block(z_far), q_block(z_far), dc=1))
+    return sibling
+
+
+def front(
+    tok, own_weights, cosine_ref, sine_ref, segment_rows, segment_row, gate, up, down, grad, picked,
+    weights_out, experts_in, experts_out, grad_all, picked_all, moe_in_all,
+    normed_out, pre_out, rot_out, kv_out, mixed_out, lse_out, hidden_out, home_scale_out,
+    weights, kv_far, biases, accs, part, part_core, part_z, home_ref,
+    send_sems, recv_sems, local_sems,
+):
+    links = Links(send_sems, recv_sems)
+    x, y, z, c = links.here
+    ctx, y_low = y // 2, lax.rem(y, 2)
+    x_after, x_before = lax.rem(x + 1, 4), lax.rem(x + 3, 4)
+    y_after, y_before, y_far = lax.rem(y + 1, 4), lax.rem(y + 3, 4), lax.rem(y + 2, 4)
+    own = c * HALF
+    links.greet(STEPS_X + STEPS_Y + STEPS_Z + STEPS_C)
+
+    low, high = pl.ds(0, 128), pl.ds(128, WROWS - 128)
+    slot = weights.at[x, y_low]
+    pair = [
+        links.send(own_weights.at[low], slot.at[low], dy=1),
+        links.send(own_weights.at[high], slot.at[high], dy=-1),
+    ]
+    local = [pltpu.make_async_copy(own_weights, slot, local_sems.at[0])]
+
+    def mine(array, group):
+        return array.at[pl.ds(group * 4, 4)]
+
+    def columns(place, low_place):
+        return pl.ds(pl.multiple_of(place * 512 + low_place * 256, 256), 256)
+
+    local.append(
+        pltpu.make_async_copy(
+            mine(gate, y), experts_in.at[:, x, y_low, :, pl.ds(0, 128)], local_sems.at[1]
+        )
+    )
+    local.append(
+        pltpu.make_async_copy(
+            mine(up, y), experts_in.at[:, x, y_low, :, pl.ds(128, 128)], local_sems.at[2]
+        )
+    )
+    local.append(
+        pltpu.make_async_copy(
+            mine(down, y), experts_out.at[:, :, columns(x, y_low)], local_sems.at[3]
+        )
+    )
+    own_rows = pl.ds(pl.multiple_of(own, HALF), HALF)
+    local.append(pltpu.make_async_copy(grad, grad_all.at[y], local_sems.at[4]))
+    local.append(pltpu.make_async_copy(picked, picked_all.at[y], local_sems.at[5]))
+    for copy in local:
+        copy.start()
+    local[0].wait()
+    arrived(pair)
+    near = [links.send(weights.at[x], weights.at[x], dx=d) for d in (1, -1)]
+
+    expert_pair = []
+    for group, start, step in ((y_after, 0, 1), (y_before, 2, -1)):
+        some = pl.ds(group * 4 + start, 2)
+        there = pl.ds(start, 2)
+        expert_pair += [
+            links.send(
+                gate.at[some], experts_in.at[there, x, y_low, :, pl.ds(0, 128)], dy=step
+            ),
+            links.send(
+                up.at[some], experts_in.at[there, x, y_low, :, pl.ds(128, 128)], dy=step
+            ),
+            links.send(down.at[some], experts_out.at[there, :, columns(x, y_low)], dy=step),
+        ]
+    grad_near = [
+        links.send(grad.at[own_rows], grad_all.at[y, own_rows], dy=d) for d in (1, -1)
+    ]
+    picked_near = [links.send(picked, picked_all.at[y], dy=d) for d in (1, -1, 2)]
+
+    rows_at = lax.broadcasted_iota(jnp.int32, (ROWS, ROWS), 0)
+    cols_at = lax.broadcasted_iota(jnp.int32, (ROWS, ROWS), 1)
+    own_first = pl.ds(pl.multiple_of(ctx * ROWS, ROWS), ROWS)
+    same = segment_rows[own_first, :] == segment_row[:, own_first]
+    biases[0] = jnp.where(same & (rows_at >= cols_at), 0.0, MASKED_SCORE)
+    earlier = segment_rows[own_first, :] == segment_row[:, pl.ds(0, ROWS)]
+    biases[1] = jnp.where(earlier, 0.0, MASKED_SCORE)
+    tokens = tok[...].astype(F32)
+    scale_one = rms_scale(tokens)
+
+    near[0].wait_recv()
+    far = [links.send(weights.at[x_before, 0], weights.at[x_before, 0], dx=1)]
+    near[1].wait_recv()
+    far.append(links.send(weights.at[x_after, 1], weights.at[x_after, 1], dx=-1))
+    arrived(far)
+    for copy in local[1:4]:
+        copy.wait()
+    arrived(expert_pair)
+
+    def expert_blocks(place, low_place=None):
+        if low_place is None:
+            cols = pl.ds(pl.multiple_of(place * 512, 512), 512)
+            return experts_in.at[:, place], experts_out.at[:, :, cols]
+        return experts_in.at[:, place, low_place], experts_out.at[:, :, columns(place, low_place)]
+
+    expert_near = [
+        [links.send(block, block, dx=d) for block in expert_blocks(x)] for d in (1, -1)
+    ]
+
+    gain_blocks = [weights[s // 2, s % 2, 256:272, 0:256].astype(F32) for s in range(8)]
+    gains = jnp.concatenate([block[0:1] for block in gain_blocks], axis=1)
+    moe_gains = jnp.concatenate([block[1:2] for block in gain_blocks], axis=1)
+    head_gains = sum(block[:, 0:128] for block in gain_blocks)
+    normed_out[...] = (tokens * scale_one * gains).astype(BF)
+
+    def project(column):
+        block = weights[:, :, 0:256, column * 256 : column * 256 + 256].reshape(WIDTH, 256)
+        return jnp.dot(normed_out[...], block, preferred_element_type=F32)
+
+    cosine, sine = cosine_ref[own_first, :], sine_ref[own_first, :]
+
+    def heads(pre, first_gain, base):
+        for h in range(2):
+            part_h = pre[:, h * 128 : h * 128 + 128]
+            unit = part_h * rms_scale(part_h) * head_gains[first_gain + h : first_gain + h + 1]
+            rot_out[:, base + h * 128 : base + h * 128 + 128] = turned(unit, cosine, sine).astype(BF)
+
+    key_pre = project(1)
+    pre_out[:, 256:512] = key_pre
+    heads(key_pre, 4, 256)
+    kv_out[:, 0:256] = rot_out[:, 256:512]
+    kv_out[:, 256:512] = project(2).astype(BF)
+    later = links.send(kv_out, kv_far, dy=2, start=False)
+
+    @pl.when(ctx == 0)
+    def _():
+        later.start()
+
+    query_pre = project(0)
+    pre_out[:, 0:256] = query_pre
+    heads(query_pre, 2, 0)
+    score_scale = 128 ** (-0.5)
+    peaks, totals = [], []
+    for h in range(2):
+        lane = slice(h * 128, h * 128 + 128)
+        scores = dot_nt(rot_out[:, lane], kv_out[:, lane]) * score_scale + biases[0]
+        peak = jnp.max(scores, axis=-1, keepdims=True)
+        exponents = jnp.exp(scores - peak)
+        lse_out[h] = jnp.broadcast_to(peak, (ROWS, 128))
+        lse_out[2 + h] = jnp.broadcast_to(
+            jnp.sum(exponents, axis=-1, keepdims=True), (ROWS, 128)
+        )
+        accs[h] = dot(exponents.astype(BF), kv_out[:, 256 + h * 128 : 384 + h * 128])
+
+    arrived(grad_near)
+    grad_lane = grad_all.at[:, own_rows]
+    quarter = pl.multiple_of(own, HALF)
+    first_half, second_half = pl.ds(quarter, 128), pl.ds(pl.multiple_of(quarter + 128, 128), 128)
+    grad_far = [
+        links.send(grad_all.at[y_before, first_half], grad_all.at[y_before, first_half], dy=1),
+        links.send(grad_all.at[y_after, second_half], grad_all.at[y_after, second_half], dy=-1),
+    ]
+    siblings = [
+        links.send(grad_all.at[place, own_rows], grad_all.at[place, own_rows], dc=1)
+        for place in (y_before, y_after)
+    ]
+
+    @pl.when(ctx == 1)
+    def _():
+        later.wait_recv()
+        for h in range(2):
+            lane = slice(h * 128, h * 128 + 128)
+            scores = dot_nt(rot_out[:, lane], kv_far[:, lane]) * score_scale + biases[1]
+            old_peak = lse_out[h][:, 0:1]
+            peak = jnp.maximum(old_peak, jnp.max(scores, axis=-1, keepdims=True))
+            exponents = jnp.exp(scores - peak)
+            old = jnp.exp(old_peak - peak)
+            lse_out[h] = jnp.broadcast_to(peak, (ROWS, 128))
+            lse_out[2 + h] = lse_out[2 + h] * old + jnp.sum(exponents, axis=-1, keepdims=True)
+            accs[h] = accs[h] * old + dot(
+                exponents.astype(BF), kv_far[:, 256 + h * 128 : 384 + h * 128]
+            )
+
+    for h in range(2):
+        total = lse_out[2 + h]
+        mixed_out[:, h * 128 : h * 128 + 128] = (accs[h] / total).astype(BF)
+        lse_out[h] = lse_out[h] + jnp.log(total)
+
+    other = pl.multiple_of((1 - c) * HALF, HALF)
+    give_rows = mixed_out[pl.ds(other, HALF), :]
+    for s in range(8):
+        block = weights[s // 2, s % 2, 0:256, 896:1152]
+        part[1, :, s * 256 : s * 256 + 256] = dot(give_rows, block).astype(BF)
+    core_sum = links.send(part.at[1], part_core, dc=1)
+    keep_rows = mixed_out[pl.ds(quarter, HALF), :]
+    for s in range(8):
+        block = weights[s // 2, s % 2, 0:256, 896:1152]
+        part[0, :, s * 256 : s * 256 + 256] = dot(keep_rows, block).astype(BF)
+    core_sum.wait_recv()
+    part[0] = (part[0].astype(F32) + part_core[...].astype(F32)).astype(BF)
+    z_sum = []
+    for k, d in enumerate((1, -1, 2)):
+        there = pl.multiple_of(lax.rem(z + d + 4, 4) * HOME, HOME)
+        z_sum.append(links.send(part.at[0, pl.ds(there, HOME)], part_z.at[k], dz=d))
+
+    for copies in expert_near:
+        arrived(copies)
+    expert_far = [links.send(block, block, dx=1) for block in expert_blocks(x_before, 0)]
+    expert_far += [links.send(block, block, dx=-1) for block in expert_blocks(x_after, 1)]
+    arrived(grad_far)
+    siblings.append(links.send(grad_all.at[y_far, own_rows], grad_all.at[y_far, own_rows], dc=1))
+
+    arrived(z_sum)
+    home_first = pl.multiple_of(quarter + z * HOME, HOME)
+    home_rows = pl.ds(home_first, HOME)
+    summed = part[0, pl.ds(pl.multiple_of(z * HOME, HOME), HOME), :].astype(F32)
+    for k in range(3):
+        summed = summed + part_z[k].astype(F32)
+    home_tokens = tok[home_rows, :].astype(F32)
+    hidden = home_tokens + summed
+    hidden_out[...] = hidden
+    home_scale_out[...] = jnp.broadcast_to(rms_scale(home_tokens), (HOME, 128))
+    home_ref[...] = (hidden * rms_scale(hidden) * moe_gains).astype(BF)
+    place_home = pltpu.make_async_copy(home_ref, moe_in_all.at[y, c, z], local_sems.at[6])
+    place_home.start()
+    keep_weights = pltpu.make_async_copy(weights, weights_out, local_sems.at[7])
+    keep_weights.start()
+    place_home.wait()
+    siblings += spread(links, moe_in_all, home_ref, y, z, c)
+    arrived(expert_far)
+    arrived(picked_near)
+    arrived(siblings)
+    local[4].wait()
+    local[5].wait()
+    keep_weights.wait()
+
+    for copy in links.made:
+        if copy is not later:
+            copy.wait_send()
+
+    @pl.when(ctx == 0)
+    def _():
+        later.wait_send()
+
+
+FRONT_COPIES = 6 + 14 + 8 + 3 + 1 + 4 + 24
+
+
+def run_front(tok, own_weights, tables, segments, gate, up, down, grad, picked):
+    shape = jax.ShapeDtypeStruct
+    outs = (
+        (shape((4, 2, WROWS, WCOLS), BF), ANY),
+        (shape((4, 4, 2, 256, 256), BF), ANY),
+        (shape((4, 128, WIDTH), BF), ANY),
+        (shape((4, ROWS, WIDTH), BF), ANY),
+        (shape((4, ROWS, 128), BF), ANY),
+        (shape((4, 2, 4, HOME, WIDTH), BF), ANY),
+        (shape((ROWS, WIDTH), BF), VMEM),
+        (shape((ROWS, 512), F32), VMEM),
+        (shape((ROWS, 512), BF), VMEM),
+        (shape((ROWS, 512), BF), VMEM),
+        (shape((ROWS, 256), BF), VMEM),
+        (shape((4, ROWS, 128), F32), VMEM),
+        (shape((HOME, WIDTH), F32), VMEM),
+        (shape((HOME, 128), F32), VMEM),
+    )
+    return pl.pallas_call(
+        front,
+        out_shape=[o for o, _ in outs],
+        in_specs=[VMEM] * 6 + [ANY] * 5,
+        out_specs=[spec for _, spec in outs],
+        scratch_shapes=[
+            pltpu.VMEM((4, 2, WROWS, WCOLS), BF),
+            pltpu.VMEM((ROWS, 512), BF),
+            pltpu.VMEM((2, ROWS, ROWS), F32),
+            pltpu.VMEM((2, ROWS, 128), F32),
+            pltpu.VMEM((2, HALF, WIDTH), BF),
+            pltpu.VMEM((HALF, WIDTH), BF),
+            pltpu.VMEM((3, HOME, WIDTH), BF),
+            pltpu.VMEM((HOME, WIDTH), BF),
+            pltpu.SemaphoreType.DMA((FRONT_COPIES,)),
+            pltpu.SemaphoreType.DMA((FRONT_COPIES,)),
+            pltpu.SemaphoreType.DMA((8,)),
+        ],
+        compiler_params=pltpu.CompilerParams(
+            collective_id=1, has_side_effects=True, vmem_limit_bytes=56 * MIB
+        ),
+        name="front",
+    )(
+        tok,
+        own_weights,
+        jnp.asarray(tables[0]),
+        jnp.asarray(tables[1]),
+        segments.reshape(-1, 1),
+        segments,
+        gate,
+        up,
+        down,
+        grad,
+        picked,
+    )
+
+
+def turn_tables():
+    frequency = ROPE_BASE ** (-(np.arange(0, 128, 2, dtype=np.float64) / 128))
+    angles = np.arange(1024, dtype=np.float64)[:, None] * frequency[None, :]
+    cosine, sine = np.cos(angles), np.sin(angles)
+    return (
+        np.concatenate([cosine, cosine], axis=1).astype(np.float32),
+        np.concatenate([-sine, sine], axis=1).astype(np.float32),
+    )
 
 
 def body(
@@ -185,12 +609,6 @@
         lane = in_order(direct_gather(part, "z"), z).reshape(4 * part.shape[0], -1)
         return with_partner(lane, hop(lane, dc=1), core)
 
-    def gather_tokens(part):
-        lane = jnp.concatenate(direct_gather(part, "z"), axis=0)
-        near = ring_gather(lane, "y")
-        mine = jnp.concatenate(near, axis=0)
-        return jnp.concatenate([mine, hop(mine, dc=1)], axis=0)
-
     def home_sum(terms):
         keep = lax.dynamic_slice_in_dim(terms, core * 256, 256, 0)
         give = lax.dynamic_slice_in_dim(terms, (1 - core) * 256, 256, 0)
@@ -198,99 +616,71 @@
         return direct_scatter(by_distance(lane, z), "z")
 
     def tokens_sum(terms):
-        half = 2 * rows
-        lane = added(terms[:half], hop(terms[half:], dc=1)).astype(BF)
-        mine = ring_scatter([lane[256 * k : 256 * k + 256] for k in range(4)], "y").astype(BF)
-        return direct_scatter([mine[home * k : home * k + home] for k in range(4)], "z")
-
-    small = jnp.zeros((256, 128), BF)
-    small = small.at[:, 0].set(attn_gain).at[:, 1].set(moe_gain)
-    head_gains = jnp.stack([query_gain, key_gain]).reshape(-1)
-    small = small.at[: head_gains.shape[0], 2].set(head_gains)
-    attn_own = jnp.concatenate([query_weight, key_weight, value_weight, small, out_weight.T], axis=1)
-    attn_pair = with_partner(
-        attn_own,
-        jnp.concatenate([hop(attn_own[:128], dy=1), hop(attn_own[128:], dy=-1)], axis=0),
-        y_low,
-    )
-    attn_all = in_order(ring_gather(attn_pair, "x"), x).reshape(width, -1)
-    w_stacked = attn_all[:, : 3 * local_width]
-    small_all = attn_all[:, 3 * local_width : 3 * local_width + 128]
-    w_out_t = attn_all[:, 3 * local_width + 128 :]
-    attn_gains = small_all[:, 0].astype(F32)
-    moe_gains = small_all[:, 1].astype(F32)
-    gains = small_all[:, 2].reshape(8, 256)[:, :64].reshape(8, 2, 2, 16)
-    gains = gains.transpose(1, 2, 0, 3).reshape(2, 2 * head_dim).astype(F32)
-    query_gains, key_gains = gains[0][None], gains[1][None]
-
-    def grouped(weight):
-        parted = weight.reshape(4, own_experts, 256, hidden_units)
-        return parted.transpose(0, 2, 1, 3).reshape(4, 256, span)
-
+        terms = terms.reshape(4, rows, -1)
+        keep = lax.dynamic_slice_in_dim(terms, core * 256, 256, 1)
+        give = lax.dynamic_slice_in_dim(terms, (1 - core) * 256, 256, 1)
+        lane = added(keep, hop(give, dc=1)).astype(BF)
+        mine = ring_scatter(by_distance(lane, y), "y").astype(BF).reshape(4, home, -1)
+        return direct_scatter(by_distance(mine, z), "z")
+
+    lanes = jnp.zeros((4, 128), BF)
+    head_gains = jnp.concatenate([query_gain, key_gain], axis=0)
+    lanes = lax.dynamic_update_slice_in_dim(lanes, head_gains, shard * 16, 1)
+    gain_rows = jnp.zeros((16, WCOLS), BF)
+    gain_rows = gain_rows.at[0, :256].set(attn_gain).at[1, :256].set(moe_gain)
+    gain_rows = gain_rows.at[2:6, :128].set(lanes)
     router_pad = jnp.pad(router_weight, ((0, 0), (0, 128 - experts)))
-    moe_groups = jnp.concatenate(
+    own_weights = jnp.concatenate(
         [
-            grouped(gate_weight),
-            grouped(up_weight),
-            jnp.broadcast_to(router_pad[None], (4, 256, 128)),
-            grouped(down_weight.transpose(0, 2, 1)),
+            jnp.concatenate([query_weight, key_weight, value_weight, router_pad, out_weight], axis=1),
+            gain_rows,
         ],
-        axis=2,
-    )
-    moe_groups, _ = lax.optimization_barrier((moe_groups, attn_pair))
-    moe_own, to_after, _, to_before = by_distance(moe_groups, y)
-    moe_pair = with_partner(
-        moe_own,
-        jnp.concatenate([hop(to_after[:128], dy=1), hop(to_before[128:], dy=-1)], axis=0),
-        y_low,
-    )
-    moe_pair, _ = lax.optimization_barrier((moe_pair, attn_all))
-    moe_all = in_order(ring_gather(moe_pair, "x"), x).reshape(width, -1)
-    w_in = moe_all[:, : 2 * span + 128]
-    w_down_t = moe_all[:, 2 * span + 128 :]
-
+        axis=0,
+    )
     own_grad = out_grad.reshape(rows, width)
     route_rows = routes.reshape(rows, -1)
     own_picked = jnp.any(
         route_rows[:, :, None] == jnp.arange(128, dtype=jnp.int32)[None, None, :], axis=1
     ).astype(BF)
-
-    def lane_rows(whole):
-        half = lax.dynamic_slice_in_dim(whole, core * (rows // 2), rows // 2, 0)
-        twice = jnp.concatenate([half, half], axis=0)
-        return lax.dynamic_slice_in_dim(twice, z * home, rows // 2, 0)
-
-    grad_half, _ = lax.optimization_barrier((lane_rows(own_grad), attn_pair))
-    grad_lane = jnp.concatenate(ring_gather(grad_half, "y"), axis=0)
-    grad_all = jnp.concatenate([grad_lane, hop(grad_lane, dc=1)], axis=0)
-    picked_lane = jnp.concatenate(direct_gather(lane_rows(own_picked), "y"), axis=0)
-    picked = jnp.concatenate([picked_lane, hop(picked_lane, dc=1)], axis=0)[:, :experts] > 0
-
+    (
+        weights, experts_in, experts_out, grad_all, picked_all, moe_in_all,
+        normed, pre, rot, key_value, mixed_low, lse, hidden, home_scale_one,
+    ) = run_front(
+        tokens.reshape(rows, width), own_weights, turn_tables(), segments,
+        gate_weight, up_weight, down_weight, own_grad, own_picked,
+    )
+    weights = weights.reshape(8, WROWS, WCOLS)
+    w_stacked = weights[:, :256, :768].reshape(width, -1)
+    w_router = weights[:, :256, 768:896].reshape(width, -1)
+    w_out_t = weights[:, :256, 896:].transpose(0, 2, 1).reshape(width, -1)
+    gain_rows = weights[:, 256:].astype(F32)
+    attn_gains = gain_rows[:, 0, :256].reshape(-1)
+    moe_gains = gain_rows[:, 1, :256].reshape(-1)
+    head_gains = jnp.sum(gain_rows[:, 2:6, :128], axis=0)
+
+    def wide(part):
+        return part.transpose(1, 2, 3, 0, 4).reshape(width, -1)
+
+    w_in = jnp.concatenate(
+        [wide(experts_in[..., :128]), wide(experts_in[..., 128:]), w_router], axis=1
+    )
+    w_down_t = experts_out.reshape(-1, width).T
+    grad_all = grad_all.reshape(4 * rows, width)
+    picked = picked_all.reshape(4 * rows, -1)[:, :experts] > 0
+    moe_in = moe_in_all.reshape(4 * rows, width)
     inputs = tokens.reshape(rows, width).astype(F32)
-    scale_one = rms_scale(inputs)
-    normed = (inputs * scale_one * attn_gains).astype(BF)
-    projected = dot(normed, w_stacked)
-    query_pre = [projected[:, h * 128 : h * 128 + 128] for h in range(2)]
-    key_pre = [projected[:, 256 + h * 128 : 384 + h * 128] for h in range(2)]
-    value_low = projected[:, 512:].astype(BF)
     first_row = ctx * rows
     places = first_row + jnp.arange(rows, dtype=jnp.int32)
     cosine, sine_table = rope_tables(places, head_dim)
+    query_pre = [pre[:, h * 128 : h * 128 + 128] for h in range(2)]
+    key_pre = [pre[:, 256 + h * 128 : 384 + h * 128] for h in range(2)]
     scale_query = [rms_scale(v) for v in query_pre]
     scale_key = [rms_scale(v) for v in key_pre]
-    gain_q = [query_gains[:, h * 128 : h * 128 + 128] for h in range(2)]
-    gain_k = [key_gains[:, h * 128 : h * 128 + 128] for h in range(2)]
-    query_low = [
-        rotate(query_pre[h] * scale_query[h] * gain_q[h], cosine, sine_table).astype(BF)
-        for h in range(2)
-    ]
-    key_low = [
-        rotate(key_pre[h] * scale_key[h] * gain_k[h], cosine, sine_table).astype(BF)
-        for h in range(2)
-    ]
-    keys_values = jnp.concatenate(key_low + [value_low], axis=1)
-    earlier = hop(keys_values, dy=2, only=lambda x, y, z, c: y < 2)
-    both = jnp.concatenate([earlier, keys_values], axis=0)
+    gain_q = [head_gains[h][None] for h in range(2)]
+    gain_k = [head_gains[2 + h][None] for h in range(2)]
+    query_low = [rot[:, h * 128 : h * 128 + 128] for h in range(2)]
+    earlier = hop(key_value, dy=2, only=lambda x, y, z, c: y < 2)
+    both = jnp.concatenate([earlier, key_value], axis=0)
     keys = [both[:, h * 128 : h * 128 + 128] for h in range(2)]
     values = [both[:, 256 + h * 128 : 384 + h * 128] for h in range(2)]
     key_places = first_row - rows + jnp.arange(2 * rows, dtype=jnp.int32)
@@ -301,22 +691,15 @@
         & (key_places[None, :] >= 0)
         & (own_segments[:, None] == key_segments[None, :])
     )
-    probs, mixed = [], []
+    probs = []
     for h in range(2):
         scores = jnp.where(allowed, dot_nt(query_low[h], keys[h]) * score_scale, MASKED_SCORE)
-        exponents = jnp.exp(scores - jnp.max(scores, axis=-1, keepdims=True))
-        probs.append(exponents / jnp.sum(exponents, axis=-1, keepdims=True))
-        mixed.append(dot(probs[h].astype(BF), values[h]))
-    mixed_low = jnp.concatenate(mixed, axis=1).astype(BF)
-    attn_part = dot_nt(mixed_low, w_out_t).astype(BF)
-
+        probs.append(jnp.exp(scores - lse[h][:, :1]))
     home_row = (core * 4 + z) * home
     home_inputs = lax.dynamic_slice_in_dim(tokens.reshape(rows, width), home_row, home, 0).astype(F32)
-    home_scale_one = lax.dynamic_slice_in_dim(scale_one, home_row, home, 0)
+    home_scale_one = home_scale_one[:, :1]
     home_grad = lax.dynamic_slice_in_dim(own_grad, home_row, home, 0).astype(F32)
-    hidden = home_inputs + home_sum(attn_part)
     scale_two = rms_scale(hidden)
-    moe_in = gather_tokens((hidden * scale_two * moe_gains).astype(BF))
 
     joined = dot(moe_in, w_in)
     logits = jnp.where(picked, joined[:, 2 * span : 2 * span + experts], -jnp.inf)

time: 742 us -> 612 us (0.82)
  waiting for transfers between devices: 291 us -> 140 us
  Pallas kernels: 0 us -> 130 us
  starting transfers between devices: 137 us -> 86.4 us
  local copies, waits for them, and re-layouts: 119 us -> 80.4 us
  other arithmetic: 90.4 us -> 70.4 us
    ppermute x101 -> x68, waiting for transfers between devices: 291 us -> 140 us  [hop(): return lax.ppermute(value, AXES, pairs)]
    pallas_call x0 -> x1, Pallas kernels: none -> 130 us  [run_front(): pl.pallas_call(front, out_shape=[o for o, _ in outs], in_specs=[VMEM] * 6...]
    ppermute x101 -> x68, starting transfers between devices: 137 us -> 86.4 us  [hop(): return lax.ppermute(value, AXES, pairs)]
    concatenate x7 -> x2, local copies, waits for them, and re-layouts: 17.1 us -> 0.05 us  [the longest x1 0.04 us: body(): both = jnp.concatenate([earlier, key_value], axis=0)]
    unnamed x222 -> x107, local copies, waits for them, and re-layouts: 35.4 us -> 20.1 us
    dynamic_update_slice x17 -> x12, local copies, waits for them, and re-layouts: 16.9 us -> 7.45 us  [in_order(): lax.dynamic_update_index_in_dim(whole, block, (start + distance) % 4, 0)]
    another operation x10 -> x2, other arithmetic: 8.83 us -> 0.14 us
    transpose x0 -> x3, local copies, waits for them, and re-layouts: none -> 8.6 us  [wide(): return part.transpose(1, 2, 3, 0, 4).reshape(width, -1)]
  transfers between devices with their start and end apart: 101 -> 68, of which waited for: 51 -> 25; matrix products, arithmetic and copies ran while one was open for 26% -> 23% of each run, Pallas kernels for 0% -> 0%
where the time goes in v2:
time: 612 us; the launch traced here: 600 us
  waiting for transfers between devices  140 us (23%)
  Pallas kernels  130 us (21%)
  matrix products  90.7 us (15%)
  starting transfers between devices  86.4 us (14%)
  local copies, waits for them, and re-layouts  80.4 us (13%)
  other arithmetic  70.4 us (12%)
    ppermute x68, waiting for transfers between devices, hop(): return lax.ppermute(value, AXES, pairs)  140 us
    pallas_call x1, Pallas kernels, run_front(): pl.pallas_call(front, out_shape=[o for o, _ in outs], in_specs=[VMEM] * 6...  130 us
    ppermute x68, starting transfers between devices, hop(): return lax.ppermute(value, AXES, pairs)  86.4 us
    dot_general x8, matrix products, dot_tn(): lax.dot_general(left, right, (((0,), (0,)), ((), ())), preferred_element_...  32.6 us
    dot_general x5, matrix products, dot(): return jnp.dot(left, right, preferred_element_type=F32)  31.3 us
    dot_general x7, matrix products, dot_nt(): lax.dot_general(left, right, (((1,), (1,)), ((), ())), preferred_element_...  26.7 us
    unnamed x107, local copies, waits for them, and re-layouts  20.1 us
  transfers between devices with their start and end apart: 68, of which 25 were waited for; matrix products, arithmetic and copies ran while one was open for 23% of the time, Pallas kernels for 0%

profile of v2, /device:TPU:14, one launch (start us, length us, event | category | flops | bytes accessed | tf_op | source)
XLA Modules:
  0.0 600.3 jit_solution(13760979070573569761)
XLA Ops:
  6.4 2.9 fusion.12
  13.4 130.0 %front.1 = (bf16[4,2,272,1152]{3,2,1,0:T(8,128)(2,1)}, bf16[4,4,2,256,256]{4,3,2,1,0:T(8,128)(2,1)}, bf16[4,128,2048]{2,1,0:T(8,128)(2,1)}, bf16[4,512,2048]{2,1...) custom-call(bf16[512,2048]{1,0:T(8,128)(2,1)} %bitcast.327, ...), custom_call_target="tpu_custom_call" | custom-call | tf_op jit(solution)/shard_map/front/pallas_call | solution.py:530
  143.4 2.7 slice_bitcast_fusion.1
  146.1 2.9 copy.81
  149.0 2.9 copy.82
  153.3 4.3 copy_bitcast_fusion
  157.5 13.8 %fusion.13 = f32[2048,1152]{0,1:T(8,128)S(1)} fusion(bf16[2048,2048]{1,0:T(8,128)(2,1)} %bitcast.358, bf16[2048,128]{1,0:T(8,128)(2,1)S(1)} %bitcast.334, bf16[2048,512]{1,0:T(8,128)(2,1)S(1)} %get-tuple-element.262, bf16[2048,512]{1,0:T(8,128)(2,1)} %get-tuple-element.263), kind=kOutput, calls=%fused_computation.62 | convolution fusion | flops 9677832192 | bytes 22544384 | tf_op jit(solution)/shard_map/dot_general | solution.py:145
  171.4 3.5 copy-done.7
  175.0 13.6 %bitcast_reduce_fusion = (f32[2048,4]{0,1:T(4,128)S(1)}, f32[2048,512]{0,1:T(8,128)}) fusion(f32[2048,1152]{0,1:T(8,128)} %copy-done.7, bf16[2048,2048]{1,0:T(8,128)(2,1)} %bitcast.360, bf16[512,2048]{1,0:T(8,128)(2,1)} %bitcast.362), kind=kOutput, calls=%fused_computation.20 | convolution fusion | flops 4304396288 | bytes 23101440 | tf_op jit(solution)/shard_map/dot_general | solution.py:145
  189.6 7.7 %multiply_convert_fusion.1 = (bf16[2048,512]{0,1:T(8,128)(2,1)}, bf16[2048,512]{0,1:T(8,128)(2,1)}, bf16[2048,512]{0,1:T(8,128)(2,1)}) fusion(f32[2048,512]{0,1:T(8,128)} %get-tuple-element.257, f32[2048,1152]{0,1:T(8,128)} %copy-done.7, f32[2048,4]{0,1:T(4,128)S(1)} %constant_dynamic-slice_fusion.7), kind=kLoop, calls=%fused_computation.23 | loop fusion | flops 17825792 | bytes 18907136 | tf_op jit(solution)/shard_map/convert_element_type | solution.py:725
  197.3 14.4 %convolution_convert_fusion.1 = bf16[2048,2048]{1,0:T(8,128)(2,1)S(1)} fusion(bf16[2048,128]{1,0:T(8,128)(2,1)S(1)} %bitcast.335, bf16[2048,512]{1,0:T(8,128)(2,1)} %copy-done.23, bf16[2048,512]{1,0:T(8,128)(2,1)} %get-tuple-element.263, bf16[2048,16]{0,1:T(8,128)(2,1)S(1)} %multiply_convert_fusion.8, bf16[2048,512]{0,1:T(8,128)(2,1)} %get-tuple-element.171, ...), kind=kOutput, calls=%fused_computation.5 | convolution fusion | flops 9700900864 | bytes 17367040 | tf_op jit(solution)/shard_map/dot_general | solution.py:149
  211.7 2.4 constant_dynamic-slice_fusion.6
  214.1 2.1 copy-done.6
  216.7 4.7 collective-permute-start.20
  225.6 10.0 %convolution_convert_fusion.4 = bf16[2048,512]{1,0:T(8,128)(2,1)} fusion(bf16[2048,2048]{1,0:T(8,128)(2,1)} %bitcast.361, bf16[2048,512]{0,1:T(8,128)(2,1)} %get-tuple-element.172), kind=kOutput, calls=%fused_computation.32 | convolution fusion | flops 4296015872 | bytes 12582912 | tf_op jit(solution)/shard_map/dot_general | solution.py:153
  235.6 15.4 %convolution_convert_fusion = bf16[2048,1152]{1,0:T(8,128)(2,1)} fusion(bf16[2048,2048]{1,0:T(8,128)(2,1)} %bitcast.359, bf16[2048,16]{0,1:T(8,128)(2,1)S(1)} %multiply_convert_fusion.8, bf16[2048,512]{0,1:T(8,128)(2,1)S(1)} %copy-done.21, bf16[2048,512]{0,1:T(8,128)(2,1)S(1)} %copy-done.20), kind=kOutput, calls=%fused_computation.4 | convolution fusion | flops 9684910080 | bytes 17367040 | tf_op jit(solution)/shard_map/dot_general | solution.py:153
  251.0 4.1 add_convert_fusion.1
  255.5 2.0 collective-permute-start.3
  258.0 11.1 %collective-permute-done.1 = bf16[128,2048]{1,0:T(8,128)(2,1)S(1)} collective-permute-done((bf16[128,2048]{1,0:T(8,128)(2,1)S(1)}, bf16[128,2048]{1,0:T(8,128)(2,1)S(1)}, u32[]{:S(2)}, u32[]{:S(2)}) %collective-permute-start.1) | collective-permute-done | bytes 524320 | tf_op jit(solution)/shard_map/ppermute | solution.py:34
  272.1 7.2 %convolution_convert_fusion.2 = bf16[2048,2048]{1,0:T(8,128)(2,1)} fusion(bf16[2048,512]{0,1:T(8,128)(2,1)S(1)} %copy-done.19, bf16[512,2048]{1,0:T(8,128)(2,1)S(1)} %bitcast.363), kind=kOutput, calls=%fused_computation.6 | convolution fusion | flops 4299161600 | bytes 12582912 | tf_op jit(solution)/shard_map/dot_general | solution.py:149
  279.3 14.7 %collective-permute-done.2 = bf16[256,2048]{1,0:T(8,128)(2,1)S(1)} collective-permute-done((bf16[256,2048]{1,0:T(8,128)(2,1)S(1)}, bf16[256,2048]{1,0:T(8,128)(2,1)S(1)}, u32[]{:S(2)}, u32[]{:S(2)}) %collective-permute-start.2) | collective-permute-done | bytes 1048608 | tf_op jit(solution)/shard_map/ppermute | solution.py:34
  298.2 2.6 collective-permute-start.6
  302.0 2.3 slice.534
  304.3 3.8 slice.555
  308.1 2.3 copy.101
  318.4 2.6 collective-permute-start.22
  321.0 2.1 convert_bitcast_fusion
  330.0 2.4 fusion.40
  332.3 4.8 constant_dynamic-slice_fusion.5
  340.1 3.8 collective-permute-start.43
  346.8 4.2 collective-permute-done.43
  354.1 2.5 collective-permute-start.47
  358.3 2.5 collective-permute-done.46
  366.9 3.5 collective-permute-done.48
  370.4 10.8 %collective-permute-done.49 = f32[272,128]{1,0:T(8,128)S(1)} collective-permute-done((f32[272,128]{1,0:T(8,128)S(1)}, f32[272,128]{1,0:T(8,128)S(1)}, u32[]{:S(2)}, u32[]{:S(2)}) %collective-permute-start.49) | collective-permute-done | bytes 139296 | tf_op jit(solution)/shard_map/ppermute | solution.py:34
  381.1 2.9 collective-permute-done.50
  390.7 3.1 convolution_convert_fusion.7
  402.3 3.4 convolution_convert_fusion.6
  405.8 9.7 %collective-permute-done.25 = bf16[512,512]{1,0:T(8,128)(2,1)S(1)} collective-permute-done((bf16[512,512]{1,0:T(8,128)(2,1)S(1)}, bf16[512,512]{1,0:T(8,128)(2,1)S(1)}, u32[]{:S(2)}, u32[]{:S(2)}) %collective-permute-start.25) | collective-permute-done | bytes 524320 | tf_op jit(solution)/shard_map/ppermute | solution.py:34
  431.6 8.7 %collective-permute-done.34 = bf16[256,1024]{1,0:T(8,128)(2,1)S(1)} collective-permute-done((bf16[256,1024]{1,0:T(8,128)(2,1)S(1)}, bf16[256,1024]{1,0:T(8,128)(2,1)S(1)}, u32[]{:S(2)}, u32[]{:S(2)}) %collective-permute-start.34) | collective-permute-done | bytes 524320 | tf_op jit(solution)/shard_map/ppermute | solution.py:34
  440.4 2.9 collective-permute-done.36
  444.0 2.0 collective-permute-start.27
  446.1 2.7 collective-permute-start.28
  451.3 2.7 collective-permute-done.27
  454.0 4.0 collective-permute-done.28
  459.6 16.1 %collective-permute-done.66 = bf16[256,1536]{1,0:T(8,128)(2,1)S(1)} collective-permute-done((bf16[256,1536]{1,0:T(8,128)(2,1)S(1)}, bf16[256,1536]{1,0:T(8,128)(2,1)S(1)}, u32[]{:S(2)}, u32[]{:S(2)}) %collective-permute-start.66) | collective-permute-done | bytes 786464 | tf_op jit(solution)/shard_map/ppermute | solution.py:34
  478.2 2.2 bitcast_dynamic-update-slice_fusion.6
  482.0 2.4 collective-permute-start.54
  484.4 4.1 add_convert_fusion
  491.0 11.0 %collective-permute-start.11 = (bf16[128,2048]{1,0:T(8,128)(2,1)}, bf16[128,2048]{1,0:T(8,128)(2,1)}, u32[]{:S(2)}, u32[]{:S(2)}) collective-permute-start(bf16[128,2048]{1,0:T(8,128)(2,1)} %get-tuple-element.184), channel_id=1, source_target_pairs={{0,24},{1,25},{2,26},{3,27},{4,28},{5,29},{6,30},{7,31},{8,16},{9,... | collective-permute-start | bytes 1572872 | tf_op jit(solution)/shard_map/ppermute | solution.py:34
  504.0 2.2 collective-permute-start.56
  510.0 2.9 copy.92
  519.9 10.6 %collective-permute-done.58 = f32[48,128]{1,0:T(8,128)S(1)} collective-permute-done((f32[48,128]{1,0:T(8,128)S(1)}, f32[48,128]{1,0:T(8,128)S(1)}, u32[]{:S(2)}, u32[]{:S(2)}) %collective-permute-start.58) | collective-permute-done | bytes 24608 | tf_op jit(solution)/shard_map/ppermute | solution.py:34
  532.4 2.4 collective-permute-start.12
  534.8 2.4 collective-permute-start.31
  538.0 12.3 %collective-permute-done.10 = bf16[256,2048]{1,0:T(8,128)(2,1)S(1)} collective-permute-done((bf16[256,2048]{1,0:T(8,128)(2,1)S(1)}, bf16[256,2048]{1,0:T(8,128)(2,1)S(1)}, u32[]{:S(2)}, u32[]{:S(2)}) %collective-permute-start.10) | collective-permute-done | bytes 1048608 | tf_op jit(solution)/shard_map/ppermute | solution.py:34
  554.6 2.1 collective-permute-start.15
  556.8 5.8 collective-permute-done.13
  562.6 3.0 collective-permute-start.39
  569.6 2.9 collective-permute-start.40
  574.6 8.6 %collective-permute-done.17 = bf16[64,2048]{1,0:T(8,128)(2,1)S(1)} collective-permute-done((bf16[64,2048]{1,0:T(8,128)(2,1)S(1)}, bf16[64,2048]{1,0:T(8,128)(2,1)S(1)}, u32[]{:S(2)}, u32[]{:S(2)}) %collective-permute-start.17) | collective-permute-done | bytes 262176 | tf_op jit(solution)/shard_map/ppermute | solution.py:34
  584.0 3.8 collective-permute-done.18
  591.7 3.8 maximum_select_fusion.2
  595.5 4.6 maximum_select_fusion
  (372 shorter events, 130.0 us)
Async XLA Ops:
  216.3 34.8 %collective-permute-start = (bf16[4,256,2048]{2,1,0:T(8,128)(2,1)}, bf16[4,256,2048]{2,1,0:T(8,128)(2,1)}, u32[]{:S(2)}, u32[]{:S(2)}) collective-permute-start(bf16[4,256,2048]{2,1,0:T(8,128)(2,1)} %constant_dynamic-slice_fusion.6), channel_id=1, source_target_pairs={{0,1},{1,0},{2,3},{3,2},{4,5},{5,4},{6,7},{7,6},{8,9},{9,8},{10,11... | collective-permute-start | bytes 12582920 | tf_op jit(solution)/shard_map/ppermute | solution.py:34
  216.7 93.6 %collective-permute-start.20 = (bf16[512,512]{1,0:T(8,128)(2,1)S(1)}, bf16[512,512]{1,0:T(8,128)(2,1)}, u32[]{:S(2)}, u32[]{:S(2)}) collective-permute-start(bf16[512,512]{1,0:T(8,128)(2,1)S(1)} %copy-done.28), channel_id=1, source_target_pairs={{0,8},{1,9},{2,10},{3,11},{4,12},{5,13},{6,14},{7,15},{16,24},{17,... | collective-permute-start | bytes 1572872 | tf_op jit(solution)/shard_map/ppermute | solution.py:34
  255.4 13.8 %collective-permute-start.1 = (bf16[128,2048]{1,0:T(8,128)(2,1)S(1)}, bf16[128,2048]{1,0:T(8,128)(2,1)S(1)}, u32[]{:S(2)}, u32[]{:S(2)}) collective-permute-start(bf16[128,2048]{1,0:T(8,128)(2,1)S(1)} %get-tuple-element.188), channel_id=1, source_target_pairs={{0,16},{1,17},{2,18},{3,19},{4,20},{5,21},{6,22},{7,23},{8,24},{9,... | collective-permute-start | bytes 1572872 | tf_op jit(solution)/shard_map/ppermute | solution.py:34
  255.5 13.8 %collective-permute-start.3 = (bf16[128,2048]{1,0:T(8,128)(2,1)S(1)}, bf16[128,2048]{1,0:T(8,128)(2,1)S(1)}, u32[]{:S(2)}, u32[]{:S(2)}) collective-permute-start(bf16[128,2048]{1,0:T(8,128)(2,1)S(1)} %get-tuple-element.190), channel_id=1, source_target_pairs={{0,24},{1,25},{2,26},{3,27},{4,28},{5,29},{6,30},{7,31},{8,16},{9,... | collective-permute-start | bytes 1572872 | tf_op jit(solution)/shard_map/ppermute | solution.py:34
  269.8 24.2 %collective-permute-start.2 = (bf16[256,2048]{1,0:T(8,128)(2,1)S(1)}, bf16[256,2048]{1,0:T(8,128)(2,1)S(1)}, u32[]{:S(2)}, u32[]{:S(2)}) collective-permute-start(bf16[256,2048]{1,0:T(8,128)(2,1)S(1)} %pad_maximum_fusion.5), channel_id=1, source_target_pairs={{0,16},{1,17},{2,18},{3,19},{4,20},{5,21},{6,22},{7,23},{8,24},{9,... | collective-permute-start | bytes 3145736 | tf_op jit(solution)/shard_map/ppermute | solution.py:34
  270.8 24.8 %collective-permute-start.4 = (bf16[256,2048]{1,0:T(8,128)(2,1)S(1)}, bf16[256,2048]{1,0:T(8,128)(2,1)S(1)}, u32[]{:S(2)}, u32[]{:S(2)}) collective-permute-start(bf16[256,2048]{1,0:T(8,128)(2,1)S(1)} %pad_maximum_fusion.6), channel_id=1, source_target_pairs={{0,24},{1,25},{2,26},{3,27},{4,28},{5,29},{6,30},{7,31},{8,16},{9,... | collective-permute-start | bytes 3145736 | tf_op jit(solution)/shard_map/ppermute | solution.py:34
  297.1 14.5 %collective-permute-start.5 = (bf16[64,2048]{1,0:T(8,128)(2,1)}, bf16[64,2048]{1,0:T(8,128)(2,1)S(1)}, u32[]{:S(2)}, u32[]{:S(2)}) collective-permute-start(bf16[64,2048]{1,0:T(8,128)(2,1)} %get-tuple-element.227), channel_id=1, source_target_pairs={{0,2},{1,3},{2,4},{3,5},{4,6},{5,7},{6,0},{7,1},{8,10},{9,11},{10,... | collective-permute-start | bytes 786440 | tf_op jit(solution)/shard_map/ppermute | solution.py:34
  298.2 13.4 %collective-permute-start.6 = (bf16[64,2048]{1,0:T(8,128)(2,1)}, bf16[64,2048]{1,0:T(8,128)(2,1)}, u32[]{:S(2)}, u32[]{:S(2)}) collective-permute-start(bf16[64,2048]{1,0:T(8,128)(2,1)} %get-tuple-element.229), channel_id=1, source_target_pairs={{0,4},{1,5},{2,6},{3,7},{4,0},{5,1},{6,2},{7,3},{8,12},{9,13},{10,... | collective-permute-start | bytes 786440 | tf_op jit(solution)/shard_map/ppermute | solution.py:34
  300.8 10.8 %collective-permute-start.7 = (bf16[64,2048]{1,0:T(8,128)(2,1)}, bf16[64,2048]{1,0:T(8,128)(2,1)}, u32[]{:S(2)}, u32[]{:S(2)}) collective-permute-start(bf16[64,2048]{1,0:T(8,128)(2,1)} %get-tuple-element.228), channel_id=1, source_target_pairs={{0,6},{1,7},{2,0},{3,1},{4,2},{5,3},{6,4},{7,5},{8,14},{9,15},{10,... | collective-permute-start | bytes 786440 | tf_op jit(solution)/shard_map/ppermute | solution.py:34
  317.6 26.3 %collective-permute-start.21 = (bf16[64,2048]{1,0:T(8,128)(2,1)}, bf16[64,2048]{1,0:T(8,128)(2,1)}, u32[]{:S(2)}, u32[]{:S(2)}) collective-permute-start(bf16[64,2048]{1,0:T(8,128)(2,1)} %get-tuple-element.164), channel_id=1, source_target_pairs={{0,6},{1,7},{2,0},{3,1},{4,2},{5,3},{6,4},{7,5},{8,14},{9,15},{10,... | collective-permute-start | bytes 786440 | tf_op jit(solution)/shard_map/ppermute | solution.py:34
  318.4 35.7 %collective-permute-start.22 = (bf16[64,2048]{1,0:T(8,128)(2,1)}, bf16[64,2048]{1,0:T(8,128)(2,1)}, u32[]{:S(2)}, u32[]{:S(2)}) collective-permute-start(bf16[64,2048]{1,0:T(8,128)(2,1)} %get-tuple-element.164), channel_id=1, source_target_pairs={{0,4},{1,5},{2,6},{3,7},{4,0},{5,1},{6,2},{7,3},{8,12},{9,13},{10,... | collective-permute-start | bytes 786440 | tf_op jit(solution)/shard_map/ppermute | solution.py:34
  321.0 42.8 %collective-permute-start.23 = (bf16[64,2048]{1,0:T(8,128)(2,1)}, bf16[64,2048]{1,0:T(8,128)(2,1)}, u32[]{:S(2)}, u32[]{:S(2)}) collective-permute-start(bf16[64,2048]{1,0:T(8,128)(2,1)} %get-tuple-element.164), channel_id=1, source_target_pairs={{0,2},{1,3},{2,4},{3,5},{4,6},{5,7},{6,0},{7,1},{8,10},{9,11},{10,... | collective-permute-start | bytes 786440 | tf_op jit(solution)/shard_map/ppermute | solution.py:34
  329.9 9.2 %collective-permute-start.41 = (f32[272,128]{1,0:T(8,128)S(1)}, f32[272,128]{1,0:T(8,128)S(1)}, u32[]{:S(2)}, u32[]{:S(2)}) collective-permute-start(f32[272,128]{1,0:T(8,128)S(1)} %reshape.544), channel_id=1, source_target_pairs={{0,1},{1,0},{2,3},{3,2},{4,5},{5,4},{6,7},{7,6},{8,9},{9,8},{10,11... | collective-permute-start | bytes 417800 | tf_op jit(solution)/shard_map/ppermute | solution.py:34
  339.1 7.6 %collective-permute-start.42 = (f32[272,128]{1,0:T(8,128)S(1)}, f32[272,128]{1,0:T(8,128)S(1)}, u32[]{:S(2)}, u32[]{:S(2)}) collective-permute-start(f32[272,128]{1,0:T(8,128)S(1)} %add.621), channel_id=1, source_target_pairs={{0,2},{1,3},{2,4},{3,5},{4,6},{5,7},{6,0},{7,1},{8,10},{9,11},{10,... | collective-permute-start | bytes 417800 | tf_op jit(solution)/shard_map/ppermute | solution.py:34
  340.1 10.8 %collective-permute-start.43 = (f32[272,128]{1,0:T(8,128)S(1)}, f32[272,128]{1,0:T(8,128)S(1)}, u32[]{:S(2)}, u32[]{:S(2)}) collective-permute-start(f32[272,128]{1,0:T(8,128)S(1)} %add.621), channel_id=1, source_target_pairs={{0,4},{1,5},{2,6},{3,7},{4,0},{5,1},{6,2},{7,3},{8,12},{9,13},{10,... | collective-permute-start | bytes 417800 | tf_op jit(solution)/shard_map/ppermute | solution.py:34
  346.8 38.6 %collective-permute-start.61 = (bf16[256,1536]{1,0:T(8,128)(2,1)}, bf16[256,1536]{1,0:T(8,128)(2,1)}, u32[]{:S(2)}, u32[]{:S(2)}) collective-permute-start(bf16[256,1536]{1,0:T(8,128)(2,1)} %get-tuple-element.209), channel_id=1, source_target_pairs={{0,32},{1,33},{2,34},{3,35},{4,36},{5,37},{6,38},{7,39},{8,40},{9,... | collective-permute-start | bytes 2359304 | tf_op jit(solution)/shard_map/ppermute | solution.py:34
  351.0 7.4 %collective-permute-start.45 = (f32[272,128]{1,0:T(8,128)S(1)}, f32[272,128]{1,0:T(8,128)S(1)}, u32[]{:S(2)}, u32[]{:S(2)}) collective-permute-start(f32[272,128]{1,0:T(8,128)S(1)} %add_add_fusion.2), channel_id=1, source_target_pairs={{0,16},{1,17},{2,18},{3,19},{4,20},{5,21},{6,22},{7,23},{8,24},{9,... | collective-permute-start | bytes 417800 | tf_op jit(solution)/shard_map/ppermute | solution.py:34
  352.8 8.1 %collective-permute-start.46 = (f32[272,128]{1,0:T(8,128)S(1)}, f32[272,128]{1,0:T(8,128)S(1)}, u32[]{:S(2)}, u32[]{:S(2)}) collective-permute-start(f32[272,128]{1,0:T(8,128)S(1)} %add_add_fusion.2), channel_id=1, source_target_pairs={{0,8},{1,9},{2,10},{3,11},{4,12},{5,13},{6,14},{7,15},{8,0},{9,1},... | collective-permute-start | bytes 417800 | tf_op jit(solution)/shard_map/ppermute | solution.py:34
  354.1 8.0 %collective-permute-start.47 = (f32[272,128]{1,0:T(8,128)S(1)}, f32[272,128]{1,0:T(8,128)S(1)}, u32[]{:S(2)}, u32[]{:S(2)}) collective-permute-start(f32[272,128]{1,0:T(8,128)S(1)} %add_add_fusion.2), channel_id=1, source_target_pairs={{0,24},{1,25},{2,26},{3,27},{4,28},{5,29},{6,30},{7,31},{8,16},{9,... | collective-permute-start | bytes 417800 | tf_op jit(solution)/shard_map/ppermute | solution.py:34
  358.3 28.8 %collective-permute-start.63 = (bf16[256,1536]{1,0:T(8,128)(2,1)}, bf16[256,1536]{1,0:T(8,128)(2,1)}, u32[]{:S(2)}, u32[]{:S(2)}) collective-permute-start(bf16[256,1536]{1,0:T(8,128)(2,1)} %get-tuple-element.210), channel_id=1, source_target_pairs={{0,96},{1,97},{2,98},{3,99},{4,100},{5,101},{6,102},{7,103},{8,104... | collective-permute-start | bytes 2359304 | tf_op jit(solution)/shard_map/ppermute | solution.py:34
  362.2 8.2 %collective-permute-start.48 = (f32[272,128]{1,0:T(8,128)S(1)}, f32[272,128]{1,0:T(8,128)S(1)}, u32[]{:S(2)}, u32[]{:S(2)}) collective-permute-start(f32[272,128]{1,0:T(8,128)S(1)} %add_add_fusion.1), channel_id=1, source_target_pairs={{0,32},{1,33},{2,34},{3,35},{4,36},{5,37},{6,38},{7,39},{8,40},{9,... | collective-permute-start | bytes 417800 | tf_op jit(solution)/shard_map/ppermute | solution.py:34
  362.2 18.9 %collective-permute-start.49 = (f32[272,128]{1,0:T(8,128)S(1)}, f32[272,128]{1,0:T(8,128)S(1)}, u32[]{:S(2)}, u32[]{:S(2)}) collective-permute-start(f32[272,128]{1,0:T(8,128)S(1)} %add_add_fusion.1), channel_id=1, source_target_pairs={{0,64},{1,65},{2,66},{3,67},{4,68},{5,69},{6,70},{7,71},{8,72},{9,... | collective-permute-start | bytes 417800 | tf_op jit(solution)/shard_map/ppermute | solution.py:34
  363.8 20.2 %collective-permute-start.50 = (f32[272,128]{1,0:T(8,128)S(1)}, f32[272,128]{1,0:T(8,128)S(1)}, u32[]{:S(2)}, u32[]{:S(2)}) collective-permute-start(f32[272,128]{1,0:T(8,128)S(1)} %add_add_fusion.1), channel_id=1, source_target_pairs={{0,96},{1,97},{2,98},{3,99},{4,100},{5,101},{6,102},{7,103},{8,104... | collective-permute-start | bytes 417800 | tf_op jit(solution)/shard_map/ppermute | solution.py:34
  370.4 114.0 %collective-permute-start.8 = (bf16[4,256,2048]{2,1,0:T(8,128)(2,1)}, bf16[4,256,2048]{2,1,0:T(8,128)(2,1)}, u32[]{:S(2)}, u32[]{:S(2)}) collective-permute-start(bf16[4,256,2048]{2,1,0:T(8,128)(2,1)} %constant_dynamic-slice_fusion.5), channel_id=1, source_target_pairs={{0,1},{1,0},{2,3},{3,2},{4,5},{5,4},{6,7},{7,6},{8,9},{9,8},{10,11... | collective-permute-start | bytes 12582920 | tf_op jit(solution)/shard_map/ppermute | solution.py:34
  381.1 9.5 %collective-permute-start.24 = (bf16[256,2048]{1,0:T(8,128)(2,1)}, bf16[256,2048]{1,0:T(8,128)(2,1)}, u32[]{:S(2)}, u32[]{:S(2)}) collective-permute-start(bf16[256,2048]{1,0:T(8,128)(2,1)} %bitcast.56), channel_id=1, source_target_pairs={{0,1},{1,0},{2,3},{3,2},{4,5},{5,4},{6,7},{7,6},{8,9},{9,8},{10,11... | collective-permute-start | bytes 3145736 | tf_op jit(solution)/shard_map/ppermute | solution.py:34
  387.0 42.4 %collective-permute-start.62 = (bf16[512,1536]{1,0:T(8,128)(2,1)S(1)}, bf16[512,1536]{1,0:T(8,128)(2,1)S(1)}, u32[]{:S(2)}, u32[]{:S(2)}) collective-permute-start(bf16[512,1536]{1,0:T(8,128)(2,1)S(1)} %fusion.15), channel_id=1, source_target_pairs={{0,32},{1,33},{2,34},{3,35},{4,36},{5,37},{6,38},{7,39},{8,40},{9,... | collective-permute-start | bytes 4718600 | tf_op jit(solution)/shard_map/ppermute | solution.py:34
  389.4 40.2 %collective-permute-start.64 = (bf16[512,1536]{1,0:T(8,128)(2,1)S(1)}, bf16[512,1536]{1,0:T(8,128)(2,1)S(1)}, u32[]{:S(2)}, u32[]{:S(2)}) collective-permute-start(bf16[512,1536]{1,0:T(8,128)(2,1)S(1)} %pad_maximum_fusion.4), channel_id=1, source_target_pairs={{0,96},{1,97},{2,98},{3,99},{4,100},{5,101},{6,102},{7,103},{8,104... | collective-permute-start | bytes 4718600 | tf_op jit(solution)/shard_map/ppermute | solution.py:34
  400.3 15.1 %collective-permute-start.25 = (bf16[512,512]{1,0:T(8,128)(2,1)S(1)}, bf16[512,512]{1,0:T(8,128)(2,1)S(1)}, u32[]{:S(2)}, u32[]{:S(2)}) collective-permute-start(bf16[512,512]{1,0:T(8,128)(2,1)S(1)} %slice.747), channel_id=1, source_target_pairs={{8,0},{9,1},{10,2},{11,3},{12,4},{13,5},{14,6},{15,7},{24,16},{25,... | collective-permute-start | bytes 1572872 | tf_op jit(solution)/shard_map/ppermute | solution.py:34
  422.1 21.4 %collective-permute-start.26 = (bf16[256,2048]{1,0:T(8,128)(2,1)S(1)}, bf16[256,2048]{1,0:T(8,128)(2,1)S(1)}, u32[]{:S(2)}, u32[]{:S(2)}) collective-permute-start(bf16[256,2048]{1,0:T(8,128)(2,1)S(1)} %constant_dynamic-slice_fusion.3), channel_id=1, source_target_pairs={{0,1},{1,0},{2,3},{3,2},{4,5},{5,4},{6,7},{7,6},{8,9},{9,8},{10,11... | collective-permute-start | bytes 3145736 | tf_op jit(solution)/shard_map/ppermute | solution.py:34
  427.2 13.0 %collective-permute-start.34 = (bf16[256,1024]{1,0:T(8,128)(2,1)S(1)}, bf16[256,1024]{1,0:T(8,128)(2,1)S(1)}, u32[]{:S(2)}, u32[]{:S(2)}) collective-permute-start(bf16[256,1024]{1,0:T(8,128)(2,1)S(1)} %get-tuple-element.217), channel_id=1, source_target_pairs={{0,32},{1,33},{2,34},{3,35},{4,36},{5,37},{6,38},{7,39},{8,40},{9,... | collective-permute-start | bytes 1572872 | tf_op jit(solution)/shard_map/ppermute | solution.py:34
  429.4 14.0 %collective-permute-start.36 = (bf16[256,1024]{1,0:T(8,128)(2,1)S(1)}, bf16[256,1024]{1,0:T(8,128)(2,1)S(1)}, u32[]{:S(2)}, u32[]{:S(2)}) collective-permute-start(bf16[256,1024]{1,0:T(8,128)(2,1)S(1)} %get-tuple-element.218), channel_id=1, source_target_pairs={{0,96},{1,97},{2,98},{3,99},{4,100},{5,101},{6,102},{7,103},{8,104... | collective-permute-start | bytes 1572872 | tf_op jit(solution)/shard_map/ppermute | solution.py:34
  430.7 28.8 %collective-permute-start.65 = (bf16[256,1536]{1,0:T(8,128)(2,1)S(1)}, bf16[256,1536]{1,0:T(8,128)(2,1)S(1)}, u32[]{:S(2)}, u32[]{:S(2)}) collective-permute-start(bf16[256,1536]{1,0:T(8,128)(2,1)S(1)} %get-tuple-element.207), channel_id=1, source_target_pairs={{0,24},{1,25},{2,26},{3,27},{4,28},{5,29},{6,30},{7,31},{8,16},{9,... | collective-permute-start | bytes 2359304 | tf_op jit(solution)/shard_map/ppermute | solution.py:34
  444.0 10.0 %collective-permute-start.27 = (bf16[64,2048]{1,0:T(8,128)(2,1)S(1)}, bf16[64,2048]{1,0:T(8,128)(2,1)S(1)}, u32[]{:S(2)}, u32[]{:S(2)}) collective-permute-start(bf16[64,2048]{1,0:T(8,128)(2,1)S(1)} %get-tuple-element.219), channel_id=1, source_target_pairs={{0,2},{1,3},{2,4},{3,5},{4,6},{5,7},{6,0},{7,1},{8,10},{9,11},{10,... | collective-permute-start | bytes 786440 | tf_op jit(solution)/shard_map/ppermute | solution.py:34
  446.1 12.0 %collective-permute-start.28 = (bf16[64,2048]{1,0:T(8,128)(2,1)S(1)}, bf16[64,2048]{1,0:T(8,128)(2,1)S(1)}, u32[]{:S(2)}, u32[]{:S(2)}) collective-permute-start(bf16[64,2048]{1,0:T(8,128)(2,1)S(1)} %get-tuple-element.221), channel_id=1, source_target_pairs={{0,4},{1,5},{2,6},{3,7},{4,0},{5,1},{6,2},{7,3},{8,12},{9,13},{10,... | collective-permute-start | bytes 786440 | tf_op jit(solution)/shard_map/ppermute | solution.py:34
  448.7 9.3 %collective-permute-start.29 = (bf16[64,2048]{1,0:T(8,128)(2,1)S(1)}, bf16[64,2048]{1,0:T(8,128)(2,1)S(1)}, u32[]{:S(2)}, u32[]{:S(2)}) collective-permute-start(bf16[64,2048]{1,0:T(8,128)(2,1)S(1)} %get-tuple-element.220), channel_id=1, source_target_pairs={{0,6},{1,7},{2,0},{3,1},{4,2},{5,3},{6,4},{7,5},{8,14},{9,15},{10,... | collective-permute-start | bytes 786440 | tf_op jit(solution)/shard_map/ppermute | solution.py:34
  454.0 21.8 %collective-permute-start.67 = (bf16[256,1536]{1,0:T(8,128)(2,1)S(1)}, bf16[256,1536]{1,0:T(8,128)(2,1)S(1)}, u32[]{:S(2)}, u32[]{:S(2)}) collective-permute-start(bf16[256,1536]{1,0:T(8,128)(2,1)S(1)} %get-tuple-element.207), channel_id=1, source_target_pairs={{0,16},{1,17},{2,18},{3,19},{4,20},{5,21},{6,22},{7,23},{8,24},{9,... | collective-permute-start | bytes 2359304 | tf_op jit(solution)/shard_map/ppermute | solution.py:34
  458.1 17.7 %collective-permute-start.66 = (bf16[256,1536]{1,0:T(8,128)(2,1)S(1)}, bf16[256,1536]{1,0:T(8,128)(2,1)S(1)}, u32[]{:S(2)}, u32[]{:S(2)}) collective-permute-start(bf16[256,1536]{1,0:T(8,128)(2,1)S(1)} %get-tuple-element.206), channel_id=1, source_target_pairs={{0,8},{1,9},{2,10},{3,11},{4,12},{5,13},{6,14},{7,15},{8,0},{9,1},... | collective-permute-start | bytes 2359304 | tf_op jit(solution)/shard_map/ppermute | solution.py:34
  459.4 21.0 %collective-permute-start.51 = (f32[48,128]{1,0:T(8,128)S(1)}, f32[48,128]{1,0:T(8,128)S(1)}, u32[]{:S(2)}, u32[]{:S(2)}) collective-permute-start(f32[48,128]{1,0:T(8,128)S(1)} %maximum_bitcast_fusion), channel_id=1, source_target_pairs={{0,1},{1,0},{2,3},{3,2},{4,5},{5,4},{6,7},{7,6},{8,9},{9,8},{10,11... | collective-permute-start | bytes 73736 | tf_op jit(solution)/shard_map/ppermute | solution.py:34
  480.5 21.6 %collective-permute-start.52 = (f32[48,128]{1,0:T(8,128)S(1)}, f32[48,128]{1,0:T(8,128)S(1)}, u32[]{:S(2)}, u32[]{:S(2)}) collective-permute-start(f32[48,128]{1,0:T(8,128)S(1)} %fusion.120), channel_id=1, source_target_pairs={{0,2},{1,3},{2,4},{3,5},{4,6},{5,7},{6,0},{7,1},{8,10},{9,11},{10,... | collective-permute-start | bytes 73736 | tf_op jit(solution)/shard_map/ppermute | solution.py:34
  480.5 21.5 %collective-permute-start.53 = (f32[48,128]{1,0:T(8,128)S(1)}, f32[48,128]{1,0:T(8,128)S(1)}, u32[]{:S(2)}, u32[]{:S(2)}) collective-permute-start(f32[48,128]{1,0:T(8,128)S(1)} %fusion.120), channel_id=1, source_target_pairs={{0,4},{1,5},{2,6},{3,7},{4,0},{5,1},{6,2},{7,3},{8,12},{9,13},{10,... | collective-permute-start | bytes 73736 | tf_op jit(solution)/shard_map/ppermute | solution.py:34
  482.0 20.1 %collective-permute-start.54 = (f32[48,128]{1,0:T(8,128)S(1)}, f32[48,128]{1,0:T(8,128)S(1)}, u32[]{:S(2)}, u32[]{:S(2)}) collective-permute-start(f32[48,128]{1,0:T(8,128)S(1)} %fusion.120), channel_id=1, source_target_pairs={{0,6},{1,7},{2,0},{3,1},{4,2},{5,3},{6,4},{7,5},{8,14},{9,15},{10,... | collective-permute-start | bytes 73736 | tf_op jit(solution)/shard_map/ppermute | solution.py:34
  491.0 25.8 %collective-permute-start.11 = (bf16[128,2048]{1,0:T(8,128)(2,1)}, bf16[128,2048]{1,0:T(8,128)(2,1)}, u32[]{:S(2)}, u32[]{:S(2)}) collective-permute-start(bf16[128,2048]{1,0:T(8,128)(2,1)} %get-tuple-element.184), channel_id=1, source_target_pairs={{0,24},{1,25},{2,26},{3,27},{4,28},{5,29},{6,30},{7,31},{8,16},{9,... | collective-permute-start | bytes 1572872 | tf_op jit(solution)/shard_map/ppermute | solution.py:34
  502.0 15.0 %collective-permute-start.9 = (bf16[128,2048]{1,0:T(8,128)(2,1)}, bf16[128,2048]{1,0:T(8,128)(2,1)}, u32[]{:S(2)}, u32[]{:S(2)}) collective-permute-start(bf16[128,2048]{1,0:T(8,128)(2,1)} %get-tuple-element.182), channel_id=1, source_target_pairs={{0,16},{1,17},{2,18},{3,19},{4,20},{5,21},{6,22},{7,23},{8,24},{9,... | collective-permute-start | bytes 1572872 | tf_op jit(solution)/shard_map/ppermute | solution.py:34
  502.1 10.8 %collective-permute-start.55 = (f32[48,128]{1,0:T(8,128)S(1)}, f32[48,128]{1,0:T(8,128)S(1)}, u32[]{:S(2)}, u32[]{:S(2)}) collective-permute-start(f32[48,128]{1,0:T(8,128)S(1)} %add_add_fusion.5), channel_id=1, source_target_pairs={{0,16},{1,17},{2,18},{3,19},{4,20},{5,21},{6,22},{7,23},{8,24},{9,... | collective-permute-start | bytes 73736 | tf_op jit(solution)/shard_map/ppermute | solution.py:34
  504.0 9.5 %collective-permute-start.56 = (f32[48,128]{1,0:T(8,128)S(1)}, f32[48,128]{1,0:T(8,128)S(1)}, u32[]{:S(2)}, u32[]{:S(2)}) collective-permute-start(f32[48,128]{1,0:T(8,128)S(1)} %add_add_fusion.5), channel_id=1, source_target_pairs={{0,8},{1,9},{2,10},{3,11},{4,12},{5,13},{6,14},{7,15},{8,0},{9,1},... | collective-permute-start | bytes 73736 | tf_op jit(solution)/shard_map/ppermute | solution.py:34
  506.2 8.7 %collective-permute-start.57 = (f32[48,128]{1,0:T(8,128)S(1)}, f32[48,128]{1,0:T(8,128)S(1)}, u32[]{:S(2)}, u32[]{:S(2)}) collective-permute-start(f32[48,128]{1,0:T(8,128)S(1)} %add_add_fusion.5), channel_id=1, source_target_pairs={{0,24},{1,25},{2,26},{3,27},{4,28},{5,29},{6,30},{7,31},{8,16},{9,... | collective-permute-start | bytes 73736 | tf_op jit(solution)/shard_map/ppermute | solution.py:34
  512.9 21.9 %collective-permute-start.35 = (bf16[512,1024]{1,0:T(8,128)(2,1)}, bf16[512,1024]{1,0:T(8,128)(2,1)S(1)}, u32[]{:S(2)}, u32[]{:S(2)}) collective-permute-start(bf16[512,1024]{1,0:T(8,128)(2,1)} %pad_maximum_fusion.9), channel_id=1, source_target_pairs={{0,32},{1,33},{2,34},{3,35},{4,36},{5,37},{6,38},{7,39},{8,40},{9,... | collective-permute-start | bytes 3145736 | tf_op jit(solution)/shard_map/ppermute | solution.py:34
  513.6 23.7 %collective-permute-start.37 = (bf16[512,1024]{1,0:T(8,128)(2,1)}, bf16[512,1024]{1,0:T(8,128)(2,1)S(1)}, u32[]{:S(2)}, u32[]{:S(2)}) collective-permute-start(bf16[512,1024]{1,0:T(8,128)(2,1)} %pad_maximum_fusion.10), channel_id=1, source_target_pairs={{0,96},{1,97},{2,98},{3,99},{4,100},{5,101},{6,102},{7,103},{8,104... | collective-permute-start | bytes 3145736 | tf_op jit(solution)/shard_map/ppermute | solution.py:34
  514.9 15.7 %collective-permute-start.58 = (f32[48,128]{1,0:T(8,128)S(1)}, f32[48,128]{1,0:T(8,128)S(1)}, u32[]{:S(2)}, u32[]{:S(2)}) collective-permute-start(f32[48,128]{1,0:T(8,128)S(1)} %add_add_fusion.4), channel_id=1, source_target_pairs={{0,32},{1,33},{2,34},{3,35},{4,36},{5,37},{6,38},{7,39},{8,40},{9,... | collective-permute-start | bytes 73736 | tf_op jit(solution)/shard_map/ppermute | solution.py:34
  516.9 14.7 %collective-permute-start.59 = (f32[48,128]{1,0:T(8,128)S(1)}, f32[48,128]{1,0:T(8,128)S(1)}, u32[]{:S(2)}, u32[]{:S(2)}) collective-permute-start(f32[48,128]{1,0:T(8,128)S(1)} %add_add_fusion.4), channel_id=1, source_target_pairs={{0,64},{1,65},{2,66},{3,67},{4,68},{5,69},{6,70},{7,71},{8,72},{9,... | collective-permute-start | bytes 73736 | tf_op jit(solution)/shard_map/ppermute | solution.py:34
  517.1 15.3 %collective-permute-start.60 = (f32[48,128]{1,0:T(8,128)S(1)}, f32[48,128]{1,0:T(8,128)S(1)}, u32[]{:S(2)}, u32[]{:S(2)}) collective-permute-start(f32[48,128]{1,0:T(8,128)S(1)} %add_add_fusion.4), channel_id=1, source_target_pairs={{0,96},{1,97},{2,98},{3,99},{4,100},{5,101},{6,102},{7,103},{8,104... | collective-permute-start | bytes 73736 | tf_op jit(solution)/shard_map/ppermute | solution.py:34
  530.6 7.3 %collective-permute-start.30 = (bf16[64,2048]{1,0:T(8,128)(2,1)S(1)}, bf16[64,2048]{1,0:T(8,128)(2,1)S(1)}, u32[]{:S(2)}, u32[]{:S(2)}) collective-permute-start(bf16[64,2048]{1,0:T(8,128)(2,1)S(1)} %get-tuple-element.161), channel_id=1, source_target_pairs={{0,6},{1,7},{2,0},{3,1},{4,2},{5,3},{6,4},{7,5},{8,14},{9,15},{10,... | collective-permute-start | bytes 786440 | tf_op jit(solution)/shard_map/ppermute | solution.py:34
  531.6 18.7 %collective-permute-start.10 = (bf16[256,2048]{1,0:T(8,128)(2,1)S(1)}, bf16[256,2048]{1,0:T(8,128)(2,1)S(1)}, u32[]{:S(2)}, u32[]{:S(2)}) collective-permute-start(bf16[256,2048]{1,0:T(8,128)(2,1)S(1)} %pad_maximum_fusion.7), channel_id=1, source_target_pairs={{0,16},{1,17},{2,18},{3,19},{4,20},{5,21},{6,22},{7,23},{8,24},{9,... | collective-permute-start | bytes 3145736 | tf_op jit(solution)/shard_map/ppermute | solution.py:34
  532.4 17.9 %collective-permute-start.12 = (bf16[256,2048]{1,0:T(8,128)(2,1)S(1)}, bf16[256,2048]{1,0:T(8,128)(2,1)S(1)}, u32[]{:S(2)}, u32[]{:S(2)}) collective-permute-start(bf16[256,2048]{1,0:T(8,128)(2,1)S(1)} %pad_maximum_fusion.8), channel_id=1, source_target_pairs={{0,24},{1,25},{2,26},{3,27},{4,28},{5,29},{6,30},{7,31},{8,16},{9,... | collective-permute-start | bytes 3145736 | tf_op jit(solution)/shard_map/ppermute | solution.py:34
  534.8 19.8 %collective-permute-start.31 = (bf16[64,2048]{1,0:T(8,128)(2,1)S(1)}, bf16[64,2048]{1,0:T(8,128)(2,1)S(1)}, u32[]{:S(2)}, u32[]{:S(2)}) collective-permute-start(bf16[64,2048]{1,0:T(8,128)(2,1)S(1)} %get-tuple-element.161), channel_id=1, source_target_pairs={{0,4},{1,5},{2,6},{3,7},{4,0},{5,1},{6,2},{7,3},{8,12},{9,13},{10,... | collective-permute-start | bytes 786440 | tf_op jit(solution)/shard_map/ppermute | solution.py:34
  537.2 31.5 %collective-permute-start.32 = (bf16[64,2048]{1,0:T(8,128)(2,1)S(1)}, bf16[64,2048]{1,0:T(8,128)(2,1)S(1)}, u32[]{:S(2)}, u32[]{:S(2)}) collective-permute-start(bf16[64,2048]{1,0:T(8,128)(2,1)S(1)} %get-tuple-element.161), channel_id=1, source_target_pairs={{0,2},{1,3},{2,4},{3,5},{4,6},{5,7},{6,0},{7,1},{8,10},{9,11},{10,... | collective-permute-start | bytes 786440 | tf_op jit(solution)/shard_map/ppermute | solution.py:34
  537.9 30.9 %collective-permute-start.38 = (bf16[128,1024]{1,0:T(8,128)(2,1)S(1)}, bf16[128,1024]{1,0:T(8,128)(2,1)S(1)}, u32[]{:S(2)}, u32[]{:S(2)}) collective-permute-start(bf16[128,1024]{1,0:T(8,128)(2,1)S(1)} %get-tuple-element.215), channel_id=1, source_target_pairs={{0,16},{1,17},{2,18},{3,19},{4,20},{5,21},{6,22},{7,23},{8,24},{9,... | collective-permute-start | bytes 786440 | tf_op jit(solution)/shard_map/ppermute | solution.py:34
  552.1 10.5 %collective-permute-start.13 = (bf16[64,2048]{1,0:T(8,128)(2,1)S(1)}, bf16[64,2048]{1,0:T(8,128)(2,1)S(1)}, u32[]{:S(2)}, u32[]{:S(2)}) collective-permute-start(bf16[64,2048]{1,0:T(8,128)(2,1)S(1)} %get-tuple-element.224), channel_id=1, source_target_pairs={{0,2},{1,3},{2,4},{3,5},{4,6},{5,7},{6,0},{7,1},{8,10},{9,11},{10,... | collective-permute-start | bytes 786440 | tf_op jit(solution)/shard_map/ppermute | solution.py:34
  553.5 12.1 %collective-permute-start.14 = (bf16[64,2048]{1,0:T(8,128)(2,1)S(1)}, bf16[64,2048]{1,0:T(8,128)(2,1)S(1)}, u32[]{:S(2)}, u32[]{:S(2)}) collective-permute-start(bf16[64,2048]{1,0:T(8,128)(2,1)S(1)} %get-tuple-element.226), channel_id=1, source_target_pairs={{0,4},{1,5},{2,6},{3,7},{4,0},{5,1},{6,2},{7,3},{8,12},{9,13},{10,... | collective-permute-start | bytes 786440 | tf_op jit(solution)/shard_map/ppermute | solution.py:34
  554.6 10.9 %collective-permute-start.15 = (bf16[64,2048]{1,0:T(8,128)(2,1)S(1)}, bf16[64,2048]{1,0:T(8,128)(2,1)S(1)}, u32[]{:S(2)}, u32[]{:S(2)}) collective-permute-start(bf16[64,2048]{1,0:T(8,128)(2,1)S(1)} %get-tuple-element.225), channel_id=1, source_target_pairs={{0,6},{1,7},{2,0},{3,1},{4,2},{5,3},{6,4},{7,5},{8,14},{9,15},{10,... | collective-permute-start | bytes 786440 | tf_op jit(solution)/shard_map/ppermute | solution.py:34
  568.7 23.0 %collective-permute-start.33 = (bf16[256,2048]{1,0:T(8,128)(2,1)S(1)}, bf16[256,2048]{1,0:T(8,128)(2,1)}, u32[]{:S(2)}, u32[]{:S(2)}) collective-permute-start(bf16[256,2048]{1,0:T(8,128)(2,1)S(1)} %bitcast.318), channel_id=1, source_target_pairs={{0,1},{1,0},{2,3},{3,2},{4,5},{5,4},{6,7},{7,6},{8,9},{9,8},{10,11... | collective-permute-start | bytes 3145736 | tf_op jit(solution)/shard_map/ppermute | solution.py:34
  569.6 20.2 %collective-permute-start.40 = (bf16[256,1024]{1,0:T(8,128)(2,1)S(1)}, bf16[256,1024]{1,0:T(8,128)(2,1)S(1)}, u32[]{:S(2)}, u32[]{:S(2)}) collective-permute-start(bf16[256,1024]{1,0:T(8,128)(2,1)S(1)} %fusion.26), channel_id=1, source_target_pairs={{0,8},{1,9},{2,10},{3,11},{4,12},{5,13},{6,14},{7,15},{8,0},{9,1},... | collective-permute-start | bytes 1572872 | tf_op jit(solution)/shard_map/ppermute | solution.py:34
  572.5 10.7 %collective-permute-start.17 = (bf16[64,2048]{1,0:T(8,128)(2,1)S(1)}, bf16[64,2048]{1,0:T(8,128)(2,1)S(1)}, u32[]{:S(2)}, u32[]{:S(2)}) collective-permute-start(bf16[64,2048]{1,0:T(8,128)(2,1)S(1)} %get-tuple-element.167), channel_id=1, source_target_pairs={{0,4},{1,5},{2,6},{3,7},{4,0},{5,1},{6,2},{7,3},{8,12},{9,13},{10,... | collective-permute-start | bytes 786440 | tf_op jit(solution)/shard_map/ppermute | solution.py:34
  572.7 15.1 %collective-permute-start.18 = (bf16[64,2048]{1,0:T(8,128)(2,1)S(1)}, bf16[64,2048]{1,0:T(8,128)(2,1)S(1)}, u32[]{:S(2)}, u32[]{:S(2)}) collective-permute-start(bf16[64,2048]{1,0:T(8,128)(2,1)S(1)} %get-tuple-element.167), channel_id=1, source_target_pairs={{0,2},{1,3},{2,4},{3,5},{4,6},{5,7},{6,0},{7,1},{8,10},{9,11},{10,... | collective-permute-start | bytes 786440 | tf_op jit(solution)/shard_map/ppermute | solution.py:34
  (53 other events, 353.6 us)

commit v3 on v2

--- a/solution.py
+++ b/solution.py
@@ -564,6 +564,327 @@
     )
 
 
+MCOLS = 1664
+
+
+def at(first, size):
+    return pl.ds(pl.multiple_of(first, size), size)
+
+
+def scatter_buffers():
+    return [
+        pltpu.VMEM((4, HALF, WIDTH), BF),
+        pltpu.VMEM((2, 2, 32, WIDTH), BF),
+        pltpu.VMEM((2, 4, 32, WIDTH), BF),
+        pltpu.VMEM((3, 32, WIDTH), BF),
+        pltpu.VMEM((4, 3, 32, WIDTH), BF),
+        pltpu.VMEM((3, 32, WIDTH), BF),
+    ]
+
+
+class TokenSum:
+    def __init__(self, links, give, keep, landings):
+        self.links, self.give, self.keep = links, give, keep
+        self.core_in, self.p_one_in, self.p_two_in, self.p_three_in, self.q_one_in, self.q_two_in = landings
+        self.core, self.p_one, self.p_two, self.q_one, self.q_two = {}, [], [], {}, []
+
+    def give_core(self, k):
+        self.core[k] = self.links.send(self.give.at[k], self.core_in.at[k], dc=1)
+
+    def q_part(self, k, place):
+        return self.keep.at[k, at(place * HOME + 32, 32)]
+
+    def add(self, k):
+        links, keep = self.links, self.keep
+        z = links.here[2]
+        self.core[k].wait_recv()
+        keep[k] = (keep[k].astype(F32) + self.core_in[k].astype(F32)).astype(BF)
+        self.q_one[k] = [
+            links.send(
+                self.q_part(k, lax.rem(z + d + 4, 4)), self.q_one_in.at[k, n], dz=d
+            )
+            for n, d in enumerate((1, -1, 2))
+        ]
+        rows = keep.at[k].reshape(4, HOME, WIDTH)
+        first = pl.ds(0, 32)
+        if k == 0:
+            self.p_one = [
+                links.send(rows.at[pl.ds(0, 2), first], self.p_one_in.at[0], dy=1),
+                links.send(rows.at[pl.ds(2, 2), first], self.p_one_in.at[1], dy=-1),
+            ]
+        elif k < 3:
+            n = k - 1
+            self.p_one[n].wait_recv()
+            for i in range(2):
+                row = (2 * n + i) * HOME
+                keep[k, row : row + 32] = (
+                    keep[k, row : row + 32].astype(F32) + self.p_one_in[n, i].astype(F32)
+                ).astype(BF)
+            self.p_two.append(
+                links.send(rows.at[:, first], self.p_two_in.at[n], dy=(1, -1)[n])
+            )
+
+    def q_sum(self, k):
+        z = self.links.here[2]
+        for copy in self.q_one[k]:
+            copy.wait_recv()
+        part = self.keep[k, at(z * HOME + 32, 32), :].astype(F32)
+        for n in range(3):
+            part = part + self.q_one_in[k, n].astype(F32)
+        return part
+
+    def q_send(self, k, buffer):
+        buffer[k] = self.q_sum(k).astype(BF)
+        self.q_two.append(
+            self.links.send(buffer.at[k], self.q_two_in.at[k], dy=(2, 1, -1)[k])
+        )
+
+    def p_send(self):
+        links, keep = self.links, self.keep
+        z = links.here[2]
+        arrived(self.p_two)
+        for place in range(4):
+            row = place * HOME
+            keep[3, row : row + 32] = (
+                keep[3, row : row + 32].astype(F32)
+                + self.p_two_in[0, place].astype(F32)
+                + self.p_two_in[1, place].astype(F32)
+            ).astype(BF)
+        self.p_three = [
+            links.send(
+                keep.at[3, at(lax.rem(z + d + 4, 4) * HOME, 32)], self.p_three_in.at[n], dz=d
+            )
+            for n, d in enumerate((1, -1, 2))
+        ]
+
+    def home(self):
+        z = self.links.here[2]
+        second = self.q_sum(3)
+        arrived(self.q_two)
+        for n in range(3):
+            second = second + self.q_two_in[n].astype(F32)
+        arrived(self.p_three)
+        first = self.keep[3, at(z * HOME, 32), :].astype(F32)
+        for n in range(3):
+            first = first + self.p_three_in[n].astype(F32)
+        return first, second
+
+
+TOKEN_SUM_COPIES = 4 + 12 + 2 + 2 + 3 + 3
+
+
+def spread_home(links, array, home_ref):
+    x, y, z, c = links.here
+    return [links.send(home_ref, array.at[c, z], dz=d) for d in (1, -1, 2)]
+
+
+def experts(
+    x_all, g_all, picked_all, w_in_hbm, w_out_hbm, weights, hidden_ref,
+    gated_out, grad_out, grad_near_out, low_all, hidden_grad_out, gain_out,
+    w_in, w_out, gain_ref, x_ref, g_ref, picked_ref, gates_ref, gate_grad_ref, back_ref, pre_ref,
+    gated_ref, give, keep, grad_ref, q_buffer, home_ref,
+    core_in, p_one_in, p_two_in, p_three_in, q_one_in, q_two_in,
+    send_sems, recv_sems, local_sems,
+):
+    links = Links(send_sems, recv_sems)
+    x, y, z, c = links.here
+    x_after, x_before, x_far = lax.rem(x + 1, 4), lax.rem(x + 3, 4), lax.rem(x + 2, 4)
+    order = (lax.rem(y + 2, 4), lax.rem(y + 1, 4), lax.rem(y + 3, 4), y)
+    loads = []
+
+    def load(source, target):
+        copy = pltpu.make_async_copy(source, target, local_sems.at[len(loads)])
+        copy.start()
+        loads.append(copy)
+        return copy
+
+    first = [load(g_all.at[order[0]], g_ref.at[0]), load(w_out_hbm, w_out)]
+    first += [load(picked_all.at[place], picked_ref.at[k]) for k, place in enumerate(order)]
+    first.append(load(weights.at[:, :, pl.ds(0, 256), pl.ds(768, 128)], w_in.at[:, :, :, pl.ds(1024, 128)]))
+    first.append(load(weights.at[:, :, pl.ds(256, 16), pl.ds(0, 256)], gain_ref))
+    first.append(load(x_all.at[order[0]], x_ref.at[0]))
+    first += [
+        load(w_in_hbm.at[e], w_in.at[:, :, :, pl.ds(e * 256, 256)]) for e in range(4)
+    ]
+    rest = [
+        [load(g_all.at[order[k]], g_ref.at[k]), load(x_all.at[order[k]], x_ref.at[k])]
+        for k in range(1, 4)
+    ]
+    links.greet(STEPS_X + STEPS_Y + STEPS_Z + STEPS_C)
+    for copy in first:
+        copy.wait()
+
+    sums = TokenSum(links, give, keep, (core_in, p_one_in, p_two_in, p_three_in, q_one_in, q_two_in))
+    lanes = lax.broadcasted_iota(jnp.int32, (ROWS, 128), 1)
+    own_rows = at(c * HALF, HALF)
+    other_rows = at((1 - c) * HALF, HALF)
+
+    def in_block(first_column, size):
+        return w_in[:, :, :, pl.ds(first_column, size)].reshape(WIDTH, size)
+
+    for k in range(4):
+        if k:
+            for copy in rest[k - 1]:
+                copy.wait()
+        logits = dot(x_ref[k], in_block(1024, 128))
+        logits = jnp.where(picked_ref[k].astype(F32) > 0.5, logits, MASKED_SCORE)
+        exponents = jnp.exp(logits - jnp.max(logits, axis=-1, keepdims=True))
+        gates_ref[...] = exponents / jnp.sum(exponents, axis=-1, keepdims=True)
+        gate_grad_ref[...] = jnp.zeros_like(gate_grad_ref)
+        back_ref[...] = dot_nt(g_ref[k], w_out[...].reshape(512, WIDTH))
+
+        def one_expert(e, carry, k=k):
+            joined = dot(x_ref[k], in_block(pl.multiple_of(e * 256, 256), 256))
+            gate_pre, up_pre = joined[:, :128], joined[:, 128:]
+            logistic = 1.0 / (1.0 + jnp.exp(-gate_pre))
+            silu_gate = gate_pre * logistic
+            silu_slope = logistic * (1.0 + gate_pre * (1.0 - logistic))
+            act = silu_gate * up_pre
+            back = back_ref[:, at(e * 128, 128)]
+            mine = lanes == y * 4 + e
+            gate = jnp.sum(jnp.where(mine, gates_ref[...], 0.0), axis=-1, keepdims=True)
+            term = jnp.sum(act.astype(BF).astype(F32) * back, axis=-1, keepdims=True)
+            gate_grad_ref[...] += jnp.where(mine, term, 0.0)
+            act_grad = back * gate
+            pre_ref[k, :, pl.ds(pl.multiple_of(e * 256, 256), 128)] = (
+                act_grad * up_pre * silu_slope
+            ).astype(BF)
+            pre_ref[k, :, pl.ds(pl.multiple_of(e * 256 + 128, 128), 128)] = (
+                act_grad * silu_gate
+            ).astype(BF)
+            gated_ref[k, :, at(e * 128, 128)] = (act * gate).astype(BF)
+            return carry
+
+        lax.fori_loop(0, 4, one_expert, 0)
+        gates, gate_grad = gates_ref[...], gate_grad_ref[...]
+        logit_grad = gates * (gate_grad - jnp.sum(gates * gate_grad, axis=-1, keepdims=True))
+        pre_ref[k, :, 1024:1152] = logit_grad.astype(BF)
+
+        def back_rows(rows, target, k=k):
+            def one_block(s, carry):
+                block = w_in[s // 2, lax.rem(s, 2)]
+                target[k, :, at(s * 256, 256)] = dot_nt(pre_ref[k, rows, :], block).astype(BF)
+                return carry
+
+            lax.fori_loop(0, 8, one_block, 0)
+
+        back_rows(other_rows, give)
+        sums.give_core(k)
+        back_rows(own_rows, keep)
+        if k:
+            sums.q_send(k - 1, q_buffer)
+        sums.add(k)
+    sums.p_send()
+    keep_gated = pltpu.make_async_copy(gated_ref, gated_out, local_sems.at[len(loads)])
+    keep_gated.start()
+
+    def weight_grad(slot):
+        columns = at(slot * 256, 256)
+        rows = x_ref[:, :, columns].reshape(4 * ROWS, 256)
+        grad_ref[slot, :, 0:1152] = dot_tn(rows, pre_ref[...].reshape(4 * ROWS, 1152)).astype(BF)
+        rows = g_ref[:, :, columns].reshape(4 * ROWS, 256)
+        grad_ref[slot, :, 1152:MCOLS] = dot_tn(rows, gated_ref[...].reshape(4 * ROWS, 512)).astype(BF)
+
+    def weight_grads(place):
+        def one_slot(i, carry):
+            weight_grad(place * 2 + i)
+            return carry
+
+        lax.fori_loop(0, 2, one_slot, 0)
+
+    weight_grads(x_far)
+    near = [
+        links.send(grad_ref.at[x_far * 2], grad_near_out.at[0], dx=1),
+        links.send(grad_ref.at[x_far * 2 + 1], grad_near_out.at[1], dx=-1),
+    ]
+
+    moe_gains = jnp.concatenate(
+        [gain_ref[s // 2, s % 2].astype(F32)[1:2] for s in range(8)], axis=1
+    )
+    moe_grad = jnp.concatenate(sums.home(), axis=0)
+    hidden = hidden_ref[...]
+    home_grad = g_ref[3, at(c * HALF + z * HOME, HOME), :].astype(F32)
+    back, gain_rows = norm_back(moe_grad, hidden, rms_scale(hidden), moe_gains)
+    hidden_grad = home_grad + back
+    hidden_grad_out[...] = hidden_grad
+    gain_out[...] = jnp.broadcast_to(jnp.sum(gain_rows, axis=0, keepdims=True), (8, WIDTH))
+    home_ref[...] = hidden_grad.astype(BF)
+    place_home = pltpu.make_async_copy(home_ref, low_all.at[c, z], local_sems.at[len(loads) + 1])
+    place_home.start()
+    low_near = spread_home(links, low_all, home_ref)
+
+    def other_grads(i, carry):
+        weight_grad(lax.rem(x_far * 2 + 2 + i, 8))
+        return carry
+
+    lax.fori_loop(0, 6, other_grads, 0)
+    arrived(low_near)
+    place_home.wait()
+    sibling = links.send(low_all.at[c], low_all.at[c], dc=1)
+    keep_grad = pltpu.make_async_copy(grad_ref, grad_out, local_sems.at[len(loads) + 2])
+    keep_grad.start()
+    arrived(near)
+    sibling.wait_recv()
+    keep_gated.wait()
+    keep_grad.wait()
+    links.finish()
+
+
+EXPERT_COPIES = TOKEN_SUM_COPIES + 2 + 3 + 1
+
+
+def run_experts(moe_in_all, grad_all, picked_all, experts_in, experts_out, weights, hidden):
+    shape = jax.ShapeDtypeStruct
+    outs = (
+        (shape((4, ROWS, 512), BF), ANY),
+        (shape((8, 256, MCOLS), BF), ANY),
+        (shape((2, 256, MCOLS), BF), ANY),
+        (shape((2, 4, HOME, WIDTH), BF), ANY),
+        (shape((HOME, WIDTH), F32), VMEM),
+        (shape((8, WIDTH), F32), VMEM),
+    )
+    return pl.pallas_call(
+        experts,
+        out_shape=[o for o, _ in outs],
+        in_specs=[ANY] * 6 + [VMEM],
+        out_specs=[spec for _, spec in outs],
+        scratch_shapes=[
+            pltpu.VMEM((4, 2, 256, 1152), BF),
+            pltpu.VMEM((4, 128, WIDTH), BF),
+            pltpu.VMEM((4, 2, 16, 256), BF),
+            pltpu.VMEM((4, ROWS, WIDTH), BF),
+            pltpu.VMEM((4, ROWS, WIDTH), BF),
+            pltpu.VMEM((4, ROWS, 128), BF),
+            pltpu.VMEM((ROWS, 128), F32),
+            pltpu.VMEM((ROWS, 128), F32),
+            pltpu.VMEM((ROWS, 512), F32),
+            pltpu.VMEM((4, ROWS, 1152), BF),
+            pltpu.VMEM((4, ROWS, 512), BF),
+            pltpu.VMEM((4, HALF, WIDTH), BF),
+            pltpu.VMEM((4, HALF, WIDTH), BF),
+            pltpu.VMEM((8, 256, MCOLS), BF),
+            pltpu.VMEM((3, 32, WIDTH), BF),
+            pltpu.VMEM((HOME, WIDTH), BF),
+            *scatter_buffers(),
+            pltpu.SemaphoreType.DMA((EXPERT_COPIES,)),
+            pltpu.SemaphoreType.DMA((EXPERT_COPIES,)),
+            pltpu.SemaphoreType.DMA((24,)),
+        ],
+        compiler_params=pltpu.CompilerParams(
+            collective_id=2, has_side_effects=True, vmem_limit_bytes=62 * MIB
+        ),
+        name="experts",
+    )(
+        moe_in_all.reshape(4, ROWS, WIDTH),
+        grad_all,
+        picked_all,
+        experts_in,
+        experts_out,
+        weights,
+        hidden,
+    )
+
+
 def turn_tables():
     frequency = ROPE_BASE ** (-(np.arange(0, 128, 2, dtype=np.float64) / 128))
     angles = np.arange(1024, dtype=np.float64)[:, None] * frequency[None, :]
@@ -649,25 +970,18 @@
         tokens.reshape(rows, width), own_weights, turn_tables(), segments,
         gate_weight, up_weight, down_weight, own_grad, own_picked,
     )
+    gated, grad_moe, grad_near, hidden_low, hidden_grad, gain_sum = run_experts(
+        moe_in_all, grad_all, picked_all, experts_in, experts_out, weights, hidden
+    )
+    hidden_low = hidden_low.reshape(rows, width)
     weights = weights.reshape(8, WROWS, WCOLS)
     w_stacked = weights[:, :256, :768].reshape(width, -1)
-    w_router = weights[:, :256, 768:896].reshape(width, -1)
     w_out_t = weights[:, :256, 896:].transpose(0, 2, 1).reshape(width, -1)
     gain_rows = weights[:, 256:].astype(F32)
     attn_gains = gain_rows[:, 0, :256].reshape(-1)
     moe_gains = gain_rows[:, 1, :256].reshape(-1)
     head_gains = jnp.sum(gain_rows[:, 2:6, :128], axis=0)
 
-    def wide(part):
-        return part.transpose(1, 2, 3, 0, 4).reshape(width, -1)
-
-    w_in = jnp.concatenate(
-        [wide(experts_in[..., :128]), wide(experts_in[..., 128:]), w_router], axis=1
-    )
-    w_down_t = experts_out.reshape(-1, width).T
-    grad_all = grad_all.reshape(4 * rows, width)
-    picked = picked_all.reshape(4 * rows, -1)[:, :experts] > 0
-    moe_in = moe_in_all.reshape(4 * rows, width)
     inputs = tokens.reshape(rows, width).astype(F32)
     first_row = ctx * rows
     places = first_row + jnp.arange(rows, dtype=jnp.int32)
@@ -698,88 +1012,45 @@
     home_row = (core * 4 + z) * home
     home_inputs = lax.dynamic_slice_in_dim(tokens.reshape(rows, width), home_row, home, 0).astype(F32)
     home_scale_one = home_scale_one[:, :1]
-    home_grad = lax.dynamic_slice_in_dim(own_grad, home_row, home, 0).astype(F32)
-    scale_two = rms_scale(hidden)
-
-    joined = dot(moe_in, w_in)
-    logits = jnp.where(picked, joined[:, 2 * span : 2 * span + experts], -jnp.inf)
-    gates = jax.nn.softmax(logits, axis=-1)
-    own_gates = lax.dynamic_slice_in_dim(gates, y * own_experts, own_experts, 1)
-    wide_gates = jnp.repeat(own_gates, hidden_units, axis=1)
-    gate_pre, up_pre = joined[:, :span], joined[:, span : 2 * span]
-    logistic = jax.nn.sigmoid(gate_pre)
-    silu_gate = gate_pre * logistic
-    silu_slope = logistic * (1.0 + gate_pre * (1.0 - logistic))
-    act = silu_gate * up_pre
-    act_back = dot(grad_all, w_down_t)
-    gate_terms = jnp.sum(
-        (act.astype(BF).astype(F32) * act_back).reshape(-1, own_experts, hidden_units), axis=-1
-    )
-    gate_grad = lax.dynamic_update_slice_in_dim(
-        jnp.zeros_like(gates), gate_terms, y * own_experts, 1
-    )
-    logit_grad = gates * (gate_grad - jnp.sum(gates * gate_grad, axis=-1, keepdims=True))
-    act_grad = act_back * wide_gates
-    pre_grad = jnp.concatenate(
-        [
-            (act_grad * up_pre * silu_slope).astype(BF),
-            (act_grad * silu_gate).astype(BF),
-            jnp.pad(logit_grad.astype(BF), ((0, 0), (0, 128 - experts))),
-        ],
-        axis=1,
-    )
-    gated_act = (act * wide_gates).astype(BF)
-    moe_in_part = dot_nt(pre_grad, w_in).astype(BF)
-    moe_in_grad = tokens_sum(moe_in_part)
-    moe_part = dot_nt(gated_act, w_down_t).astype(BF)
-    moe_part, _ = lax.optimization_barrier((moe_part, moe_in_grad))
+
+    moe_part = dot(gated.reshape(4 * rows, -1), experts_out.reshape(-1, width)).astype(BF)
+    far, after, before, mine = [moe_part[k * rows : k * rows + rows] for k in range(4)]
+    moe_part = in_order([mine, after, far, before], y).reshape(4 * rows, width)
     layer_rows = (hidden + tokens_sum(moe_part)).astype(BF)
     layer_out = spread_rows(layer_rows).reshape(tokens.shape)
-    grad_in = dot_tn(moe_in, pre_grad).astype(BF)
-    grad_down_t = dot_tn(grad_all, gated_act).astype(BF)
-    grad_in, grad_down_t, _ = lax.optimization_barrier((grad_in, grad_down_t, moe_in_grad))
-    grad_moe = ring_scatter(
-        [
-            jnp.concatenate([a[:, : 2 * span], b], axis=1)
-            for a, b in zip(
-                by_distance(grad_in.reshape(4, 512, -1), x),
-                by_distance(grad_down_t.reshape(4, 512, -1), x),
-            )
-        ],
-        "x",
-    ).astype(BF)
-    grad_moe = grad_moe.reshape(2, 256, -1)
+    own_chunk, to_after, _, to_before = by_distance(grad_moe.reshape(4, 2, 256, -1), x)
+    to_after = jnp.stack([added(to_after[0], grad_near[0]).astype(BF), to_after[1]])
+    to_before = jnp.stack([to_before[0], added(to_before[1], grad_near[1]).astype(BF)])
+    grad_moe = added(own_chunk, hop(to_after, dx=1), hop(to_before, dx=-1))
+    grad_router = jnp.concatenate(
+        [grad_moe[0, :, 1024 : 1024 + experts], grad_moe[1, :, 1024 : 1024 + experts]], axis=0
+    ).T.reshape(-1, 128)
+    grad_moe = grad_moe.astype(BF)
     keep = lax.dynamic_index_in_dim(grad_moe, y_low, 0, keepdims=False)
     give = lax.dynamic_index_in_dim(grad_moe, 1 - y_low, 0, keepdims=False)
     grad_groups = in_order(
         [keep, hop(give, dy=-1), hop(keep, dy=2), hop(give, dy=1)], y
     )
-
-    def ungrouped(part):
-        parted = part.reshape(4, 256, own_experts, hidden_units)
-        return parted.transpose(0, 2, 1, 3).reshape(experts, 256, hidden_units).astype(F32)
-
-    grad_gate_weight = ungrouped(grad_groups[:, :, :span])
-    grad_up_weight = ungrouped(grad_groups[:, :, span : 2 * span])
+    joined = grad_groups[:, :, :1024].reshape(4, 256, own_experts, 256).transpose(0, 2, 1, 3)
+    grad_gate_weight = joined[..., :128].reshape(experts, 256, hidden_units).astype(F32)
+    grad_up_weight = joined[..., 128:].reshape(experts, 256, hidden_units).astype(F32)
     grad_down_weight = (
-        grad_groups[:, :, 2 * span :]
+        grad_groups[:, :, 1152:]
         .reshape(4, 256, own_experts, hidden_units)
         .transpose(0, 2, 3, 1)
         .reshape(experts, hidden_units, 256)
         .astype(F32)
     )
-
-    hidden_norm_grad, moe_gain_rows = norm_back(moe_in_grad, hidden, scale_two, moe_gains)
-    hidden_grad = home_grad + hidden_norm_grad
-    hidden_low = spread_rows(hidden_grad.astype(BF))
-    grad_router = grad_in[:, 2 * span : 2 * span + experts]
-    early = jnp.concatenate([grad_router.T.astype(F32), jnp.sum(moe_gain_rows, axis=0)[None]], axis=0)
-    early = early.reshape(-1, 128)
+    grad_router = grad_router + hop(grad_router, dc=1)
+    for axis in "zy":
+        grad_router = direct_scatter([grad_router] * 4, axis)
+    grad_router = grad_router.reshape(experts, 2, 256)
+    grad_router = lax.dynamic_index_in_dim(grad_router, y_low, 1, keepdims=False).T
+    early = gain_sum[0].reshape(-1, 128)
     early = early + hop(early, dc=1)
     for axis in "zyx":
         early = direct_scatter([early] * 4, axis)
-    early = early.reshape(experts + 1, width)
-    early = lax.dynamic_slice_in_dim(early, shard * 256, 256, 1)
+    grad_moe_gain = lax.dynamic_slice_in_dim(early.reshape(-1), shard * 256, 256, 0)
 
     mixed_grad = dot(hidden_low, w_out_t).astype(BF)
     grad_out_t = dot_tn(hidden_low, mixed_low)
@@ -840,9 +1111,9 @@
         grad_attn[:, 256:512],
         grad_attn[:, 512:768],
         grad_attn[:, 768:].T,
-        early[:experts].T,
+        grad_router,
         grad_attn_gain,
-        early[experts],
+        grad_moe_gain,
         late_heads[0],
         late_heads[1],
         grad_gate_weight,

time: 612 us -> 556 us (0.908)
  Pallas kernels: 130 us -> 219 us
  matrix products: 90.7 us -> 22.2 us
  waiting for transfers between devices: 140 us -> 97.1 us
  other arithmetic: 70.4 us -> 57.3 us
  local copies, waits for them, and re-layouts: 80.4 us -> 67.8 us
    pallas_call x0 -> x1, Pallas kernels: none -> 88.5 us  [run_experts(): pl.pallas_call(experts, out_shape=[o for o, _ in outs], in_specs=[ANY] *...]
    ppermute x68 -> x61, waiting for transfers between devices: 140 us -> 97.1 us  [hop(): return lax.ppermute(value, AXES, pairs)]
    dot_general x8 -> x6, matrix products: 32.6 us -> 6.6 us  [dot_tn(): lax.dot_general(left, right, (((0,), (0,)), ((), ())), preferred_element_...]
    dot_general x7 -> x5, matrix products: 26.7 us -> 5.11 us  [dot_nt(): lax.dot_general(left, right, (((1,), (1,)), ((), ())), preferred_element_...]
    dot_general x5 -> x4, matrix products: 31.3 us -> 10.5 us  [dot(): return jnp.dot(left, right, preferred_element_type=F32)]
    transpose x4 -> x0, local copies, waits for them, and re-layouts: 9.21 us -> none  [the longest x3 8.6 us: wide(): return part.transpose(1, 2, 3, 0, 4).reshape(width, -1)]
    broadcast_in_dim x1 -> x3, local copies, waits for them, and re-layouts: 0.01 us -> 6.54 us  [in_order(): lax.dynamic_update_index_in_dim(whole, block, (start + distance) % 4, 0)]
    convert_element_type x7 -> x4, other arithmetic: 15.2 us -> 8.81 us  [the longest x1 2.72 us: body(): added(to_after[0], grad_near[0]).astype(BF)]
  transfers between devices with their start and end apart: 68 -> 61, of which waited for: 25 -> 26; matrix products, arithmetic and copies ran while one was open for 23% -> 22% of each run, Pallas kernels for 0% -> 0%
where the time goes in v3:
time: 556 us; the launch traced here: 549 us
  Pallas kernels  219 us (39%)
  waiting for transfers between devices  97.1 us (17%)
  starting transfers between devices  83.5 us (15%)
  local copies, waits for them, and re-layouts  67.8 us (12%)
  other arithmetic  57.3 us (10%)
  matrix products  22.2 us (4%)
    pallas_call x1, Pallas kernels, run_front(): pl.pallas_call(front, out_shape=[o for o, _ in outs], in_specs=[VMEM] * 6...  130 us
    ppermute x61, waiting for transfers between devices, hop(): return lax.ppermute(value, AXES, pairs)  97.1 us
    pallas_call x1, Pallas kernels, run_experts(): pl.pallas_call(experts, out_shape=[o for o, _ in outs], in_specs=[ANY] *...  88.5 us
    ppermute x61, starting transfers between devices, hop(): return lax.ppermute(value, AXES, pairs)  83.5 us
    unnamed x73, local copies, waits for them, and re-layouts  16.7 us
  transfers between devices with their start and end apart: 61, of which 26 were waited for; matrix products, arithmetic and copies ran while one was open for 22% of the time, Pallas kernels for 0%

profile of v3, /device:TPU:14, one launch (start us, length us, event | category | flops | bytes accessed | tf_op | source)
XLA Modules:
  0.0 548.5 jit_solution(5834445919151781042)
XLA Ops:
  6.4 2.9 fusion.9
  13.4 130.0 %front.1 = (bf16[4,2,272,1152]{3,2,1,0:T(8,128)(2,1)}, bf16[4,4,2,256,256]{4,3,2,1,0:T(8,128)(2,1)}, bf16[4,128,2048]{2,1,0:T(8,128)(2,1)}, bf16[4,512,2048]{2,1...) custom-call(bf16[512,2048]{1,0:T(8,128)(2,1)} %bitcast.258, ...), custom_call_target="tpu_custom_call" | custom-call | tf_op jit(solution)/shard_map/front/pallas_call | solution.py:530
  143.4 88.5 %experts.1 = (bf16[4,512,512]{2,1,0:T(8,128)(2,1)}, bf16[8,256,1664]{2,1,0:T(8,128)(2,1)}, bf16[2,256,1664]{2,1,0:T(8,128)(2,1)}, bf16[2,4,64,2048]{3,2,1,0:T(8,...) custom-call(bf16[4,512,2048]{2,1,0:T(8,128)(2,1)} %bitcast.247, bf16[4,512,2048]{2,1,0:T(8,128)(2,1)} %get-tuple-element.72.g_all, ...), custom_call_target="tpu_custom_call" | custom-call | tf_op jit(solution)/shard_map/experts/pallas_call | solution.py:846
  231.9 2.6 dynamic-slice_bitcast_fusion.2
  234.5 2.7 fusion.11
  238.5 2.6 collective-permute-start.29
  242.0 5.0 collective-permute-start.12
  253.0 2.9 copy.117
  255.8 2.8 pad_maximum_fusion.2
  258.6 3.3 convolution_convert_fusion.4
  262.1 2.8 convolution_convert_fusion.3
  265.0 6.3 %convolution_convert_fusion = bf16[2048,2048]{1,0:T(8,128)(2,1)S(1)} fusion(bf16[2048,512]{1,0:T(8,128)(2,1)} %bitcast.286, bf16[512,2048]{1,0:T(8,128)(2,1)S(1)} %bitcast.264), kind=kOutput, calls=%fused_computation.1 | convolution fusion | flops 4299161600 | bytes 12582912 | tf_op jit(solution)/shard_map/dot_general | solution.py:145
  273.6 2.6 constant_dynamic-slice_fusion.6
  276.2 2.0 copy-done
  279.5 2.4 collective-permute-start.50
  285.7 3.0 collective-permute-start.53
  294.6 3.9 slice.459
  312.9 15.1 %collective-permute-done.13 = bf16[512,512]{1,0:T(8,128)(2,1)S(1)} collective-permute-done((bf16[512,512]{1,0:T(8,128)(2,1)S(1)}, bf16[512,512]{1,0:T(8,128)(2,1)S(1)}, u32[]{:S(2)}, u32[]{:S(2)}) %collective-permute-start.13) | collective-permute-done | bytes 524320 | tf_op jit(solution)/shard_map/ppermute | solution.py:34
  332.7 1.8 convolution_convert_fusion.2
  334.6 1.9 convolution_convert_fusion.1
  338.4 2.0 collective-permute-start.22
  341.3 11.6 %collective-permute-done.22 = bf16[256,1024]{1,0:T(8,128)(2,1)S(1)} collective-permute-done((bf16[256,1024]{1,0:T(8,128)(2,1)S(1)}, bf16[256,1024]{1,0:T(8,128)(2,1)S(1)}, u32[]{:S(2)}, u32[]{:S(2)}) %collective-permute-start.22) | collective-permute-done | bytes 524320 | tf_op jit(solution)/shard_map/ppermute | solution.py:34
  356.1 2.6 fusion.96
  360.3 2.2 copy.122
  364.3 2.7 collective-permute-start.33
  367.0 1.9 add_convert_fusion.1
  369.1 2.2 collective-permute-start.15
  372.1 2.0 collective-permute-start.17
  374.7 9.6 %collective-permute-done.15 = bf16[64,2048]{1,0:T(8,128)(2,1)S(1)} collective-permute-done((bf16[64,2048]{1,0:T(8,128)(2,1)S(1)}, bf16[64,2048]{1,0:T(8,128)(2,1)S(1)}, u32[]{:S(2)}, u32[]{:S(2)}) %collective-permute-start.15) | collective-permute-done | bytes 262176 | tf_op jit(solution)/shard_map/ppermute | solution.py:34
  384.3 2.2 collective-permute-start.36
  386.5 2.7 fusion.39
  389.2 4.4 collective-permute-done.36
  393.6 2.4 collective-permute-done.37
  396.2 2.5 collective-permute-start.40
  402.6 2.3 collective-permute-start.43
  412.9 2.3 bitcast_dynamic-update-slice_fusion.3
  415.2 3.2 collective-permute-start.23
  419.6 2.6 collective-permute-start.59
  423.6 2.2 copy.123
  425.7 5.4 add_convert_fusion
  433.8 2.0 collective-permute-start.3
  435.9 3.7 collective-permute-done.59
  439.6 2.2 copy.124
  441.8 11.2 %collective-permute-done.60 = bf16[256,1664]{1,0:T(8,128)(2,1)} collective-permute-done((bf16[256,1664]{1,0:T(8,128)(2,1)}, bf16[256,1664]{1,0:T(8,128)(2,1)}, u32[]{:S(2)}, u32[]{:S(2)}) %collective-permute-start.60) | collective-permute-done | bytes 852000 | tf_op jit(solution)/shard_map/ppermute | solution.py:34
  452.9 2.8 collective-permute-start.18
  455.7 2.2 copy.125
  459.6 4.6 collective-permute-done.1
  465.8 5.3 collective-permute-start.2
  471.2 1.9 collective-permute-start.4
  477.0 6.5 %collective-permute-done.19 = bf16[64,2048]{1,0:T(8,128)(2,1)S(1)} collective-permute-done((bf16[64,2048]{1,0:T(8,128)(2,1)S(1)}, bf16[64,2048]{1,0:T(8,128)(2,1)S(1)}, u32[]{:S(2)}, u32[]{:S(2)}) %collective-permute-start.19) | collective-permute-done | bytes 262176 | tf_op jit(solution)/shard_map/ppermute | solution.py:34
  484.3 2.2 collective-permute-done.2
  487.2 4.6 collective-permute-start.6
  491.9 2.1 fusion.6
  495.0 3.6 collective-permute-start.27
  499.0 2.3 collective-permute-done.7
  503.3 2.2 collective-permute-start.8
  507.2 4.2 collective-permute-start.28
  513.0 9.1 %collective-permute-done.9 = bf16[64,2048]{1,0:T(8,128)(2,1)S(1)} collective-permute-done((bf16[64,2048]{1,0:T(8,128)(2,1)S(1)}, bf16[64,2048]{1,0:T(8,128)(2,1)S(1)}, u32[]{:S(2)}, u32[]{:S(2)}) %collective-permute-start.9) | collective-permute-done | bytes 262176 | tf_op jit(solution)/shard_map/ppermute | solution.py:34
  522.8 3.9 collective-permute-done.10
  527.4 1.9 bitcast_convert_fusion
  529.4 2.9 copy.127
  532.3 1.8 copy.128
  538.7 5.0 maximum_select_fusion.1
  543.7 4.6 maximum_select_fusion
  (294 shorter events, 99.7 us)
Async XLA Ops:
  238.5 117.6 %collective-permute-start.29 = (bf16[2,256,1664]{2,1,0:T(8,128)(2,1)}, bf16[2,256,1664]{2,1,0:T(8,128)(2,1)}, u32[]{:S(2)}, u32[]{:S(2)}) collective-permute-start(bf16[2,256,1664]{2,1,0:T(8,128)(2,1)} %pad_maximum_fusion.1), channel_id=1, source_target_pairs={{0,32},{1,33},{2,34},{3,35},{4,36},{5,37},{6,38},{7,39},{8,40},{9,... | collective-permute-start | bytes 5111816 | tf_op jit(solution)/shard_map/ppermute | solution.py:34
  242.0 36.2 %collective-permute-start.48 = (f32[16,128]{1,0:T(8,128)S(1)}, f32[16,128]{1,0:T(8,128)S(1)}, u32[]{:S(2)}, u32[]{:S(2)}) collective-permute-start(f32[16,128]{1,0:T(8,128)S(1)} %bitcast.272), channel_id=1, source_target_pairs={{0,1},{1,0},{2,3},{3,2},{4,5},{5,4},{6,7},{7,6},{8,9},{9,8},{10,11... | collective-permute-start | bytes 24584 | tf_op jit(solution)/shard_map/ppermute | solution.py:34
  242.0 60.0 %collective-permute-start.12 = (bf16[512,512]{1,0:T(8,128)(2,1)}, bf16[512,512]{1,0:T(8,128)(2,1)}, u32[]{:S(2)}, u32[]{:S(2)}) collective-permute-start(bf16[512,512]{1,0:T(8,128)(2,1)} %get-tuple-element.82), channel_id=1, source_target_pairs={{0,8},{1,9},{2,10},{3,11},{4,12},{5,13},{6,14},{7,15},{16,24},{17,... | collective-permute-start | bytes 1572872 | tf_op jit(solution)/shard_map/ppermute | solution.py:34
  252.9 133.6 %copy-start.29 = (f32[64]{0:T(128)}, f32[64]{0:T(128)S(1)}, u32[]{:S(2)}) copy-start(f32[64]{0:T(128)S(1)} %slice_reduce_fusion.2) | copy-start | bytes 772
  278.2 4.9 collective-permute-start.49
  279.5 5.2 collective-permute-start.50
  281.9 3.7 collective-permute-start.51
  285.5 3.8 collective-permute-start.52
  285.7 5.2 collective-permute-start.53
  288.7 3.7 collective-permute-start.54
  292.3 7.6 %collective-permute-start.55 = (f32[16,128]{1,0:T(8,128)S(1)}, f32[16,128]{1,0:T(8,128)S(1)}, u32[]{:S(2)}, u32[]{:S(2)}) collective-permute-start(f32[16,128]{1,0:T(8,128)S(1)} %add_add_fusion.5), channel_id=1, source_target_pairs={{0,32},{1,33},{2,34},{3,35},{4,36},{5,37},{6,38},{7,39},{8,40},{9,... | collective-permute-start | bytes 24584 | tf_op jit(solution)/shard_map/ppermute | solution.py:34
  292.4 8.9 %collective-permute-start.56 = (f32[16,128]{1,0:T(8,128)S(1)}, f32[16,128]{1,0:T(8,128)S(1)}, u32[]{:S(2)}, u32[]{:S(2)}) collective-permute-start(f32[16,128]{1,0:T(8,128)S(1)} %add_add_fusion.5), channel_id=1, source_target_pairs={{0,64},{1,65},{2,66},{3,67},{4,68},{5,69},{6,70},{7,71},{8,72},{9,... | collective-permute-start | bytes 24584 | tf_op jit(solution)/shard_map/ppermute | solution.py:34
  293.9 7.5 %collective-permute-start.57 = (f32[16,128]{1,0:T(8,128)S(1)}, f32[16,128]{1,0:T(8,128)S(1)}, u32[]{:S(2)}, u32[]{:S(2)}) collective-permute-start(f32[16,128]{1,0:T(8,128)S(1)} %add_add_fusion.5), channel_id=1, source_target_pairs={{0,96},{1,97},{2,98},{3,99},{4,100},{5,101},{6,102},{7,103},{8,104... | collective-permute-start | bytes 24584 | tf_op jit(solution)/shard_map/ppermute | solution.py:34
  299.9 36.6 %copy-start.6 = (bf16[4,512,256]{2,1,0:T(8,128)(2,1)}, bf16[4,512,256]{2,1,0:T(8,128)(2,1)S(1)}, u32[]{:S(2)}) copy-start(bf16[4,512,256]{2,1,0:T(8,128)(2,1)S(1)} %copy.119) | copy-start | bytes 3145732
  300.0 56.2 %collective-permute-start.30 = (bf16[2,256,1664]{2,1,0:T(8,128)(2,1)}, bf16[2,256,1664]{2,1,0:T(8,128)(2,1)S(1)}, u32[]{:S(2)}, u32[]{:S(2)}) collective-permute-start(bf16[2,256,1664]{2,1,0:T(8,128)(2,1)} %pad_maximum_fusion.2), channel_id=1, source_target_pairs={{0,96},{1,97},{2,98},{3,99},{4,100},{5,101},{6,102},{7,103},{8,104... | collective-permute-start | bytes 5111816 | tf_op jit(solution)/shard_map/ppermute | solution.py:34
  301.3 124.4 %collective-permute-start = (bf16[4,256,2048]{2,1,0:T(8,128)(2,1)}, bf16[4,256,2048]{2,1,0:T(8,128)(2,1)}, u32[]{:S(2)}, u32[]{:S(2)}) collective-permute-start(bf16[4,256,2048]{2,1,0:T(8,128)(2,1)} %constant_dynamic-slice_fusion.6), channel_id=1, source_target_pairs={{0,1},{1,0},{2,3},{3,2},{4,5},{5,4},{6,7},{7,6},{8,9},{9,8},{10,11... | collective-permute-start | bytes 12582920 | tf_op jit(solution)/shard_map/ppermute | solution.py:34
  310.3 17.7 %collective-permute-start.13 = (bf16[512,512]{1,0:T(8,128)(2,1)S(1)}, bf16[512,512]{1,0:T(8,128)(2,1)S(1)}, u32[]{:S(2)}, u32[]{:S(2)}) collective-permute-start(bf16[512,512]{1,0:T(8,128)(2,1)S(1)} %slice.609), channel_id=1, source_target_pairs={{8,0},{9,1},{10,2},{11,3},{12,4},{13,5},{14,6},{15,7},{24,16},{25,... | collective-permute-start | bytes 1572872 | tf_op jit(solution)/shard_map/ppermute | solution.py:34
  338.4 14.4 %collective-permute-start.22 = (bf16[256,1024]{1,0:T(8,128)(2,1)S(1)}, bf16[256,1024]{1,0:T(8,128)(2,1)S(1)}, u32[]{:S(2)}, u32[]{:S(2)}) collective-permute-start(bf16[256,1024]{1,0:T(8,128)(2,1)S(1)} %get-tuple-element.210), channel_id=1, source_target_pairs={{0,32},{1,33},{2,34},{3,35},{4,36},{5,37},{6,38},{7,39},{8,40},{9,... | collective-permute-start | bytes 1572872 | tf_op jit(solution)/shard_map/ppermute | solution.py:34
  340.4 14.5 %collective-permute-start.24 = (bf16[256,1024]{1,0:T(8,128)(2,1)S(1)}, bf16[256,1024]{1,0:T(8,128)(2,1)S(1)}, u32[]{:S(2)}, u32[]{:S(2)}) collective-permute-start(bf16[256,1024]{1,0:T(8,128)(2,1)S(1)} %get-tuple-element.211), channel_id=1, source_target_pairs={{0,96},{1,97},{2,98},{3,99},{4,100},{5,101},{6,102},{7,103},{8,104... | collective-permute-start | bytes 1572872 | tf_op jit(solution)/shard_map/ppermute | solution.py:34
  352.8 14.2 %collective-permute-start.14 = (bf16[256,2048]{1,0:T(8,128)(2,1)S(1)}, bf16[256,2048]{1,0:T(8,128)(2,1)}, u32[]{:S(2)}, u32[]{:S(2)}) collective-permute-start(bf16[256,2048]{1,0:T(8,128)(2,1)S(1)} %constant_dynamic-slice_fusion.4), channel_id=1, source_target_pairs={{0,1},{1,0},{2,3},{3,2},{4,5},{5,4},{6,7},{7,6},{8,9},{9,8},{10,11... | collective-permute-start | bytes 3145736 | tf_op jit(solution)/shard_map/ppermute | solution.py:34
  358.9 3.6 collective-permute-start.31
  362.5 8.8 %collective-permute-start.32 = (f32[64,128]{1,0:T(8,128)S(1)}, f32[64,128]{1,0:T(8,128)S(1)}, u32[]{:S(2)}, u32[]{:S(2)}) collective-permute-start(f32[64,128]{1,0:T(8,128)S(1)} %add.547), channel_id=1, source_target_pairs={{0,2},{1,3},{2,4},{3,5},{4,6},{5,7},{6,0},{7,1},{8,10},{9,11},{10,... | collective-permute-start | bytes 98312 | tf_op jit(solution)/shard_map/ppermute | solution.py:34
  364.3 7.8 %collective-permute-start.33 = (f32[64,128]{1,0:T(8,128)S(1)}, f32[64,128]{1,0:T(8,128)S(1)}, u32[]{:S(2)}, u32[]{:S(2)}) collective-permute-start(f32[64,128]{1,0:T(8,128)S(1)} %add.547), channel_id=1, source_target_pairs={{0,4},{1,5},{2,6},{3,7},{4,0},{5,1},{6,2},{7,3},{8,12},{9,13},{10,... | collective-permute-start | bytes 98312 | tf_op jit(solution)/shard_map/ppermute | solution.py:34
  367.0 7.4 %collective-permute-start.34 = (f32[64,128]{1,0:T(8,128)S(1)}, f32[64,128]{1,0:T(8,128)S(1)}, u32[]{:S(2)}, u32[]{:S(2)}) collective-permute-start(f32[64,128]{1,0:T(8,128)S(1)} %add.547), channel_id=1, source_target_pairs={{0,6},{1,7},{2,0},{3,1},{4,2},{5,3},{6,4},{7,5},{8,14},{9,15},{10,... | collective-permute-start | bytes 98312 | tf_op jit(solution)/shard_map/ppermute | solution.py:34
  369.1 15.2 %collective-permute-start.15 = (bf16[64,2048]{1,0:T(8,128)(2,1)S(1)}, bf16[64,2048]{1,0:T(8,128)(2,1)S(1)}, u32[]{:S(2)}, u32[]{:S(2)}) collective-permute-start(bf16[64,2048]{1,0:T(8,128)(2,1)S(1)} %get-tuple-element.212), channel_id=1, source_target_pairs={{0,2},{1,3},{2,4},{3,5},{4,6},{5,7},{6,0},{7,1},{8,10},{9,11},{10,... | collective-permute-start | bytes 786440 | tf_op jit(solution)/shard_map/ppermute | solution.py:34
  371.3 13.0 %collective-permute-start.16 = (bf16[64,2048]{1,0:T(8,128)(2,1)S(1)}, bf16[64,2048]{1,0:T(8,128)(2,1)S(1)}, u32[]{:S(2)}, u32[]{:S(2)}) collective-permute-start(bf16[64,2048]{1,0:T(8,128)(2,1)S(1)} %get-tuple-element.214), channel_id=1, source_target_pairs={{0,4},{1,5},{2,6},{3,7},{4,0},{5,1},{6,2},{7,3},{8,12},{9,13},{10,... | collective-permute-start | bytes 786440 | tf_op jit(solution)/shard_map/ppermute | solution.py:34
  372.1 14.4 %collective-permute-start.17 = (bf16[64,2048]{1,0:T(8,128)(2,1)S(1)}, bf16[64,2048]{1,0:T(8,128)(2,1)S(1)}, u32[]{:S(2)}, u32[]{:S(2)}) collective-permute-start(bf16[64,2048]{1,0:T(8,128)(2,1)S(1)} %get-tuple-element.213), channel_id=1, source_target_pairs={{0,6},{1,7},{2,0},{3,1},{4,2},{5,3},{6,4},{7,5},{8,14},{9,15},{10,... | collective-permute-start | bytes 786440 | tf_op jit(solution)/shard_map/ppermute | solution.py:34
  374.4 49.2 %collective-permute-start.58 = (bf16[256,1664]{1,0:T(8,128)(2,1)}, bf16[256,1664]{1,0:T(8,128)(2,1)}, u32[]{:S(2)}, u32[]{:S(2)}) collective-permute-start(bf16[256,1664]{1,0:T(8,128)(2,1)} %get-tuple-element.202), channel_id=1, source_target_pairs={{0,24},{1,25},{2,26},{3,27},{4,28},{5,29},{6,30},{7,31},{8,16},{9,... | collective-permute-start | bytes 2555912 | tf_op jit(solution)/shard_map/ppermute | solution.py:34
  384.3 4.9 collective-permute-start.35
  384.3 9.3 %collective-permute-start.36 = (f32[64,128]{1,0:T(8,128)S(1)}, f32[64,128]{1,0:T(8,128)S(1)}, u32[]{:S(2)}, u32[]{:S(2)}) collective-permute-start(f32[64,128]{1,0:T(8,128)S(1)} %add_add_fusion.1), channel_id=1, source_target_pairs={{0,8},{1,9},{2,10},{3,11},{4,12},{5,13},{6,14},{7,15},{8,0},{9,1},... | collective-permute-start | bytes 98312 | tf_op jit(solution)/shard_map/ppermute | solution.py:34
  386.5 9.5 %collective-permute-start.37 = (f32[64,128]{1,0:T(8,128)S(1)}, f32[64,128]{1,0:T(8,128)S(1)}, u32[]{:S(2)}, u32[]{:S(2)}) collective-permute-start(f32[64,128]{1,0:T(8,128)S(1)} %add_add_fusion.1), channel_id=1, source_target_pairs={{0,24},{1,25},{2,26},{3,27},{4,28},{5,29},{6,30},{7,31},{8,16},{9,... | collective-permute-start | bytes 98312 | tf_op jit(solution)/shard_map/ppermute | solution.py:34
  389.2 6.9 %collective-permute-start.38 = (f32[48,128]{1,0:T(8,128)S(1)}, f32[48,128]{1,0:T(8,128)S(1)}, u32[]{:S(2)}, u32[]{:S(2)}) collective-permute-start(f32[48,128]{1,0:T(8,128)S(1)} %maximum_bitcast_fusion.1), channel_id=1, source_target_pairs={{0,1},{1,0},{2,3},{3,2},{4,5},{5,4},{6,7},{7,6},{8,9},{9,8},{10,11... | collective-permute-start | bytes 73736 | tf_op jit(solution)/shard_map/ppermute | solution.py:34
  396.1 5.1 collective-permute-start.39
  396.2 5.4 collective-permute-start.40
  398.7 3.8 collective-permute-start.41
  402.5 4.8 collective-permute-start.42
  402.6 5.4 collective-permute-start.43
  404.9 3.8 collective-permute-start.44
  408.8 6.5 %collective-permute-start.45 = (f32[48,128]{1,0:T(8,128)S(1)}, f32[48,128]{1,0:T(8,128)S(1)}, u32[]{:S(2)}, u32[]{:S(2)}) collective-permute-start(f32[48,128]{1,0:T(8,128)S(1)} %add_add_fusion.3), channel_id=1, source_target_pairs={{0,32},{1,33},{2,34},{3,35},{4,36},{5,37},{6,38},{7,39},{8,40},{9,... | collective-permute-start | bytes 73736 | tf_op jit(solution)/shard_map/ppermute | solution.py:34
  410.4 8.1 %collective-permute-start.46 = (f32[48,128]{1,0:T(8,128)S(1)}, f32[48,128]{1,0:T(8,128)S(1)}, u32[]{:S(2)}, u32[]{:S(2)}) collective-permute-start(f32[48,128]{1,0:T(8,128)S(1)} %add_add_fusion.3), channel_id=1, source_target_pairs={{0,64},{1,65},{2,66},{3,67},{4,68},{5,69},{6,70},{7,71},{8,72},{9,... | collective-permute-start | bytes 73736 | tf_op jit(solution)/shard_map/ppermute | solution.py:34
  411.9 7.8 %collective-permute-start.47 = (f32[48,128]{1,0:T(8,128)S(1)}, f32[48,128]{1,0:T(8,128)S(1)}, u32[]{:S(2)}, u32[]{:S(2)}) collective-permute-start(f32[48,128]{1,0:T(8,128)S(1)} %add_add_fusion.3), channel_id=1, source_target_pairs={{0,96},{1,97},{2,98},{3,99},{4,100},{5,101},{6,102},{7,103},{8,104... | collective-permute-start | bytes 73736 | tf_op jit(solution)/shard_map/ppermute | solution.py:34
  415.2 76.6 %collective-permute-start.23 = (bf16[512,1024]{1,0:T(8,128)(2,1)}, bf16[512,1024]{1,0:T(8,128)(2,1)}, u32[]{:S(2)}, u32[]{:S(2)}) collective-permute-start(bf16[512,1024]{1,0:T(8,128)(2,1)} %pad_maximum_fusion.5), channel_id=1, source_target_pairs={{0,32},{1,33},{2,34},{3,35},{4,36},{5,37},{6,38},{7,39},{8,40},{9,... | collective-permute-start | bytes 3145736 | tf_op jit(solution)/shard_map/ppermute | solution.py:34
  418.4 34.5 %collective-permute-start.60 = (bf16[256,1664]{1,0:T(8,128)(2,1)}, bf16[256,1664]{1,0:T(8,128)(2,1)}, u32[]{:S(2)}, u32[]{:S(2)}) collective-permute-start(bf16[256,1664]{1,0:T(8,128)(2,1)} %get-tuple-element.202), channel_id=1, source_target_pairs={{0,16},{1,17},{2,18},{3,19},{4,20},{5,21},{6,22},{7,23},{8,24},{9,... | collective-permute-start | bytes 2555912 | tf_op jit(solution)/shard_map/ppermute | solution.py:34
  419.6 20.0 %collective-permute-start.59 = (bf16[256,1664]{1,0:T(8,128)(2,1)}, bf16[256,1664]{1,0:T(8,128)(2,1)}, u32[]{:S(2)}, u32[]{:S(2)}) collective-permute-start(bf16[256,1664]{1,0:T(8,128)(2,1)} %bitcast.98), channel_id=1, source_target_pairs={{0,8},{1,9},{2,10},{3,11},{4,12},{5,13},{6,14},{7,15},{8,0},{9,1},... | collective-permute-start | bytes 2555912 | tf_op jit(solution)/shard_map/ppermute | solution.py:34
  433.8 30.4 %collective-permute-start.1 = (bf16[128,2048]{1,0:T(8,128)(2,1)}, bf16[128,2048]{1,0:T(8,128)(2,1)}, u32[]{:S(2)}, u32[]{:S(2)}) collective-permute-start(bf16[128,2048]{1,0:T(8,128)(2,1)} %get-tuple-element.194), channel_id=1, source_target_pairs={{0,16},{1,17},{2,18},{3,19},{4,20},{5,21},{6,22},{7,23},{8,24},{9,... | collective-permute-start | bytes 1572872 | tf_op jit(solution)/shard_map/ppermute | solution.py:34
  433.8 30.4 %collective-permute-start.3 = (bf16[128,2048]{1,0:T(8,128)(2,1)}, bf16[128,2048]{1,0:T(8,128)(2,1)}, u32[]{:S(2)}, u32[]{:S(2)}) collective-permute-start(bf16[128,2048]{1,0:T(8,128)(2,1)} %get-tuple-element.196), channel_id=1, source_target_pairs={{0,24},{1,25},{2,26},{3,27},{4,28},{5,29},{6,30},{7,31},{8,16},{9,... | collective-permute-start | bytes 1572872 | tf_op jit(solution)/shard_map/ppermute | solution.py:34
  439.6 52.3 %collective-permute-start.25 = (bf16[512,1024]{1,0:T(8,128)(2,1)}, bf16[512,1024]{1,0:T(8,128)(2,1)}, u32[]{:S(2)}, u32[]{:S(2)}) collective-permute-start(bf16[512,1024]{1,0:T(8,128)(2,1)} %pad_maximum_fusion.6), channel_id=1, source_target_pairs={{0,96},{1,97},{2,98},{3,99},{4,100},{5,101},{6,102},{7,103},{8,104... | collective-permute-start | bytes 3145736 | tf_op jit(solution)/shard_map/ppermute | solution.py:34
  452.9 21.5 %collective-permute-start.18 = (bf16[64,2048]{1,0:T(8,128)(2,1)}, bf16[64,2048]{1,0:T(8,128)(2,1)}, u32[]{:S(2)}, u32[]{:S(2)}) collective-permute-start(bf16[64,2048]{1,0:T(8,128)(2,1)} %get-tuple-element.181), channel_id=1, source_target_pairs={{0,6},{1,7},{2,0},{3,1},{4,2},{5,3},{6,4},{7,5},{8,14},{9,15},{10,... | collective-permute-start | bytes 786440 | tf_op jit(solution)/shard_map/ppermute | solution.py:34
  459.6 11.6 %copy-start.16 = (bf16[128,2048]{1,0:T(8,128)(2,1)S(1)}, bf16[128,2048]{1,0:T(8,128)(2,1)}, u32[]{:S(2)}) copy-start(bf16[128,2048]{1,0:T(8,128)(2,1)} %get-tuple-element.195) | copy-start | bytes 1572868
  465.8 20.7 %collective-permute-start.2 = (bf16[256,2048]{1,0:T(8,128)(2,1)S(1)}, bf16[256,2048]{1,0:T(8,128)(2,1)S(1)}, u32[]{:S(2)}, u32[]{:S(2)}) collective-permute-start(bf16[256,2048]{1,0:T(8,128)(2,1)S(1)} %pad_maximum_fusion.3), channel_id=1, source_target_pairs={{0,16},{1,17},{2,18},{3,19},{4,20},{5,21},{6,22},{7,23},{8,24},{9,... | collective-permute-start | bytes 3145736 | tf_op jit(solution)/shard_map/ppermute | solution.py:34
  471.2 15.3 %collective-permute-start.4 = (bf16[256,2048]{1,0:T(8,128)(2,1)S(1)}, bf16[256,2048]{1,0:T(8,128)(2,1)S(1)}, u32[]{:S(2)}, u32[]{:S(2)}) collective-permute-start(bf16[256,2048]{1,0:T(8,128)(2,1)S(1)} %pad_maximum_fusion.4), channel_id=1, source_target_pairs={{0,24},{1,25},{2,26},{3,27},{4,28},{5,29},{6,30},{7,31},{8,16},{9,... | collective-permute-start | bytes 3145736 | tf_op jit(solution)/shard_map/ppermute | solution.py:34
  474.5 9.1 %collective-permute-start.19 = (bf16[64,2048]{1,0:T(8,128)(2,1)S(1)}, bf16[64,2048]{1,0:T(8,128)(2,1)S(1)}, u32[]{:S(2)}, u32[]{:S(2)}) collective-permute-start(bf16[64,2048]{1,0:T(8,128)(2,1)S(1)} %copy-done.23), channel_id=1, source_target_pairs={{0,4},{1,5},{2,6},{3,7},{4,0},{5,1},{6,2},{7,3},{8,12},{9,13},{10,... | collective-permute-start | bytes 786440 | tf_op jit(solution)/shard_map/ppermute | solution.py:34
  483.5 22.0 %collective-permute-start.20 = (bf16[64,2048]{1,0:T(8,128)(2,1)S(1)}, bf16[64,2048]{1,0:T(8,128)(2,1)S(1)}, u32[]{:S(2)}, u32[]{:S(2)}) collective-permute-start(bf16[64,2048]{1,0:T(8,128)(2,1)S(1)} %copy-done.23), channel_id=1, source_target_pairs={{0,2},{1,3},{2,4},{3,5},{4,6},{5,7},{6,0},{7,1},{8,10},{9,11},{10,... | collective-permute-start | bytes 786440 | tf_op jit(solution)/shard_map/ppermute | solution.py:34
  487.1 7.8 %collective-permute-start.5 = (bf16[64,2048]{1,0:T(8,128)(2,1)S(1)}, bf16[64,2048]{1,0:T(8,128)(2,1)S(1)}, u32[]{:S(2)}, u32[]{:S(2)}) collective-permute-start(bf16[64,2048]{1,0:T(8,128)(2,1)S(1)} %get-tuple-element.217), channel_id=1, source_target_pairs={{0,2},{1,3},{2,4},{3,5},{4,6},{5,7},{6,0},{7,1},{8,10},{9,11},{10,... | collective-permute-start | bytes 786440 | tf_op jit(solution)/shard_map/ppermute | solution.py:34
  487.2 11.8 %collective-permute-start.6 = (bf16[64,2048]{1,0:T(8,128)(2,1)S(1)}, bf16[64,2048]{1,0:T(8,128)(2,1)S(1)}, u32[]{:S(2)}, u32[]{:S(2)}) collective-permute-start(bf16[64,2048]{1,0:T(8,128)(2,1)S(1)} %get-tuple-element.219), channel_id=1, source_target_pairs={{0,4},{1,5},{2,6},{3,7},{4,0},{5,1},{6,2},{7,3},{8,12},{9,13},{10,... | collective-permute-start | bytes 786440 | tf_op jit(solution)/shard_map/ppermute | solution.py:34
  491.9 9.4 %collective-permute-start.7 = (bf16[64,2048]{1,0:T(8,128)(2,1)S(1)}, bf16[64,2048]{1,0:T(8,128)(2,1)S(1)}, u32[]{:S(2)}, u32[]{:S(2)}) collective-permute-start(bf16[64,2048]{1,0:T(8,128)(2,1)S(1)} %get-tuple-element.218), channel_id=1, source_target_pairs={{0,6},{1,7},{2,0},{3,1},{4,2},{5,3},{6,4},{7,5},{8,14},{9,15},{10,... | collective-permute-start | bytes 786440 | tf_op jit(solution)/shard_map/ppermute | solution.py:34
  494.0 12.2 %collective-permute-start.26 = (bf16[128,1024]{1,0:T(8,128)(2,1)S(1)}, bf16[128,1024]{1,0:T(8,128)(2,1)S(1)}, u32[]{:S(2)}, u32[]{:S(2)}) collective-permute-start(bf16[128,1024]{1,0:T(8,128)(2,1)S(1)} %get-tuple-element.208), channel_id=1, source_target_pairs={{0,16},{1,17},{2,18},{3,19},{4,20},{5,21},{6,22},{7,23},{8,24},{9,... | collective-permute-start | bytes 786440 | tf_op jit(solution)/shard_map/ppermute | solution.py:34
  495.0 11.2 %collective-permute-start.27 = (bf16[128,1024]{1,0:T(8,128)(2,1)S(1)}, bf16[128,1024]{1,0:T(8,128)(2,1)S(1)}, u32[]{:S(2)}, u32[]{:S(2)}) collective-permute-start(bf16[128,1024]{1,0:T(8,128)(2,1)S(1)} %get-tuple-element.209), channel_id=1, source_target_pairs={{0,24},{1,25},{2,26},{3,27},{4,28},{5,29},{6,30},{7,31},{8,16},{9,... | collective-permute-start | bytes 786440 | tf_op jit(solution)/shard_map/ppermute | solution.py:34
  503.3 9.0 %collective-permute-start.8 = (bf16[64,2048]{1,0:T(8,128)(2,1)S(1)}, bf16[64,2048]{1,0:T(8,128)(2,1)S(1)}, u32[]{:S(2)}, u32[]{:S(2)}) collective-permute-start(bf16[64,2048]{1,0:T(8,128)(2,1)S(1)} %get-tuple-element.184), channel_id=1, source_target_pairs={{0,6},{1,7},{2,0},{3,1},{4,2},{5,3},{6,4},{7,5},{8,14},{9,15},{10,... | collective-permute-start | bytes 786440 | tf_op jit(solution)/shard_map/ppermute | solution.py:34
  506.2 32.5 %collective-permute-start.21 = (bf16[256,2048]{1,0:T(8,128)(2,1)}, bf16[256,2048]{1,0:T(8,128)(2,1)}, u32[]{:S(2)}, u32[]{:S(2)}) collective-permute-start(bf16[256,2048]{1,0:T(8,128)(2,1)} %bitcast.55), channel_id=1, source_target_pairs={{0,1},{1,0},{2,3},{3,2},{4,5},{5,4},{6,7},{7,6},{8,9},{9,8},{10,11... | collective-permute-start | bytes 3145736 | tf_op jit(solution)/shard_map/ppermute | solution.py:34
  507.2 28.4 %collective-permute-start.28 = (bf16[256,1024]{1,0:T(8,128)(2,1)}, bf16[256,1024]{1,0:T(8,128)(2,1)}, u32[]{:S(2)}, u32[]{:S(2)}) collective-permute-start(bf16[256,1024]{1,0:T(8,128)(2,1)} %fusion.22), channel_id=1, source_target_pairs={{0,8},{1,9},{2,10},{3,11},{4,12},{5,13},{6,14},{7,15},{8,0},{9,1},... | collective-permute-start | bytes 1572872 | tf_op jit(solution)/shard_map/ppermute | solution.py:34
  511.4 10.7 %collective-permute-start.9 = (bf16[64,2048]{1,0:T(8,128)(2,1)S(1)}, bf16[64,2048]{1,0:T(8,128)(2,1)S(1)}, u32[]{:S(2)}, u32[]{:S(2)}) collective-permute-start(bf16[64,2048]{1,0:T(8,128)(2,1)S(1)} %get-tuple-element.184), channel_id=1, source_target_pairs={{0,4},{1,5},{2,6},{3,7},{4,0},{5,1},{6,2},{7,3},{8,12},{9,13},{10,... | collective-permute-start | bytes 786440 | tf_op jit(solution)/shard_map/ppermute | solution.py:34
  511.4 15.3 %collective-permute-start.10 = (bf16[64,2048]{1,0:T(8,128)(2,1)S(1)}, bf16[64,2048]{1,0:T(8,128)(2,1)S(1)}, u32[]{:S(2)}, u32[]{:S(2)}) collective-permute-start(bf16[64,2048]{1,0:T(8,128)(2,1)S(1)} %get-tuple-element.184), channel_id=1, source_target_pairs={{0,2},{1,3},{2,4},{3,5},{4,6},{5,7},{6,0},{7,1},{8,10},{9,11},{10,... | collective-permute-start | bytes 786440 | tf_op jit(solution)/shard_map/ppermute | solution.py:34
  527.4 16.3 %collective-permute-start.11 = (bf16[256,2048]{1,0:T(8,128)(2,1)}, bf16[256,2048]{1,0:T(8,128)(2,1)}, u32[]{:S(2)}, u32[]{:S(2)}) collective-permute-start(bf16[256,2048]{1,0:T(8,128)(2,1)} %bitcast.28), channel_id=1, source_target_pairs={{0,1},{1,0},{2,3},{3,2},{4,5},{5,4},{6,7},{7,6},{8,9},{9,8},{10,11... | collective-permute-start | bytes 3145736 | tf_op jit(solution)/shard_map/ppermute | solution.py:34
  (28 other events, 122.3 us)

commit v4 on v3

--- a/solution.py
+++ b/solution.py
@@ -13,102 +13,6 @@
 BF = jnp.bfloat16
 F32 = jnp.float32
 
-
-def place_of(index):
-    shard, rest = divmod(index, 16)
-    ctx, tp = divmod(rest, 8)
-    return shard // 2, ctx * 2 + shard % 2, tp // 2, tp % 2
-
-
-def index_of(x, y, z, c):
-    x, y, z, c = x % 4, y % 4, z % 4, c % 2
-    return (x * 2 + y % 2) * 16 + (y // 2) * 8 + z * 2 + c
-
-
-def hop(value, dx=0, dy=0, dz=0, dc=0, only=None):
-    pairs = []
-    for index in range(128):
-        x, y, z, c = place_of(index)
-        if only is None or only(x, y, z, c):
-            pairs.append((index, index_of(x + dx, y + dy, z + dz, c + dc)))
-    return lax.ppermute(value, AXES, pairs)
-
-
-def step_of(axis, amount):
-    return {"d" + axis: amount}
-
-
-def halves(value):
-    middle = value.shape[0] // 2
-    return value[:middle], value[middle:]
-
-
-def ring_gather(block, axis):
-    from_before = hop(block, **step_of(axis, 1))
-    from_after = hop(block, **step_of(axis, -1))
-    first = hop(halves(from_before)[0], **step_of(axis, 1))
-    second = hop(halves(from_after)[1], **step_of(axis, -1))
-    return [block, from_after, jnp.concatenate([first, second], axis=0), from_before]
-
-
-def direct_gather(block, axis):
-    return [
-        block,
-        hop(block, **step_of(axis, -1)),
-        hop(block, **step_of(axis, 2)),
-        hop(block, **step_of(axis, 1)),
-    ]
-
-
-def in_order(blocks, start):
-    whole = jnp.zeros((4,) + blocks[0].shape, blocks[0].dtype)
-    for distance, block in enumerate(blocks):
-        whole = lax.dynamic_update_index_in_dim(whole, block, (start + distance) % 4, 0)
-    return whole
-
-
-def by_distance(whole, start):
-    return [
-        lax.dynamic_index_in_dim(whole, (start + distance) % 4, 0, keepdims=False)
-        for distance in range(4)
-    ]
-
-
-def added(*values):
-    total = values[0].astype(F32)
-    for value in values[1:]:
-        total = total + value.astype(F32)
-    return total
-
-
-def ring_scatter(chunks, axis):
-    far_first, far_second = halves(chunks[2])
-    got_first = hop(far_first, **step_of(axis, 1))
-    got_second = hop(far_second, **step_of(axis, -1))
-    after_first, after_second = halves(chunks[1])
-    before_first, before_second = halves(chunks[3])
-    to_after = jnp.concatenate([added(after_first, got_first).astype(BF), after_second], axis=0)
-    to_before = jnp.concatenate([before_first, added(before_second, got_second).astype(BF)], axis=0)
-    from_before = hop(to_after, **step_of(axis, 1))
-    from_after = hop(to_before, **step_of(axis, -1))
-    return added(chunks[0], from_before, from_after)
-
-
-def direct_scatter(chunks, axis):
-    return added(
-        chunks[0],
-        hop(chunks[1], **step_of(axis, 1)),
-        hop(chunks[2], **step_of(axis, 2)),
-        hop(chunks[3], **step_of(axis, -1)),
-    )
-
-
-def with_partner(own, other, number):
-    return jnp.where(
-        number == 0, jnp.concatenate([own, other], 0), jnp.concatenate([other, own], 0)
-    )
-
-
 def rms_scale(values):
     return lax.rsqrt(jnp.mean(values * values, axis=-1, keepdims=True) + EPSILON)
 
@@ -122,25 +26,6 @@
     return (grad_source, grad_normed * unit_values)
 
 
-def rope_tables(positions, head_width):
-    frequency = ROPE_BASE ** (-(jnp.arange(0, head_width, 2, dtype=F32) / head_width))
-    angles = positions.astype(F32)[:, None] * frequency[None, :]
-    return (jnp.cos(angles), jnp.sin(angles))
-
-
-def rotate(values, cosine, sine_table):
-    half_width = values.shape[-1] // 2
-    first_half = values[..., :half_width]
-    second_half = values[..., half_width:]
-    return jnp.concatenate(
-        [
-            first_half * cosine - second_half * sine_table,
-            second_half * cosine + first_half * sine_table,
-        ],
-        axis=-1,
-    )
-
-
 def dot(left, right):
     return jnp.dot(left, right, preferred_element_type=F32)
 
@@ -170,14 +55,19 @@
     return {"shard": x * 2 + lax.rem(y, 2), "ctx": y // 2, "tp": z * 2 + c}
 
 
+def at(first, size):
+    return pl.ds(pl.multiple_of(first, size), size)
+
+
 class Links:
     def __init__(self, send_sems, recv_sems):
         self.here = places()
-        self.send_sems, self.recv_sems, self.made = send_sems, recv_sems, []
+        self.send_sems, self.recv_sems, self.made, self.count = send_sems, recv_sems, [], 0
 
     def send(self, source, target, dx=0, dy=0, dz=0, dc=0, start=True):
         x, y, z, c = self.here
-        number = len(self.made)
+        number = self.count
+        self.count += 1
         copy = pltpu.make_async_remote_copy(
             src_ref=source,
             dst_ref=target,
@@ -190,6 +80,10 @@
         if start:
             copy.start()
         return copy
+
+    def left(self, copy):
+        copy.wait_send()
+        self.made = [other for other in self.made if other is not copy]
 
     def finish(self):
         for copy in self.made:
@@ -270,11 +164,23 @@
     return sibling
 
 
+def own_mask(segment_rows, segment_row, own_first):
+    rows_at = lax.broadcasted_iota(jnp.int32, (ROWS, ROWS), 0)
+    cols_at = lax.broadcasted_iota(jnp.int32, (ROWS, ROWS), 1)
+    same = segment_rows[own_first, :] == segment_row[:, own_first]
+    return jnp.where(same & (rows_at >= cols_at), 0.0, MASKED_SCORE)
+
+
+def earlier_mask(segment_rows, segment_row, own_first):
+    same = segment_rows[own_first, :] == segment_row[:, pl.ds(0, ROWS)]
+    return jnp.where(same, 0.0, MASKED_SCORE)
+
+
 def front(
     tok, own_weights, cosine_ref, sine_ref, segment_rows, segment_row, gate, up, down, grad, picked,
     weights_out, experts_in, experts_out, grad_all, picked_all, moe_in_all,
-    normed_out, pre_out, rot_out, kv_out, mixed_out, lse_out, hidden_out, home_scale_out,
-    weights, kv_far, biases, accs, part, part_core, part_z, home_ref,
+    normed_out, pre_out, rot_out, kv_out, kv_far, mixed_out, lse_out, hidden_out, home_scale_out,
+    weights, biases, accs, part, part_core, part_z, home_ref,
     send_sems, recv_sems, local_sems,
 ):
     links = Links(send_sems, recv_sems)
@@ -341,13 +247,9 @@
     ]
     picked_near = [links.send(picked, picked_all.at[y], dy=d) for d in (1, -1, 2)]
 
-    rows_at = lax.broadcasted_iota(jnp.int32, (ROWS, ROWS), 0)
-    cols_at = lax.broadcasted_iota(jnp.int32, (ROWS, ROWS), 1)
-    own_first = pl.ds(pl.multiple_of(ctx * ROWS, ROWS), ROWS)
-    same = segment_rows[own_first, :] == segment_row[:, own_first]
-    biases[0] = jnp.where(same & (rows_at >= cols_at), 0.0, MASKED_SCORE)
-    earlier = segment_rows[own_first, :] == segment_row[:, pl.ds(0, ROWS)]
-    biases[1] = jnp.where(earlier, 0.0, MASKED_SCORE)
+    own_first = at(ctx * ROWS, ROWS)
+    biases[0] = own_mask(segment_rows, segment_row, own_first)
+    biases[1] = earlier_mask(segment_rows, segment_row, own_first)
     tokens = tok[...].astype(F32)
     scale_one = rms_scale(tokens)
 
@@ -398,6 +300,7 @@
     @pl.when(ctx == 0)
     def _():
         later.start()
+        kv_far[...] = jnp.zeros_like(kv_far)
 
     query_pre = project(0)
     pre_out[:, 0:256] = query_pre
@@ -522,6 +425,7 @@
         (shape((ROWS, 512), F32), VMEM),
         (shape((ROWS, 512), BF), VMEM),
         (shape((ROWS, 512), BF), VMEM),
+        (shape((ROWS, 512), BF), VMEM),
         (shape((ROWS, 256), BF), VMEM),
         (shape((4, ROWS, 128), F32), VMEM),
         (shape((HOME, WIDTH), F32), VMEM),
@@ -534,7 +438,6 @@
         out_specs=[spec for _, spec in outs],
         scratch_shapes=[
             pltpu.VMEM((4, 2, WROWS, WCOLS), BF),
-            pltpu.VMEM((ROWS, 512), BF),
             pltpu.VMEM((2, ROWS, ROWS), F32),
             pltpu.VMEM((2, ROWS, 128), F32),
             pltpu.VMEM((2, HALF, WIDTH), BF),
@@ -567,10 +470,6 @@
 MCOLS = 1664
 
 
-def at(first, size):
-    return pl.ds(pl.multiple_of(first, size), size)
-
-
 def scatter_buffers():
     return [
         pltpu.VMEM((4, HALF, WIDTH), BF),
@@ -588,8 +487,16 @@
         self.core_in, self.p_one_in, self.p_two_in, self.p_three_in, self.q_one_in, self.q_two_in = landings
         self.core, self.p_one, self.p_two, self.q_one, self.q_two = {}, [], [], {}, []
 
+    def give_slot(self, k):
+        slots = self.give.shape[0]
+        if k >= slots:
+            self.links.left(self.core[k - slots])
+        return k % slots
+
     def give_core(self, k):
-        self.core[k] = self.links.send(self.give.at[k], self.core_in.at[k], dc=1)
+        self.core[k] = self.links.send(
+            self.give.at[k % self.give.shape[0]], self.core_in.at[k], dc=1
+        )
 
     def q_part(self, k, place):
         return self.keep.at[k, at(place * HOME + 32, 32)]
@@ -885,6 +792,445 @@
     )
 
 
+SMALL = 264
+
+
+def back(
+    grad_moe, grad_near, low_hbm, weights, mixed_hbm, rot_hbm, kv_hbm, kv_far_hbm, lse_hbm, pre_hbm,
+    normed_hbm, gated_hbm, w_out_hbm, tok_hbm,
+    hidden_ref, hidden_grad_ref, home_scale_ref, gain_ref, cosine_ref, sine_ref, segment_rows, segment_row,
+    layer_all, input_all, groups_in, groups_out, moe_in,
+    grad_q, grad_k, grad_v, grad_o, small_out, heads_out,
+    w_ref, w_gains, low, mixed, rot, kv, kv_far, lse, pre, gated, w_out, home_tok,
+    bias, mixed_grad, dq, dkv, kv_give, kv_got, stacked,
+    moe_after, moe_before, moe_near, pay_in, pay_out,
+    attn_grad, attn_one, attn_two, attn_give, attn_keep, attn_y_one, attn_y_two,
+    part, part_core, part_z, home_in, home_layer,
+    give, keep, q_buffer, core_in, p_one_in, p_two_in, p_three_in, q_one_in, q_two_in,
+    sums_ref, sums_x, sums_y, pair_ref, small_ref, small_z, small_c, routed,
+    send_sems, recv_sems, local_sems,
+):
+    links = Links(send_sems, recv_sems)
+    x, y, z, c = links.here
+    ctx, y_low = y // 2, lax.rem(y, 2)
+    x_after, x_before, x_far = lax.rem(x + 1, 4), lax.rem(x + 3, 4), lax.rem(x + 2, 4)
+    own_rows, other_rows = at(c * HALF, HALF), at((1 - c) * HALF, HALF)
+    loads = []
+
+    def load(source, target):
+        copy = pltpu.make_async_copy(source, target, local_sems.at[len(loads)])
+        copy.start()
+        loads.append(copy)
+        return copy
+
+    def pair_of(array, place):
+        return array.at[at(place * 2, 2)]
+
+    near_loads = [
+        load(pair_of(grad_moe, x_after), moe_after),
+        load(pair_of(grad_moe, x_before), moe_before),
+        load(grad_near, moe_near),
+    ]
+    every = pl.ds(0, 256)
+    out_loads = [
+        load(low_hbm, low),
+        load(weights.at[:, :, every, pl.ds(896, 256)], w_ref.at[:, :, :, pl.ds(768, 256)]),
+        load(mixed_hbm, mixed),
+        load(rot_hbm, rot),
+        load(kv_hbm, kv),
+        load(kv_far_hbm, kv_far),
+        load(lse_hbm.at[pl.ds(0, 2)], lse),
+    ]
+    next_loads = [
+        load(pre_hbm, pre),
+        load(weights.at[:, :, every, pl.ds(0, 768)], w_ref.at[:, :, :, pl.ds(0, 768)]),
+        load(weights.at[:, :, pl.ds(256, 16), every], w_gains),
+        load(tok_hbm.at[at(c * HALF + z * HOME, HOME)], home_tok),
+    ]
+    last_loads = [
+        load(gated_hbm, gated),
+        load(w_out_hbm, w_out),
+    ]
+    links.greet(STEPS_X + [(2, 0, 0, 0)] + STEPS_Y + STEPS_Z + STEPS_C)
+
+    for copy in near_loads:
+        copy.wait()
+    moe_after[0] = (moe_after[0].astype(F32) + moe_near[0].astype(F32)).astype(BF)
+    moe_two = [links.send(moe_after, moe_in.at[0], dx=1)]
+    moe_before[1] = (moe_before[1].astype(F32) + moe_near[1].astype(F32)).astype(BF)
+    moe_two.append(links.send(moe_before, moe_in.at[1], dx=-1))
+    moe_own = moe_near
+    own_load = load(pair_of(grad_moe, x), moe_own)
+
+    own_first = at(ctx * ROWS, ROWS)
+    for copy in out_loads:
+        copy.wait()
+    total = jnp.zeros((ROWS, 256), F32)
+    for s in range(8):
+        total = total + dot_nt(low[:, s * 256 : s * 256 + 256], w_ref[s // 2, s % 2, :, 768:1024])
+    mixed_grad[...] = total.astype(BF)
+
+    score_scale = 128 ** (-0.5)
+    deltas = []
+    for h in range(2):
+        lane = slice(h * 128, h * 128 + 128)
+        deltas.append(
+            jnp.sum(
+                mixed_grad[:, lane].astype(F32) * mixed[:, lane].astype(F32), axis=-1, keepdims=True
+            )
+        )
+
+    def scores_back(h, keys_values):
+        lane = slice(h * 128, h * 128 + 128)
+        keys, values = keys_values[:, lane], keys_values[:, 256 + h * 128 : 384 + h * 128]
+        scores = dot_nt(rot[:, lane], keys) * score_scale + bias[...]
+        probs = jnp.exp(scores - lse[h][:, 0:1])
+        prob_grad = dot_nt(mixed_grad[:, lane], values)
+        score_grad = (probs * (prob_grad - deltas[h])).astype(BF)
+        query_part = dot(score_grad, keys) * score_scale
+        key_part = dot_tn(score_grad, rot[:, lane]) * score_scale
+        value_part = dot_tn(probs.astype(BF), mixed_grad[:, lane])
+        return query_part, key_part, value_part
+
+    earlier = links.send(kv_give, kv_got, dy=2, start=False)
+
+    @pl.when(ctx == 1)
+    def _():
+        bias[...] = earlier_mask(segment_rows, segment_row, own_first)
+        for h in range(2):
+            query_part, key_part, value_part = scores_back(h, kv_far)
+            dq[:, h * 128 : h * 128 + 128] = query_part
+            kv_give[:, h * 128 : h * 128 + 128] = key_part.astype(BF)
+            kv_give[:, 256 + h * 128 : 384 + h * 128] = value_part.astype(BF)
+        earlier.start()
+
+    @pl.when(ctx == 0)
+    def _():
+        dq[...] = jnp.zeros_like(dq)
+
+    bias[...] = own_mask(segment_rows, segment_row, own_first)
+    for h in range(2):
+        query_part, key_part, value_part = scores_back(h, kv)
+        dq[:, h * 128 : h * 128 + 128] += query_part
+        dkv[:, h * 128 : h * 128 + 128] = key_part
+        dkv[:, 256 + h * 128 : 384 + h * 128] = value_part
+
+    def out_grad_block(s, carry):
+        attn_grad[s, :, 768:1024] = dot_tn(mixed[...], low[:, at(s * 256, 256)]).astype(BF)
+        return carry
+
+    lax.fori_loop(0, 8, out_grad_block, 0)
+    normed = low
+    normed_load = load(normed_hbm, normed)
+    for copy in next_loads:
+        copy.wait()
+    head_gains = jnp.zeros((16, 128), F32)
+    for s in range(8):
+        head_gains = head_gains + w_gains[s // 2, s % 2, :, 0:128].astype(F32)
+    cosine, sine = cosine_ref[own_first, :], sine_ref[own_first, :]
+
+    def head_back(grads, first, first_gain):
+        for h in range(2):
+            lane = slice(first + h * 128, first + h * 128 + 128)
+            unit_grad = turned(
+                grads[:, h * 128 : h * 128 + 128].astype(BF).astype(F32), cosine, -sine
+            )
+            source = pre[:, lane]
+            gain = head_gains[first_gain + h : first_gain + h + 1]
+            grad, gain_rows = norm_back(unit_grad, source, rms_scale(source), gain)
+            stacked[:, lane] = grad.astype(BF)
+            row = first_gain - 2 + h
+            heads_row = jnp.sum(gain_rows, axis=0, keepdims=True)
+            for s in range(8):
+                sums_ref[s // 2, s % 2, row + 2 : row + 3, 0:128] = heads_row
+                sums_ref[s // 2, s % 2, row + 2 : row + 3, 128:256] = jnp.zeros_like(heads_row)
+
+    head_back(dq, 0, 2)
+
+    @pl.when(ctx == 0)
+    def _():
+        earlier.wait_recv()
+        dkv[...] += kv_got[...].astype(F32)
+
+    head_back(dkv, 256, 4)
+    stacked[:, 512:768] = dkv[:, 256:512].astype(BF)
+
+    def input_rows(rows, target):
+        def one_block(s, carry):
+            block = w_ref[s // 2, lax.rem(s, 2), :, 0:768]
+            part[target, :, at(s * 256, 256)] = dot_nt(stacked[rows, :], block).astype(BF)
+            return carry
+
+        lax.fori_loop(0, 8, one_block, 0)
+
+    input_rows(other_rows, 1)
+    core_sum = links.send(part.at[1], part_core, dc=1)
+    input_rows(own_rows, 0)
+
+    def weight_block(slot):
+        attn_grad[slot, :, 0:768] = dot_tn(normed[:, at(slot * 256, 256)], stacked[...]).astype(BF)
+
+    normed_load.wait()
+    weight_block(x_far * 2)
+    weight_block(x_far * 2 + 1)
+    attn_first = [
+        links.send(attn_grad.at[x_far * 2], attn_one.at[0], dx=1),
+        links.send(attn_grad.at[x_far * 2 + 1], attn_one.at[1], dx=-1),
+    ]
+    core_sum.wait_recv()
+    part[0] = (part[0].astype(F32) + part_core[...].astype(F32)).astype(BF)
+    z_sum = [
+        links.send(part.at[0, at(lax.rem(z + d + 4, 4) * HOME, HOME)], part_z.at[k], dz=d)
+        for k, d in enumerate((1, -1, 2))
+    ]
+
+    def other_blocks(i, carry):
+        weight_block(lax.rem(x_far * 2 + 2 + i, 8))
+        return carry
+
+    lax.fori_loop(0, 6, other_blocks, 0)
+
+    for copy in last_loads:
+        copy.wait()
+    sums = TokenSum(links, give, keep, (core_in, p_one_in, p_two_in, p_three_in, q_one_in, q_two_in))
+
+    def expert_rows(k, rows, target):
+        def one_block(s, carry):
+            block = w_out[:, :, at(s * 256, 256)].reshape(512, 256)
+            target[:, at(s * 256, 256)] = dot(gated[k, rows, :], block).astype(BF)
+            return carry
+
+        lax.fori_loop(0, 8, one_block, 0)
+
+    def expert_chunk(k):
+        expert_rows(k, other_rows, give.at[sums.give_slot(k)])
+        sums.give_core(k)
+        expert_rows(k, own_rows, keep.at[k])
+        if k:
+            sums.q_send(k - 1, q_buffer)
+        sums.add(k)
+
+    expert_chunk(0)
+    expert_chunk(1)
+
+    arrived(z_sum)
+    normed_grad = part[0, at(z * HOME, HOME), :].astype(F32)
+    for k in range(3):
+        normed_grad = normed_grad + part_z[k].astype(F32)
+    gains = jnp.concatenate(
+        [w_gains[s // 2, s % 2].astype(F32)[0:1] for s in range(8)], axis=1
+    )
+    input_back, gain_rows = norm_back(
+        normed_grad, home_tok[...].astype(F32), home_scale_ref[:, 0:1], gains
+    )
+    home_in[...] = (hidden_grad_ref[...] + input_back).astype(BF)
+    gain_row = jnp.sum(gain_rows, axis=0, keepdims=True)
+    for s in range(8):
+        columns = slice(s * 256, s * 256 + 256)
+        sums_ref[s // 2, s % 2, 0:1, :] = gain_row[:, columns]
+        sums_ref[s // 2, s % 2, 1:2, :] = gain_ref[0:1, columns]
+        sums_ref[s // 2, s % 2, 6:16, :] = jnp.zeros((10, 256), F32)
+    place_in = load(home_in, input_all.at[c, z])
+    input_near = spread_home(links, input_all, home_in)
+    sum_x = [
+        links.send(sums_ref.at[lax.rem(x + d + 4, 4)], sums_x.at[k], dx=d)
+        for k, d in enumerate((1, -1, 2))
+    ]
+    expert_chunk(2)
+    expert_chunk(3)
+    sums.p_send()
+
+    arrived(moe_two)
+    arrivals = []
+    for n, target in enumerate((moe_after, moe_before)):
+        links.left(moe_two[n])
+        arrivals.append(load(moe_in.at[n], target))
+    own_load.wait()
+    for copy in arrivals:
+        copy.wait()
+    for i in range(2):
+        total = moe_own[i].astype(F32) + moe_after[i].astype(F32) + moe_before[i].astype(F32)
+        for e in range(4):
+            pay_in[i, e] = total[:, e * 256 : e * 256 + 128].astype(BF)
+            pay_in[i, 4 + e] = total[:, e * 256 + 128 : e * 256 + 256].astype(BF)
+            pay_out[i, e] = total[:, 1152 + e * 128 : 1280 + e * 128].T.astype(BF)
+        pay_in[i, 8] = total[:, 1024:1152].astype(BF)
+    groups = []
+    for d, low_place in ((1, 1 - y_low), (-1, 1 - y_low), (2, y_low)):
+        groups.append(links.send(pay_in.at[low_place], groups_in.at[y], dy=d))
+        groups.append(links.send(pay_out.at[low_place], groups_out.at[y], dy=d))
+    place_groups = [load(pay_in.at[y_low], groups_in.at[y]), load(pay_out.at[y_low], groups_out.at[y])]
+
+    arrived(attn_first)
+    slot = x_after * 2
+    attn_grad[slot] = (attn_grad[slot].astype(F32) + attn_one[0].astype(F32)).astype(BF)
+    attn_next = [links.send(pair_of(attn_grad, x_after), attn_two.at[0], dx=1)]
+    slot = x_before * 2 + 1
+    attn_grad[slot] = (attn_grad[slot].astype(F32) + attn_one[1].astype(F32)).astype(BF)
+    attn_next.append(links.send(pair_of(attn_grad, x_before), attn_two.at[1], dx=-1))
+
+    first, second = sums.home()
+    home_layer[...] = (hidden_ref[...] + jnp.concatenate([first, second], axis=0)).astype(BF)
+    place_layer = load(home_layer, layer_all.at[c, z])
+    layer_near = spread_home(links, layer_all, home_layer)
+    arrived(input_near)
+    place_in.wait()
+    siblings = [links.send(input_all.at[c], input_all.at[c], dc=1)]
+
+    arrived(sum_x)
+    pair_ref[...] = sums_ref[x] + sums_x[0] + sums_x[1] + sums_x[2]
+    sum_y = [
+        links.send(pair_ref.at[low_place], sums_y.at[k], dy=d)
+        for k, (d, low_place) in enumerate(((1, 1 - y_low), (-1, 1 - y_low), (2, y_low)))
+    ]
+    arrived(layer_near)
+    place_layer.wait()
+    siblings.append(links.send(layer_all.at[c], layer_all.at[c], dc=1))
+    arrived(groups)
+    for copy in place_groups:
+        copy.wait()
+    get_routed = load(groups_in.at[:, 8], routed)
+    arrived(sum_y)
+    summed = pair_ref[y_low] + sums_y[0] + sums_y[1] + sums_y[2]
+    heads_out[...] = jnp.concatenate([summed[2:6, 0:128], jnp.zeros((4, 128), F32)], axis=0)
+    get_routed.wait()
+    small_ref[0:256] = (
+        routed[0].astype(F32) + routed[1].astype(F32) + routed[2].astype(F32) + routed[3].astype(F32)
+    )
+    small_ref[256:SMALL] = jnp.concatenate(
+        [summed[0:2, 0:128], summed[0:2, 128:256], jnp.zeros((4, 128), F32)], axis=0
+    )
+    small_sums = [
+        links.send(small_ref, small_z.at[k], dz=d) for k, d in enumerate((1, -1, 2))
+    ]
+
+    arrived(attn_next)
+    def attn_total(low_place):
+        slot = x * 2 + low_place
+        return (
+            attn_grad[slot].astype(F32)
+            + attn_two[0, low_place].astype(F32)
+            + attn_two[1, low_place].astype(F32)
+        )
+
+    attn_give[...] = attn_total(1 - y_low).astype(BF)
+    top, bottom = pl.ds(0, 128), pl.ds(128, 128)
+    y_first = [
+        links.send(attn_give.at[top], attn_y_one.at[top], dy=1),
+        links.send(attn_give.at[bottom], attn_y_one.at[bottom], dy=-1),
+    ]
+    kept = attn_total(y_low)
+    arrived(small_sums)
+    small_ref_total = small_ref[...] + small_z[0] + small_z[1] + small_z[2]
+    small_out[...] = small_ref_total
+    small_core = links.send(small_out, small_c, dc=1)
+    arrived(y_first)
+    attn_keep[...] = (kept + attn_y_one[...].astype(F32)).astype(BF)
+    y_second = links.send(attn_keep, attn_y_two, dy=2)
+    small_core.wait()
+    small_out[...] = small_ref_total + small_c[...]
+    arrived(siblings)
+    y_second.wait_recv()
+    for n, target in enumerate((grad_q, grad_k, grad_v, grad_o)):
+        columns = slice(n * 256, n * 256 + 256)
+        target[...] = attn_keep[:, columns].astype(F32) + attn_y_two[:, columns].astype(F32)
+
+    for copy in links.made:
+        if copy is not earlier and copy is not small_core:
+            copy.wait_send()
+
+    @pl.when(ctx == 1)
+    def _():
+        earlier.wait_send()
+
+
+BACK_COPIES = 2 + 1 + 1 + 3 + 2 + TOKEN_SUM_COPIES + 3 + 3 + 6 + 2 + 3 + 2 + 3 + 3 + 1 + 3
+
+
+def run_back(hbm, vmem):
+    shape = jax.ShapeDtypeStruct
+    outs = (
+        (shape((2, 4, HOME, WIDTH), BF), ANY),
+        (shape((2, 4, HOME, WIDTH), BF), ANY),
+        (shape((4, 9, 256, 128), BF), ANY),
+        (shape((4, 4, 128, 256), BF), ANY),
+        (shape((2, 2, 256, MCOLS), BF), ANY),
+        (shape((256, 256), F32), VMEM),
+        (shape((256, 256), F32), VMEM),
+        (shape((256, 256), F32), VMEM),
+        (shape((256, 256), F32), VMEM),
+        (shape((SMALL, 128), F32), VMEM),
+        (shape((8, 128), F32), VMEM),
+    )
+
+    def buffer(*dims, kind=BF):
+        return pltpu.VMEM(dims, kind)
+
+    return pl.pallas_call(
+        back,
+        out_shape=[o for o, _ in outs],
+        in_specs=[ANY] * len(hbm) + [VMEM] * len(vmem),
+        out_specs=[spec for _, spec in outs],
+        scratch_shapes=[
+            buffer(4, 2, 256, 1024),
+            buffer(4, 2, 16, 256),
+            buffer(ROWS, WIDTH),
+            buffer(ROWS, 256),
+            buffer(ROWS, 512),
+            buffer(ROWS, 512),
+            buffer(ROWS, 512),
+            buffer(2, ROWS, 128, kind=F32),
+            buffer(ROWS, 512, kind=F32),
+            buffer(4, ROWS, 512),
+            buffer(4, 128, WIDTH),
+            buffer(HOME, WIDTH),
+            buffer(ROWS, ROWS, kind=F32),
+            buffer(ROWS, 256),
+            buffer(ROWS, 256, kind=F32),
+            buffer(ROWS, 512, kind=F32),
+            buffer(ROWS, 512),
+            buffer(ROWS, 512),
+            buffer(ROWS, 768),
+            buffer(2, 256, MCOLS),
+            buffer(2, 256, MCOLS),
+            buffer(2, 256, MCOLS),
+            buffer(2, 9, 256, 128),
+            buffer(2, 4, 128, 256),
+            buffer(8, 256, 1024),
+            buffer(2, 256, 1024),
+            buffer(2, 2, 256, 1024),
+            buffer(256, 1024),
+            buffer(256, 1024),
+            buffer(256, 1024),
+            buffer(256, 1024),
+            buffer(2, HALF, WIDTH),
+            buffer(HALF, WIDTH),
+            buffer(3, HOME, WIDTH),
+            buffer(HOME, WIDTH),
+            buffer(HOME, WIDTH),
+            buffer(2, HALF, WIDTH),
+            buffer(4, HALF, WIDTH),
+            buffer(3, 32, WIDTH),
+            *scatter_buffers(),
+            buffer(4, 2, 16, 256, kind=F32),
+            buffer(3, 2, 16, 256, kind=F32),
+            buffer(3, 16, 256, kind=F32),
+            buffer(2, 16, 256, kind=F32),
+            buffer(SMALL, 128, kind=F32),
+            buffer(3, SMALL, 128, kind=F32),
+            buffer(SMALL, 128, kind=F32),
+            buffer(4, 256, 128),
+            pltpu.SemaphoreType.DMA((BACK_COPIES,)),
+            pltpu.SemaphoreType.DMA((BACK_COPIES,)),
+            pltpu.SemaphoreType.DMA((32,)),
+        ],
+        compiler_params=pltpu.CompilerParams(
+            collective_id=3, has_side_effects=True, vmem_limit_bytes=62 * MIB
+        ),
+        name="back",
+    )(*hbm, *vmem)
+
+
 def turn_tables():
     frequency = ROPE_BASE ** (-(np.arange(0, 128, 2, dtype=np.float64) / 128))
     angles = np.arange(1024, dtype=np.float64)[:, None] * frequency[None, :]
@@ -914,35 +1260,8 @@
     down_weight,
 ):
     rows, width = tokens.shape[1], tokens.shape[2]
-    experts = gate_weight.shape[0]
-    own_experts = experts // 4
-    hidden_units = gate_weight.shape[2]
-    span = own_experts * hidden_units
-    shard, ctx, tp = lax.axis_index("shard"), lax.axis_index("ctx"), lax.axis_index("tp")
-    x, y_low, z, core = shard // 2, shard % 2, tp // 2, tp % 2
-    y = ctx * 2 + y_low
-    home = rows // 8
-    head_dim = 128
-    local_width = 256
-    score_scale = head_dim ** (-0.5)
-
-    def spread_rows(part):
-        lane = in_order(direct_gather(part, "z"), z).reshape(4 * part.shape[0], -1)
-        return with_partner(lane, hop(lane, dc=1), core)
-
-    def home_sum(terms):
-        keep = lax.dynamic_slice_in_dim(terms, core * 256, 256, 0)
-        give = lax.dynamic_slice_in_dim(terms, (1 - core) * 256, 256, 0)
-        lane = added(keep, hop(give, dc=1)).astype(BF).reshape(4, home, -1)
-        return direct_scatter(by_distance(lane, z), "z")
-
-    def tokens_sum(terms):
-        terms = terms.reshape(4, rows, -1)
-        keep = lax.dynamic_slice_in_dim(terms, core * 256, 256, 1)
-        give = lax.dynamic_slice_in_dim(terms, (1 - core) * 256, 256, 1)
-        lane = added(keep, hop(give, dc=1)).astype(BF)
-        mine = ring_scatter(by_distance(lane, y), "y").astype(BF).reshape(4, home, -1)
-        return direct_scatter(by_distance(mine, z), "z")
+    experts_count = gate_weight.shape[0]
+    shard = lax.axis_index("shard")
 
     lanes = jnp.zeros((4, 128), BF)
     head_gains = jnp.concatenate([query_gain, key_gain], axis=0)
@@ -950,7 +1269,7 @@
     gain_rows = jnp.zeros((16, WCOLS), BF)
     gain_rows = gain_rows.at[0, :256].set(attn_gain).at[1, :256].set(moe_gain)
     gain_rows = gain_rows.at[2:6, :128].set(lanes)
-    router_pad = jnp.pad(router_weight, ((0, 0), (0, 128 - experts)))
+    router_pad = jnp.pad(router_weight, ((0, 0), (0, 128 - experts_count)))
     own_weights = jnp.concatenate(
         [
             jnp.concatenate([query_weight, key_weight, value_weight, router_pad, out_weight], axis=1),
@@ -965,7 +1284,7 @@
     ).astype(BF)
     (
         weights, experts_in, experts_out, grad_all, picked_all, moe_in_all,
-        normed, pre, rot, key_value, mixed_low, lse, hidden, home_scale_one,
+        normed, pre, rot, key_value, key_value_far, mixed, lse, hidden, home_scale,
     ) = run_front(
         tokens.reshape(rows, width), own_weights, turn_tables(), segments,
         gate_weight, up_weight, down_weight, own_grad, own_picked,
@@ -973,152 +1292,39 @@
     gated, grad_moe, grad_near, hidden_low, hidden_grad, gain_sum = run_experts(
         moe_in_all, grad_all, picked_all, experts_in, experts_out, weights, hidden
     )
-    hidden_low = hidden_low.reshape(rows, width)
-    weights = weights.reshape(8, WROWS, WCOLS)
-    w_stacked = weights[:, :256, :768].reshape(width, -1)
-    w_out_t = weights[:, :256, 896:].transpose(0, 2, 1).reshape(width, -1)
-    gain_rows = weights[:, 256:].astype(F32)
-    attn_gains = gain_rows[:, 0, :256].reshape(-1)
-    moe_gains = gain_rows[:, 1, :256].reshape(-1)
-    head_gains = jnp.sum(gain_rows[:, 2:6, :128], axis=0)
-
-    inputs = tokens.reshape(rows, width).astype(F32)
-    first_row = ctx * rows
-    places = first_row + jnp.arange(rows, dtype=jnp.int32)
-    cosine, sine_table = rope_tables(places, head_dim)
-    query_pre = [pre[:, h * 128 : h * 128 + 128] for h in range(2)]
-    key_pre = [pre[:, 256 + h * 128 : 384 + h * 128] for h in range(2)]
-    scale_query = [rms_scale(v) for v in query_pre]
-    scale_key = [rms_scale(v) for v in key_pre]
-    gain_q = [head_gains[h][None] for h in range(2)]
-    gain_k = [head_gains[2 + h][None] for h in range(2)]
-    query_low = [rot[:, h * 128 : h * 128 + 128] for h in range(2)]
-    earlier = hop(key_value, dy=2, only=lambda x, y, z, c: y < 2)
-    both = jnp.concatenate([earlier, key_value], axis=0)
-    keys = [both[:, h * 128 : h * 128 + 128] for h in range(2)]
-    values = [both[:, 256 + h * 128 : 384 + h * 128] for h in range(2)]
-    key_places = first_row - rows + jnp.arange(2 * rows, dtype=jnp.int32)
-    own_segments = lax.dynamic_slice_in_dim(segments[0], first_row, rows, 0)
-    key_segments = jnp.concatenate([segments[0, :rows], own_segments])
-    allowed = (
-        (places[:, None] >= key_places[None, :])
-        & (key_places[None, :] >= 0)
-        & (own_segments[:, None] == key_segments[None, :])
-    )
-    probs = []
-    for h in range(2):
-        scores = jnp.where(allowed, dot_nt(query_low[h], keys[h]) * score_scale, MASKED_SCORE)
-        probs.append(jnp.exp(scores - lse[h][:, :1]))
-    home_row = (core * 4 + z) * home
-    home_inputs = lax.dynamic_slice_in_dim(tokens.reshape(rows, width), home_row, home, 0).astype(F32)
-    home_scale_one = home_scale_one[:, :1]
-
-    moe_part = dot(gated.reshape(4 * rows, -1), experts_out.reshape(-1, width)).astype(BF)
-    far, after, before, mine = [moe_part[k * rows : k * rows + rows] for k in range(4)]
-    moe_part = in_order([mine, after, far, before], y).reshape(4 * rows, width)
-    layer_rows = (hidden + tokens_sum(moe_part)).astype(BF)
-    layer_out = spread_rows(layer_rows).reshape(tokens.shape)
-    own_chunk, to_after, _, to_before = by_distance(grad_moe.reshape(4, 2, 256, -1), x)
-    to_after = jnp.stack([added(to_after[0], grad_near[0]).astype(BF), to_after[1]])
-    to_before = jnp.stack([to_before[0], added(to_before[1], grad_near[1]).astype(BF)])
-    grad_moe = added(own_chunk, hop(to_after, dx=1), hop(to_before, dx=-1))
-    grad_router = jnp.concatenate(
-        [grad_moe[0, :, 1024 : 1024 + experts], grad_moe[1, :, 1024 : 1024 + experts]], axis=0
-    ).T.reshape(-1, 128)
-    grad_moe = grad_moe.astype(BF)
-    keep = lax.dynamic_index_in_dim(grad_moe, y_low, 0, keepdims=False)
-    give = lax.dynamic_index_in_dim(grad_moe, 1 - y_low, 0, keepdims=False)
-    grad_groups = in_order(
-        [keep, hop(give, dy=-1), hop(keep, dy=2), hop(give, dy=1)], y
-    )
-    joined = grad_groups[:, :, :1024].reshape(4, 256, own_experts, 256).transpose(0, 2, 1, 3)
-    grad_gate_weight = joined[..., :128].reshape(experts, 256, hidden_units).astype(F32)
-    grad_up_weight = joined[..., 128:].reshape(experts, 256, hidden_units).astype(F32)
-    grad_down_weight = (
-        grad_groups[:, :, 1152:]
-        .reshape(4, 256, own_experts, hidden_units)
-        .transpose(0, 2, 3, 1)
-        .reshape(experts, hidden_units, 256)
-        .astype(F32)
-    )
-    grad_router = grad_router + hop(grad_router, dc=1)
-    for axis in "zy":
-        grad_router = direct_scatter([grad_router] * 4, axis)
-    grad_router = grad_router.reshape(experts, 2, 256)
-    grad_router = lax.dynamic_index_in_dim(grad_router, y_low, 1, keepdims=False).T
-    early = gain_sum[0].reshape(-1, 128)
-    early = early + hop(early, dc=1)
-    for axis in "zyx":
-        early = direct_scatter([early] * 4, axis)
-    grad_moe_gain = lax.dynamic_slice_in_dim(early.reshape(-1), shard * 256, 256, 0)
-
-    mixed_grad = dot(hidden_low, w_out_t).astype(BF)
-    grad_out_t = dot_tn(hidden_low, mixed_low)
-    query_grads, key_terms, value_terms = [], [], []
-    for h in range(2):
-        grad_h = mixed_grad[:, h * 128 : h * 128 + 128]
-        prob_grad = dot_nt(grad_h, values[h])
-        row_delta = jnp.sum(probs[h] * prob_grad, axis=-1, keepdims=True)
-        score_grad = (probs[h] * (prob_grad - row_delta)).astype(BF)
-        query_grads.append((dot(score_grad, keys[h]) * score_scale).astype(BF).astype(F32))
-        key_terms.append(dot_tn(score_grad, query_low[h]) * score_scale)
-        value_terms.append(dot_tn(probs[h].astype(BF), grad_h))
-    terms = jnp.concatenate(key_terms + value_terms, axis=1)
-    later = hop(terms[:rows].astype(BF), dy=2, only=lambda x, y, z, c: y >= 2)
-    key_value_grad = added(terms[rows:], later).astype(BF)
-    stacked, gain_sums = [], []
-    for pre, scale, gain, grads in (
-        (query_pre, scale_query, gain_q, query_grads),
-        (key_pre, scale_key, gain_k, [key_value_grad[:, :128], key_value_grad[:, 128:256]]),
-    ):
-        for h in range(2):
-            unit_grad = rotate(grads[h].astype(F32), cosine, -sine_table)
-            pre_back, gain_rows = norm_back(unit_grad, pre[h], scale[h], gain[h])
-            stacked.append(pre_back.astype(BF))
-            gain_sums.append(jnp.sum(gain_rows, axis=0))
-    stacked = jnp.concatenate(stacked + [key_value_grad[:, 256:]], axis=1)
-    normed_part = dot_nt(stacked, w_stacked).astype(BF)
-    grad_stacked = dot_tn(normed, stacked)
-    normed_grad = home_sum(normed_part)
-    input_norm_grad, attn_gain_rows = norm_back(
-        normed_grad, home_inputs, home_scale_one, attn_gains
-    )
-    input_grad = spread_rows((hidden_grad + input_norm_grad).astype(BF)).reshape(tokens.shape)
-    grad_attn = jnp.concatenate([grad_stacked, grad_out_t], axis=1).astype(BF)
-    grad_attn = ring_scatter(by_distance(grad_attn.reshape(4, 512, -1), x), "x").astype(BF)
-    grad_attn = grad_attn.reshape(2, 256, -1)
-    keep = lax.dynamic_index_in_dim(grad_attn, y_low, 0, keepdims=False)
-    give = lax.dynamic_index_in_dim(grad_attn, 1 - y_low, 0, keepdims=False)
-    got = jnp.concatenate([hop(give[:128], dy=1), hop(give[128:], dy=-1)], axis=0)
-    keep = added(keep, got).astype(BF)
-    grad_attn = added(keep, hop(keep, dy=2))
-    head_gain_sums = jnp.stack(gain_sums).reshape(2, 1, 2, 128)
-    mine = (jnp.arange(8) == tp).astype(F32)[None, :, None, None]
-    late = jnp.concatenate(
-        [jnp.sum(attn_gain_rows, axis=0), (mine * head_gain_sums).reshape(-1)]
-    ).reshape(48, 128)
-    late = late + hop(late, dc=1)
-    for axis in "zyx":
-        late = direct_scatter([late] * 4, axis)
-    grad_attn_gain = lax.dynamic_slice_in_dim(late[:16].reshape(-1), shard * 256, 256, 0)
-    late_heads = late[16:].reshape(2, 8, 2, 128)
-    late_heads = lax.dynamic_index_in_dim(late_heads, tp, 1, keepdims=False)
-    late_heads = lax.dynamic_slice_in_dim(late_heads, shard * 16, 16, 2)
+    tables = turn_tables()
+    (
+        layer_all, input_all, groups_in, groups_out, _, grad_q, grad_k, grad_v, grad_o, small, heads,
+    ) = run_back(
+        [
+            grad_moe, grad_near, hidden_low.reshape(rows, width), weights, mixed, rot, key_value,
+            key_value_far, lse, pre, normed, gated, experts_out, tokens.reshape(rows, width),
+        ],
+        [
+            hidden, hidden_grad, home_scale, gain_sum, jnp.asarray(tables[0]), jnp.asarray(tables[1]),
+            segments.reshape(-1, 1), segments,
+        ],
+    )
+    head_grads = lax.dynamic_slice_in_dim(heads[:4], shard * 16, 16, 1)
+
+    def grown(groups):
+        return groups.reshape((experts_count,) + groups.shape[2:]).astype(F32)
+
     return (
-        layer_out,
-        input_grad,
-        grad_attn[:, :256],
-        grad_attn[:, 256:512],
-        grad_attn[:, 512:768],
-        grad_attn[:, 768:].T,
-        grad_router,
-        grad_attn_gain,
-        grad_moe_gain,
-        late_heads[0],
-        late_heads[1],
-        grad_gate_weight,
-        grad_up_weight,
-        grad_down_weight,
+        layer_all.reshape(tokens.shape),
+        input_all.reshape(tokens.shape),
+        grad_q,
+        grad_k,
+        grad_v,
+        grad_o,
+        small[:256, :experts_count],
+        small[256::2][:2].reshape(-1),
+        small[257::2][:2].reshape(-1),
+        head_grads[:2],
+        head_grads[2:],
+        grown(groups_in[:, :4]),
+        grown(groups_in[:, 4:8]),
+        grown(groups_out),
     )
 
 

time: 556 us -> 400 us (0.72)
  Pallas kernels: 219 us -> 361 us
  waiting for transfers between devices: 97.1 us -> 0 us
  starting transfers between devices: 83.5 us -> 0 us
  local copies, waits for them, and re-layouts: 67.8 us -> 19.1 us
  other arithmetic: 57.3 us -> 10.6 us
  matrix products: 22.2 us -> 0 us
    pallas_call x0 -> x1, Pallas kernels: none -> 145 us  [run_back(): pl.pallas_call(back, out_shape=[o for o, _ in outs], in_specs=[ANY] * len...]
    ppermute x61 -> x0, waiting for transfers between devices: 97.1 us -> none  [hop(): return lax.ppermute(value, AXES, pairs)]
    ppermute x61 -> x0, starting transfers between devices: 83.5 us -> none  [hop(): return lax.ppermute(value, AXES, pairs)]
    dot_general x15 -> x0, matrix products: 22.2 us -> none  [the longest x4 10.5 us: dot(): return jnp.dot(left, right, preferred_element_type=F32)]
    convert_element_type x19 -> x2, other arithmetic: 23.6 us -> 5.41 us  [grown(): return groups.reshape((experts_count,) + groups.shape[2:]).astype(F32)]
    select_n x2 -> x0, other arithmetic: 9.55 us -> none  [with_partner(): jnp.where(number == 0, jnp.concatenate([own, other], 0), jnp.concatenate(...]
    slice x18 -> x6, local copies, waits for them, and re-layouts: 12.8 us -> 3.83 us  [the longest x1 0.91 us: body(): small[:256, :experts_count]]
    dynamic_update_slice x14 -> x0, local copies, waits for them, and re-layouts: 7.96 us -> none  [in_order(): lax.dynamic_update_index_in_dim(whole, block, (start + distance) % 4, 0)]
  transfers between devices with their start and end apart: 61 -> 0, of which waited for: 26 -> 0; matrix products, arithmetic and copies ran while one was open for 22% -> 0% of each run, Pallas kernels for 0% -> 0%
where the time goes in v4:
time: 400 us; the launch traced here: 392 us
  Pallas kernels  361 us (90%)
  local copies, waits for them, and re-layouts  19.1 us (5%)
  other arithmetic  10.6 us (3%)
    pallas_call x1, Pallas kernels, run_back(): pl.pallas_call(back, out_shape=[o for o, _ in outs], in_specs=[ANY] * len...  145 us
    pallas_call x1, Pallas kernels, run_front(): pl.pallas_call(front, out_shape=[o for o, _ in outs], in_specs=[VMEM] * 6...  130 us
    pallas_call x1, Pallas kernels, run_experts(): pl.pallas_call(experts, out_shape=[o for o, _ in outs], in_specs=[ANY] *...  86 us
    unnamed x30, local copies, waits for them, and re-layouts  9.88 us

profile of v4, /device:TPU:14, one launch (start us, length us, event | category | flops | bytes accessed | tf_op | source)
XLA Modules:
  0.0 392.4 jit_solution(18084264381347522827)
XLA Ops:
  0.6 0.0 copy-start.8
  0.7 0.0 copy-start.7
  0.7 0.7 reshape.161
  1.4 0.7 reshape.162
  2.0 0.7 pad_maximum_fusion.1
  2.7 0.3 dynamic_update_slice.5
  3.0 0.2 scatter.11
  3.3 0.3 scatter.14
  3.6 0.8 copy.42
  4.4 0.8 copy.43
  5.3 2.9 fusion
  8.2 0.7 convert_element_type.23.picked
  8.8 1.7 copy.44.segment_rows
  10.6 0.9 constant_dynamic-update-slice_fusion.3
  11.5 0.9 constant_dynamic-update-slice_fusion.2
  12.4 0.0 copy-done.7
  12.4 0.0 copy-done.8
  12.5 0.9 pad_maximum_fusion.own_weights
  13.4 130.4 %front.1 = (bf16[4,2,272,1152]{3,2,1,0:T(8,128)(2,1)}, bf16[4,4,2,256,256]{4,3,2,1,0:T(8,128)(2,1)}, bf16[4,128,2048]{2,1,0:T(8,128)(2,1)}, bf16[4,512,2048]{2,1...) custom-call(bf16[512,2048]{1,0:T(8,128)(2,1)} %bitcast.21, ...), custom_call_target="tpu_custom_call" | custom-call | tf_op jit(solution)/shard_map/front/pallas_call | solution.py:434
  143.8 86.0 %experts.1 = (bf16[4,512,512]{2,1,0:T(8,128)(2,1)}, bf16[8,256,1664]{2,1,0:T(8,128)(2,1)}, bf16[2,256,1664]{2,1,0:T(8,128)(2,1)}, bf16[2,4,64,2048]{3,2,1,0:T(8,...) custom-call(bf16[4,512,2048]{2,1,0:T(8,128)(2,1)} %bitcast.23, bf16[4,512,2048]{2,1,0:T(8,128)(2,1)} %get-tuple-element.82.g_all, ...), custom_call_target="tpu_custom_call" | custom-call | tf_op jit(solution)/shard_map/experts/pallas_call | solution.py:753
  229.8 145.0 %back.1 = (bf16[2,4,64,2048]{3,2,1,0:T(8,128)(2,1)}, bf16[2,4,64,2048]{3,2,1,0:T(8,128)(2,1)}, bf16[4,9,256,128]{3,2,1,0:T(8,128)(2,1)}, bf16[4,4,128,256]{3,2,1...) custom-call(bf16[8,256,1664]{2,1,0:T(8,128)(2,1)} %get-tuple-element, ...), custom_call_target="tpu_custom_call" | custom-call | tf_op jit(solution)/shard_map/back/pallas_call | solution.py:1169
  374.9 0.0 copy-start.2
  374.9 0.8 slice.93
  375.7 0.1 constant_dynamic-slice_fusion
  375.8 0.6 fusion.2
  376.4 0.7 slice.91
  377.0 0.7 slice.89
  377.7 0.9 slice.88
  378.7 0.7 copy.46
  379.3 0.6 slice_bitcast_fusion
  379.9 2.8 bitcast_convert_fusion
  382.7 0.0 copy-done.2
  382.7 0.1 fusion.1
  382.8 0.0 copy-start.1
  382.8 2.6 bitcast_convert_fusion.1
  385.5 0.0 copy-done.1
  385.5 0.0 copy-start
  385.5 1.3 copy.60
  386.8 1.0 copy-done
  387.8 0.0 copy-start.6
  387.8 0.0 copy-start.5
  387.8 0.0 copy-start.4
  387.8 0.0 copy-start.3
  387.8 1.3 copy.61
  389.1 0.0 copy-done.6
  389.2 0.7 copy.62
  389.9 0.0 copy-done.5
  389.9 0.7 copy.63
  390.6 0.0 copy-done.4
  390.6 0.7 copy.64
  391.3 0.0 copy-done.3
  391.3 0.7 copy.65
  (5 shorter events, 0.1 us)
Async XLA Ops:
  0.6 11.8 %copy-start.8 = (bf16[256,256]{1,0:T(8,128)(2,1)S(1)}, bf16[256,256]{1,0:T(8,128)(2,1)}, u32[]{:S(2)}) copy-start(bf16[256,256]{1,0:T(8,128)(2,1)} %param.33) | copy-start | bytes 393220
  0.7 11.7 %copy-start.7 = (bf16[256,256]{1,0:T(8,128)(2,1)S(1)}, bf16[256,256]{1,0:T(8,128)(2,1)}, u32[]{:S(2)}) copy-start(bf16[256,256]{1,0:T(8,128)(2,1)} %param.32) | copy-start | bytes 393220
  374.9 7.8 %copy-start.2 = (bf16[4,9,256,128]{3,2,1,0:T(8,128)(2,1)S(1)}, bf16[4,9,256,128]{3,2,1,0:T(8,128)(2,1)}, u32[]{:S(2)}) copy-start(bf16[4,9,256,128]{3,2,1,0:T(8,128)(2,1)} %get-tuple-element.110) | copy-start | bytes 7077892
  382.8 2.7 copy-start.1
  385.5 2.3 copy-start
  387.8 1.3 copy-start.6
  387.8 2.0 copy-start.5
  387.8 2.7 copy-start.4
  387.8 3.4 copy-start.3

commit v5 on v4

--- a/solution.py
+++ b/solution.py
@@ -42,7 +42,7 @@
 VMEM = pl.BlockSpec(memory_space=pltpu.VMEM)
 MIB = 1024 * 1024
 ROWS, WIDTH, HOME, HALF = 512, 2048, 64, 256
-WROWS, WCOLS = 272, 1152
+WROWS = 272
 
 
 def places():
@@ -117,70 +117,144 @@
     return values * cosine + pltpu.roll(values, 64, 1) * sine
 
 
-def spread(links, array, home_ref, y, z, c):
-    first, second = pl.ds(0, 32), pl.ds(32, 32)
-    y_after, y_before, y_far = lax.rem(y + 1, 4), lax.rem(y + 3, 4), lax.rem(y + 2, 4)
-    z_after, z_before, z_far = lax.rem(z + 1, 4), lax.rem(z + 3, 4), lax.rem(z + 2, 4)
-    p_one = [
-        links.send(home_ref.at[first], array.at[y, c, z, first], dz=d) for d in (1, -1, 2)
-    ]
-    q_one = [
-        links.send(home_ref.at[second], array.at[y, c, z, second], dy=d) for d in (1, -1, 2)
-    ]
-
-    def p_block(place):
-        return array.at[place, c, :, first]
-
-    def q_block(place):
-        return array.at[:, c, place, second]
-
-    arrived(p_one)
-    p_two = [links.send(p_block(y), p_block(y), dy=d) for d in (1, -1)]
-    sibling = [links.send(p_block(y), p_block(y), dc=1)]
-    arrived(q_one)
-    q_two = [links.send(q_block(z), q_block(z), dz=d) for d in (1, -1)]
-    sibling.append(links.send(q_block(z), q_block(z), dc=1))
-    p_two[0].wait_recv()
-    low, high = pl.ds(0, 2), pl.ds(2, 2)
-    ahead = array.at[y_before, c, low, first]
-    p_far = [links.send(ahead, ahead, dy=1)]
-    sibling.append(links.send(p_block(y_before), p_block(y_before), dc=1))
-    q_two[0].wait_recv()
-    ahead = array.at[low, c, z_before, second]
-    q_far = [links.send(ahead, ahead, dz=1)]
-    sibling.append(links.send(q_block(z_before), q_block(z_before), dc=1))
-    p_two[1].wait_recv()
-    behind = array.at[y_after, c, high, first]
-    p_far.append(links.send(behind, behind, dy=-1))
-    sibling.append(links.send(p_block(y_after), p_block(y_after), dc=1))
-    q_two[1].wait_recv()
-    behind = array.at[high, c, z_after, second]
-    q_far.append(links.send(behind, behind, dz=-1))
-    sibling.append(links.send(q_block(z_after), q_block(z_after), dc=1))
-    arrived(p_far)
-    sibling.append(links.send(p_block(y_far), p_block(y_far), dc=1))
-    arrived(q_far)
-    sibling.append(links.send(q_block(z_far), q_block(z_far), dc=1))
-    return sibling
-
-
-def own_mask(segment_rows, segment_row, own_first):
+class Spread:
+    def __init__(self, links, array, home_ref, first, start):
+        self.links, self.first, self.second = links, first, "z" if first == "y" else "y"
+        rows = pl.ds(start, 32)
+        x, y, z, c = links.here
+        self.source = home_ref.at[rows]
+        if first == "z":
+            self.block = lambda one, two: array.at[
+                lax.rem(y + two + 4, 4), c, lax.rem(z + one + 4, 4), rows
+            ]
+            self.blocks = lambda two: array.at[lax.rem(y + two + 4, 4), c, :, rows]
+        else:
+            self.block = lambda one, two: array.at[
+                lax.rem(y + one + 4, 4), c, lax.rem(z + two + 4, 4), rows
+            ]
+            self.blocks = lambda two: array.at[:, c, lax.rem(z + two + 4, 4), rows]
+        self.near, self.siblings = {}, []
+
+    def pass_on(self, one):
+        block = self.block(one, 0)
+        self.near[one] = {
+            d: self.links.send(block, block, **{"d" + self.second: d}) for d in (1, -1)
+        }
+
+    def to_sibling(self, two):
+        self.siblings.append(self.links.send(self.blocks(two), self.blocks(two), dc=1))
+
+    def begin(self):
+        self.coming = {
+            -d if d != 2 else 2: self.links.send(
+                self.source, self.block(0, 0), **{"d" + self.first: d}
+            )
+            for d in (1, -1, 2)
+        }
+        block = self.block(0, 0)
+        self.near[0] = {
+            d: self.links.send(self.source, block, **{"d" + self.second: d}) for d in (1, -1)
+        }
+
+    def neighbours(self):
+        for one in (-1, 1):
+            self.coming[one].wait_recv()
+            self.pass_on(one)
+
+    def opposite(self):
+        self.coming[2].wait_recv()
+        self.pass_on(2)
+        self.to_sibling(0)
+
+    def onward(self):
+        self.far = []
+        for one, d in ((0, 1), (1, -1), (-1, 1), (2, -1)):
+            self.near[one][d].wait_recv()
+            block = self.block(one, -d)
+            self.far.append(self.links.send(block, block, **{"d" + self.second: d}))
+
+    def rest(self):
+        for one, d in ((0, -1), (1, 1), (-1, -1), (2, 1)):
+            self.near[one][d].wait_recv()
+        self.to_sibling(-1)
+        self.to_sibling(1)
+
+    def end(self):
+        arrived(self.far)
+        self.to_sibling(2)
+
+
+def spread(links, array, home_ref, between):
+    halves = (Spread(links, array, home_ref, "z", 0), Spread(links, array, home_ref, "y", 32))
+    for step in ("begin", "neighbours", "opposite", "onward", "rest", "end"):
+        for half in halves:
+            getattr(half, step)()
+        if step == "opposite":
+            between()
+    return halves[0].siblings + halves[1].siblings
+
+
+class SlotGather:
+    def __init__(self, links, array, first, size):
+        x, y, z, c = links.here
+        self.links, self.array, self.place, self.low = links, array, x, lax.rem(y, 2)
+        self.all = pl.ds(first, size)
+        self.halves = pl.ds(first, size // 2), pl.ds(first + size // 2, size // 2)
+        self.along_y = []
+
+    def part(self, d, rows):
+        return self.array.at[lax.rem(self.place + d + 4, 4), self.low, rows]
+
+    def to_pair(self, d):
+        for rows, step in zip(self.halves, (1, -1)):
+            block = self.part(d, rows)
+            self.along_y.append(self.links.send(block, block, dy=step))
+
+    def begin(self):
+        block = self.part(0, self.all)
+        self.near = {d: self.links.send(block, block, dx=d) for d in (1, -1)}
+        self.to_pair(0)
+
+    def onward(self):
+        self.far = []
+        for rows, d in zip(self.halves, (1, -1)):
+            self.near[d].wait_recv()
+            block = self.part(-d, rows)
+            self.far.append(self.links.send(block, block, dx=d))
+            self.to_pair(-d)
+
+    def end(self):
+        arrived(self.far)
+        self.to_pair(2)
+
+
+def wide_column(segment_row, first):
+    blocks = []
+    for n in range(4):
+        row = segment_row[:, pl.ds(pl.multiple_of(first + n * 128, 128), 128)].astype(F32)
+        block = jnp.broadcast_to(row, (128, 128)).T
+        blocks.append(jnp.concatenate([block] * 4, axis=1))
+    return jnp.concatenate(blocks, axis=0)
+
+
+def own_mask(segment_row, first):
     rows_at = lax.broadcasted_iota(jnp.int32, (ROWS, ROWS), 0)
     cols_at = lax.broadcasted_iota(jnp.int32, (ROWS, ROWS), 1)
-    same = segment_rows[own_first, :] == segment_row[:, own_first]
+    same = wide_column(segment_row, first) == segment_row[:, at(first, ROWS)].astype(F32)
     return jnp.where(same & (rows_at >= cols_at), 0.0, MASKED_SCORE)
 
 
-def earlier_mask(segment_rows, segment_row, own_first):
-    same = segment_rows[own_first, :] == segment_row[:, pl.ds(0, ROWS)]
+def earlier_mask(segment_row, first):
+    same = wide_column(segment_row, first) == segment_row[:, pl.ds(0, ROWS)].astype(F32)
     return jnp.where(same, 0.0, MASKED_SCORE)
 
 
 def front(
-    tok, own_weights, cosine_ref, sine_ref, segment_rows, segment_row, gate, up, down, grad, picked,
-    weights_out, experts_in, experts_out, grad_all, picked_all, moe_in_all,
+    tok, router, gain_pair, query_gain, key_gain, cosine_ref, sine_ref, segment_row, routes,
+    query_weight, key_weight, value_weight, out_weight, gate, up, down, grad,
+    weights_out, others_out, experts_in, experts_out, grad_all, picked_all, moe_in_all,
     normed_out, pre_out, rot_out, kv_out, kv_far, mixed_out, lse_out, hidden_out, home_scale_out,
-    weights, biases, accs, part, part_core, part_z, home_ref,
+    weights, others, picked, stage_in, stage_out, biases, accs, totals, part, part_core, part_z, home_ref,
     send_sems, recv_sems, local_sems,
 ):
     links = Links(send_sems, recv_sems)
@@ -189,15 +263,22 @@
     x_after, x_before = lax.rem(x + 1, 4), lax.rem(x + 3, 4)
     y_after, y_before, y_far = lax.rem(y + 1, 4), lax.rem(y + 3, 4), lax.rem(y + 2, 4)
     own = c * HALF
-    links.greet(STEPS_X + STEPS_Y + STEPS_Z + STEPS_C)
-
-    low, high = pl.ds(0, 128), pl.ds(128, WROWS - 128)
-    slot = weights.at[x, y_low]
-    pair = [
-        links.send(own_weights.at[low], slot.at[low], dy=1),
-        links.send(own_weights.at[high], slot.at[high], dy=-1),
-    ]
-    local = [pltpu.make_async_copy(own_weights, slot, local_sems.at[0])]
+    own_rows = pl.ds(pl.multiple_of(own, HALF), HALF)
+    loads = []
+
+    def load(source, target):
+        copy = pltpu.make_async_copy(source, target, local_sems.at[len(loads)])
+        copy.start()
+        loads.append(copy)
+        return copy
+
+    slot, other_slot = weights.at[x, y_low], others.at[x, y_low]
+    every = pl.ds(0, 256)
+    slot_loads = [
+        load(array, slot.at[every, pl.ds(n * 256, 256)])
+        for n, array in enumerate((query_weight, key_weight, value_weight))
+    ]
+    other_load = load(out_weight, other_slot.at[:, pl.ds(128, 256)])
 
     def mine(array, group):
         return array.at[pl.ds(group * 4, 4)]
@@ -205,30 +286,99 @@
     def columns(place, low_place):
         return pl.ds(pl.multiple_of(place * 512 + low_place * 256, 256), 256)
 
-    local.append(
-        pltpu.make_async_copy(
-            mine(gate, y), experts_in.at[:, x, y_low, :, pl.ds(0, 128)], local_sems.at[1]
-        )
-    )
-    local.append(
-        pltpu.make_async_copy(
-            mine(up, y), experts_in.at[:, x, y_low, :, pl.ds(128, 128)], local_sems.at[2]
-        )
-    )
-    local.append(
-        pltpu.make_async_copy(
-            mine(down, y), experts_out.at[:, :, columns(x, y_low)], local_sems.at[3]
-        )
-    )
-    own_rows = pl.ds(pl.multiple_of(own, HALF), HALF)
-    local.append(pltpu.make_async_copy(grad, grad_all.at[y], local_sems.at[4]))
-    local.append(pltpu.make_async_copy(picked, picked_all.at[y], local_sems.at[5]))
-    for copy in local:
-        copy.start()
-    local[0].wait()
+    staged = [
+        load(mine(gate, y), stage_in.at[:, :, pl.ds(0, 128)]),
+        load(mine(up, y), stage_in.at[:, :, pl.ds(128, 128)]),
+        load(mine(down, y), stage_out),
+    ]
+    lanes = lax.broadcasted_iota(jnp.int32, (16, 128), 1)
+    rows_of = lax.broadcasted_iota(jnp.int32, (16, 128), 0)
+    turned_to = (lanes == (x * 2 + y_low) * 16 + rows_of).astype(BF)
+    head_rows = dot(jnp.concatenate([query_gain[...], key_gain[...]], axis=0), turned_to)
+    gain_block = jnp.concatenate(
+        [
+            gain_pair[...].astype(F32),
+            jnp.concatenate([head_rows, jnp.zeros((4, 128), F32)], axis=1),
+            jnp.zeros((10, 256), F32),
+        ],
+        axis=0,
+    )
+    weights[x, y_low, 256:272, 0:256] = gain_block.astype(BF)
+    weights[x, y_low, 256:272, 256:768] = jnp.zeros((16, 512), BF)
+    others[x, y_low, :, 0:128] = jnp.concatenate(
+        [router[...].astype(F32), jnp.zeros((256, 112), F32)], axis=1
+    ).astype(BF)
+    links.greet(STEPS_X + STEPS_Y + STEPS_Z + STEPS_C)
+    for copy in slot_loads:
+        copy.wait()
+
+    first_rows = pl.ds(0, 80)
+    pair = [
+        links.send(slot.at[pl.ds(0, 48)], slot.at[pl.ds(0, 48)], dy=1),
+        links.send(slot.at[pl.ds(48, 32)], slot.at[pl.ds(48, 32)], dy=-1),
+    ]
+    most = SlotGather(links, weights, 80, WROWS - 80)
+    most.begin()
+    other_load.wait()
+    behind = SlotGather(links, others, 0, 256)
+
+    def grad_block(dy, dz, first=0, size=HOME):
+        start = own + lax.rem(z + dz + 4, 4) * HOME + first
+        return grad_all.at[lax.rem(y + dy + 4, 4), pl.ds(pl.multiple_of(start, 32), size)]
+
+    home_rows = pl.ds(pl.multiple_of(own + z * HOME, HOME), HOME)
+    grad_near = {
+        -d if d != 2 else 2: links.send(grad.at[home_rows], grad_block(0, 0), dy=d)
+        for d in (1, -1, 2)
+    }
+    for copy in staged:
+        copy.wait()
+    place_staged = [
+        load(stage_in, experts_in.at[:, x, y_low]),
+        load(stage_out, experts_out.at[:, :, columns(x, y_low)]),
+    ]
     arrived(pair)
-    near = [links.send(weights.at[x], weights.at[x], dx=d) for d in (1, -1)]
-
+    both = weights.at[x, :, first_rows]
+    near = [links.send(both, both, dx=d) for d in (1, -1)]
+    behind.begin()
+
+    expert_lanes = lax.broadcasted_iota(jnp.int32, (ROWS, 128), 1)
+    marked = expert_lanes == routes[:, 0:1]
+    for k in range(1, 8):
+        marked = marked | (expert_lanes == routes[:, k : k + 1])
+    picked[...] = jnp.where(marked, 1.0, 0.0).T[0:16].astype(BF)
+    place_picked = load(picked, picked_all.at[y])
+    most.onward()
+    first_row = ctx * ROWS
+    own_first = at(first_row, ROWS)
+    biases[0] = own_mask(segment_row, first_row)
+    biases[1] = earlier_mask(segment_row, first_row)
+    far = []
+    for n, (d, place) in enumerate(((1, x_before), (-1, x_after))):
+        near[n].wait_recv()
+        block = weights.at[place, n, first_rows]
+        far.append(links.send(block, block, dx=d))
+    tokens = tok[...].astype(F32)
+    scale_one = rms_scale(tokens)
+    most.end()
+    grad_next = {}
+    for dy in (-1, 1, 2):
+        grad_near[dy].wait_recv()
+        block = grad_block(dy, 0)
+        grad_next[dy] = {d: links.send(block, block, dz=d) for d in (1, -1)}
+    behind.onward()
+
+    def expert_block(place, low_place):
+        return [
+            experts_in.at[:, place, low_place],
+            experts_out.at[:, :, columns(place, low_place)],
+        ]
+
+    for copy in place_staged:
+        copy.wait()
+    expert_near = {
+        d: [links.send(block, block, dx=d) for block in expert_block(x, y_low)] for d in (1, -1)
+    }
     expert_pair = []
     for group, start, step in ((y_after, 0, 1), (y_before, 2, -1)):
         some = pl.ds(group * 4 + start, 2)
@@ -242,35 +392,8 @@
             ),
             links.send(down.at[some], experts_out.at[there, :, columns(x, y_low)], dy=step),
         ]
-    grad_near = [
-        links.send(grad.at[own_rows], grad_all.at[y, own_rows], dy=d) for d in (1, -1)
-    ]
-    picked_near = [links.send(picked, picked_all.at[y], dy=d) for d in (1, -1, 2)]
-
-    own_first = at(ctx * ROWS, ROWS)
-    biases[0] = own_mask(segment_rows, segment_row, own_first)
-    biases[1] = earlier_mask(segment_rows, segment_row, own_first)
-    tokens = tok[...].astype(F32)
-    scale_one = rms_scale(tokens)
-
-    near[0].wait_recv()
-    far = [links.send(weights.at[x_before, 0], weights.at[x_before, 0], dx=1)]
-    near[1].wait_recv()
-    far.append(links.send(weights.at[x_after, 1], weights.at[x_after, 1], dx=-1))
+    arrived(most.along_y)
     arrived(far)
-    for copy in local[1:4]:
-        copy.wait()
-    arrived(expert_pair)
-
-    def expert_blocks(place, low_place=None):
-        if low_place is None:
-            cols = pl.ds(pl.multiple_of(place * 512, 512), 512)
-            return experts_in.at[:, place], experts_out.at[:, :, cols]
-        return experts_in.at[:, place, low_place], experts_out.at[:, :, columns(place, low_place)]
-
-    expert_near = [
-        [links.send(block, block, dx=d) for block in expert_blocks(x)] for d in (1, -1)
-    ]
 
     gain_blocks = [weights[s // 2, s % 2, 256:272, 0:256].astype(F32) for s in range(8)]
     gains = jnp.concatenate([block[0:1] for block in gain_blocks], axis=1)
@@ -302,35 +425,31 @@
         later.start()
         kv_far[...] = jnp.zeros_like(kv_far)
 
+    picked_near = [links.send(picked, picked_all.at[y], dy=d) for d in (1, -1, 2)]
     query_pre = project(0)
     pre_out[:, 0:256] = query_pre
     heads(query_pre, 2, 0)
     score_scale = 128 ** (-0.5)
-    peaks, totals = [], []
     for h in range(2):
         lane = slice(h * 128, h * 128 + 128)
         scores = dot_nt(rot_out[:, lane], kv_out[:, lane]) * score_scale + biases[0]
         peak = jnp.max(scores, axis=-1, keepdims=True)
         exponents = jnp.exp(scores - peak)
         lse_out[h] = jnp.broadcast_to(peak, (ROWS, 128))
-        lse_out[2 + h] = jnp.broadcast_to(
-            jnp.sum(exponents, axis=-1, keepdims=True), (ROWS, 128)
-        )
+        totals[h] = jnp.broadcast_to(jnp.sum(exponents, axis=-1, keepdims=True), (ROWS, 128))
         accs[h] = dot(exponents.astype(BF), kv_out[:, 256 + h * 128 : 384 + h * 128])
 
-    arrived(grad_near)
-    grad_lane = grad_all.at[:, own_rows]
-    quarter = pl.multiple_of(own, HALF)
-    first_half, second_half = pl.ds(quarter, 128), pl.ds(pl.multiple_of(quarter + 128, 128), 128)
-    grad_far = [
-        links.send(grad_all.at[y_before, first_half], grad_all.at[y_before, first_half], dy=1),
-        links.send(grad_all.at[y_after, second_half], grad_all.at[y_after, second_half], dy=-1),
-    ]
-    siblings = [
-        links.send(grad_all.at[place, own_rows], grad_all.at[place, own_rows], dc=1)
-        for place in (y_before, y_after)
-    ]
-
+    behind.end()
+    grad_far = []
+    for dy in (-1, 1, 2):
+        for d, first in ((1, 0), (-1, 32)):
+            grad_next[dy][d].wait_recv()
+            block = grad_block(dy, -d, first, 32)
+            grad_far.append(links.send(block, block, dz=d))
+    arrived(expert_pair)
+    expert_pair_near = {
+        d: [links.send(block, block, dx=d) for block in expert_block(x, 1 - y_low)] for d in (1, -1)
+    }
     @pl.when(ctx == 1)
     def _():
         later.wait_recv()
@@ -342,25 +461,27 @@
             exponents = jnp.exp(scores - peak)
             old = jnp.exp(old_peak - peak)
             lse_out[h] = jnp.broadcast_to(peak, (ROWS, 128))
-            lse_out[2 + h] = lse_out[2 + h] * old + jnp.sum(exponents, axis=-1, keepdims=True)
+            totals[h] = totals[h] * old + jnp.sum(exponents, axis=-1, keepdims=True)
             accs[h] = accs[h] * old + dot(
                 exponents.astype(BF), kv_far[:, 256 + h * 128 : 384 + h * 128]
             )
 
     for h in range(2):
-        total = lse_out[2 + h]
+        total = totals[h]
         mixed_out[:, h * 128 : h * 128 + 128] = (accs[h] / total).astype(BF)
         lse_out[h] = lse_out[h] + jnp.log(total)
 
+    quarter = pl.multiple_of(own, HALF)
+    arrived(behind.along_y)
     other = pl.multiple_of((1 - c) * HALF, HALF)
     give_rows = mixed_out[pl.ds(other, HALF), :]
     for s in range(8):
-        block = weights[s // 2, s % 2, 0:256, 896:1152]
+        block = others[s // 2, s % 2, :, 128:384]
         part[1, :, s * 256 : s * 256 + 256] = dot(give_rows, block).astype(BF)
     core_sum = links.send(part.at[1], part_core, dc=1)
     keep_rows = mixed_out[pl.ds(quarter, HALF), :]
     for s in range(8):
-        block = weights[s // 2, s % 2, 0:256, 896:1152]
+        block = others[s // 2, s % 2, :, 128:384]
         part[0, :, s * 256 : s * 256 + 256] = dot(keep_rows, block).astype(BF)
     core_sum.wait_recv()
     part[0] = (part[0].astype(F32) + part_core[...].astype(F32)).astype(BF)
@@ -369,16 +490,14 @@
         there = pl.multiple_of(lax.rem(z + d + 4, 4) * HOME, HOME)
         z_sum.append(links.send(part.at[0, pl.ds(there, HOME)], part_z.at[k], dz=d))
 
-    for copies in expert_near:
-        arrived(copies)
-    expert_far = [links.send(block, block, dx=1) for block in expert_blocks(x_before, 0)]
-    expert_far += [links.send(block, block, dx=-1) for block in expert_blocks(x_after, 1)]
     arrived(grad_far)
-    siblings.append(links.send(grad_all.at[y_far, own_rows], grad_all.at[y_far, own_rows], dc=1))
-
+    siblings = [
+        links.send(grad_all.at[place, own_rows], grad_all.at[place, own_rows], dc=1)
+        for place in (y_before, y_after, y_far)
+    ]
+    arrived(expert_near[1] + expert_near[-1])
+    expert_far = [links.send(block, block, dx=1) for block in expert_block(x_before, y_low)]
     arrived(z_sum)
-    home_first = pl.multiple_of(quarter + z * HOME, HOME)
-    home_rows = pl.ds(home_first, HOME)
     summed = part[0, pl.ds(pl.multiple_of(z * HOME, HOME), HOME), :].astype(F32)
     for k in range(3):
         summed = summed + part_z[k].astype(F32)
@@ -387,18 +506,23 @@
     hidden_out[...] = hidden
     home_scale_out[...] = jnp.broadcast_to(rms_scale(home_tokens), (HOME, 128))
     home_ref[...] = (hidden * rms_scale(hidden) * moe_gains).astype(BF)
-    place_home = pltpu.make_async_copy(home_ref, moe_in_all.at[y, c, z], local_sems.at[6])
-    place_home.start()
-    keep_weights = pltpu.make_async_copy(weights, weights_out, local_sems.at[7])
-    keep_weights.start()
+    place_home = load(home_ref, moe_in_all.at[y, c, z])
+    keep_weights = [load(weights, weights_out), load(others, others_out)]
     place_home.wait()
-    siblings += spread(links, moe_in_all, home_ref, y, z, c)
+
+    def onward():
+        arrived(expert_pair_near[1] + expert_pair_near[-1])
+        expert_far.extend(
+            links.send(block, block, dx=-1) for block in expert_block(x_after, 1 - y_low)
+        )
+
+    siblings += spread(links, moe_in_all, home_ref, lambda: onward())
     arrived(expert_far)
     arrived(picked_near)
     arrived(siblings)
-    local[4].wait()
-    local[5].wait()
-    keep_weights.wait()
+    place_picked.wait()
+    for copy in keep_weights:
+        copy.wait()
 
     for copy in links.made:
         if copy is not later:
@@ -409,17 +533,18 @@
         later.wait_send()
 
 
-FRONT_COPIES = 6 + 14 + 8 + 3 + 1 + 4 + 24
-
-
-def run_front(tok, own_weights, tables, segments, gate, up, down, grad, picked):
+FRONT_COPIES = 6 + 12 + 12 + 18 + 18 + 3 + 1 + 4 + 38
+
+
+def run_front(vmem, hbm):
     shape = jax.ShapeDtypeStruct
     outs = (
-        (shape((4, 2, WROWS, WCOLS), BF), ANY),
+        (shape((4, 2, WROWS, 768), BF), ANY),
+        (shape((4, 2, 256, 384), BF), ANY),
         (shape((4, 4, 2, 256, 256), BF), ANY),
         (shape((4, 128, WIDTH), BF), ANY),
         (shape((4, ROWS, WIDTH), BF), ANY),
-        (shape((4, ROWS, 128), BF), ANY),
+        (shape((4, 16, ROWS), BF), ANY),
         (shape((4, 2, 4, HOME, WIDTH), BF), ANY),
         (shape((ROWS, WIDTH), BF), VMEM),
         (shape((ROWS, 512), F32), VMEM),
@@ -427,18 +552,23 @@
         (shape((ROWS, 512), BF), VMEM),
         (shape((ROWS, 512), BF), VMEM),
         (shape((ROWS, 256), BF), VMEM),
-        (shape((4, ROWS, 128), F32), VMEM),
+        (shape((2, ROWS, 128), F32), VMEM),
         (shape((HOME, WIDTH), F32), VMEM),
         (shape((HOME, 128), F32), VMEM),
     )
     return pl.pallas_call(
         front,
         out_shape=[o for o, _ in outs],
-        in_specs=[VMEM] * 6 + [ANY] * 5,
+        in_specs=[VMEM] * len(vmem) + [ANY] * len(hbm),
         out_specs=[spec for _, spec in outs],
         scratch_shapes=[
-            pltpu.VMEM((4, 2, WROWS, WCOLS), BF),
+            pltpu.VMEM((4, 2, WROWS, 768), BF),
+            pltpu.VMEM((4, 2, 256, 384), BF),
+            pltpu.VMEM((16, ROWS), BF),
+            pltpu.VMEM((4, 256, 256), BF),
+            pltpu.VMEM((4, 128, 256), BF),
             pltpu.VMEM((2, ROWS, ROWS), F32),
+            pltpu.VMEM((2, ROWS, 128), F32),
             pltpu.VMEM((2, ROWS, 128), F32),
             pltpu.VMEM((2, HALF, WIDTH), BF),
             pltpu.VMEM((HALF, WIDTH), BF),
@@ -446,25 +576,13 @@
             pltpu.VMEM((HOME, WIDTH), BF),
             pltpu.SemaphoreType.DMA((FRONT_COPIES,)),
             pltpu.SemaphoreType.DMA((FRONT_COPIES,)),
-            pltpu.SemaphoreType.DMA((8,)),
+            pltpu.SemaphoreType.DMA((16,)),
         ],
         compiler_params=pltpu.CompilerParams(
             collective_id=1, has_side_effects=True, vmem_limit_bytes=56 * MIB
         ),
         name="front",
-    )(
-        tok,
-        own_weights,
-        jnp.asarray(tables[0]),
-        jnp.asarray(tables[1]),
-        segments.reshape(-1, 1),
-        segments,
-        gate,
-        up,
-        down,
-        grad,
-        picked,
-    )
+    )(*vmem, *hbm)
 
 
 MCOLS = 1664
@@ -472,78 +590,95 @@
 
 def scatter_buffers():
     return [
-        pltpu.VMEM((4, HALF, WIDTH), BF),
+        pltpu.VMEM((2, HALF, WIDTH), BF),
         pltpu.VMEM((2, 2, 32, WIDTH), BF),
         pltpu.VMEM((2, 4, 32, WIDTH), BF),
         pltpu.VMEM((3, 32, WIDTH), BF),
-        pltpu.VMEM((4, 3, 32, WIDTH), BF),
+        pltpu.VMEM((4, 2, 16, WIDTH), BF),
+        pltpu.VMEM((4, 2, 32, WIDTH), BF),
         pltpu.VMEM((3, 32, WIDTH), BF),
     ]
 
 
 class TokenSum:
-    def __init__(self, links, give, keep, landings):
-        self.links, self.give, self.keep = links, give, keep
-        self.core_in, self.p_one_in, self.p_two_in, self.p_three_in, self.q_one_in, self.q_two_in = landings
-        self.core, self.p_one, self.p_two, self.q_one, self.q_two = {}, [], [], {}, []
-
-    def give_slot(self, k):
-        slots = self.give.shape[0]
-        if k >= slots:
-            self.links.left(self.core[k - slots])
-        return k % slots
+    def __init__(self, links, give, keep, landings, credit):
+        self.links, self.give, self.keep, self.credit = links, give, keep, credit
+        (
+            self.core_in, self.p_one_in, self.p_two_in, self.p_three_in,
+            self.q_one_in, self.q_two_in, self.q_three_in,
+        ) = landings
+        self.core, self.p_one, self.p_two, self.q_one, self.q_two, self.q_three = {}, [], [], {}, {}, []
+
+    def free(self, k):
+        if k:
+            self.links.left(self.core[k - 1])
 
     def give_core(self, k):
-        self.core[k] = self.links.send(
-            self.give.at[k % self.give.shape[0]], self.core_in.at[k], dc=1
-        )
-
-    def q_part(self, k, place):
-        return self.keep.at[k, at(place * HOME + 32, 32)]
+        if k >= 2:
+            pl.semaphore_wait(self.credit, 1)
+        self.core[k] = self.links.send(self.give, self.core_in.at[k % 2], dc=1)
+
+    def q_rows(self, d, first=0, size=32):
+        place = lax.rem(self.links.here[2] + d + 4, 4)
+        return pl.ds(pl.multiple_of(place * HOME + 32 + first, 16), size)
 
     def add(self, k):
         links, keep = self.links, self.keep
-        z = links.here[2]
         self.core[k].wait_recv()
-        keep[k] = (keep[k].astype(F32) + self.core_in[k].astype(F32)).astype(BF)
+        keep[k] = keep[k] + self.core_in[k % 2]
+        if k < 2:
+            x, y, z, c = links.here
+            pl.semaphore_signal(
+                self.credit,
+                inc=1,
+                device_id=device(x, y, z, c + 1),
+                device_id_type=pl.DeviceIdType.MESH,
+            )
         self.q_one[k] = [
-            links.send(
-                self.q_part(k, lax.rem(z + d + 4, 4)), self.q_one_in.at[k, n], dz=d
-            )
-            for n, d in enumerate((1, -1, 2))
+            links.send(keep.at[k, self.q_rows(2, 16 * n, 16)], self.q_one_in.at[k, n], dz=d)
+            for n, d in enumerate((1, -1))
         ]
-        rows = keep.at[k].reshape(4, HOME, WIDTH)
-        first = pl.ds(0, 32)
         if k == 0:
+            rows = keep.at[0].reshape(4, HOME, WIDTH)
+            first = pl.ds(0, 32)
             self.p_one = [
                 links.send(rows.at[pl.ds(0, 2), first], self.p_one_in.at[0], dy=1),
                 links.send(rows.at[pl.ds(2, 2), first], self.p_one_in.at[1], dy=-1),
             ]
-        elif k < 3:
-            n = k - 1
-            self.p_one[n].wait_recv()
-            for i in range(2):
-                row = (2 * n + i) * HOME
-                keep[k, row : row + 32] = (
-                    keep[k, row : row + 32].astype(F32) + self.p_one_in[n, i].astype(F32)
-                ).astype(BF)
-            self.p_two.append(
-                links.send(rows.at[:, first], self.p_two_in.at[n], dy=(1, -1)[n])
+
+    def p_step(self, k):
+        links, keep, n = self.links, self.keep, k - 1
+        self.p_one[n].wait_recv()
+        for i in range(2):
+            row = (2 * n + i) * HOME
+            keep[k, row : row + 32] = keep[k, row : row + 32] + self.p_one_in[n, i]
+        rows = keep.at[k].reshape(4, HOME, WIDTH)
+        self.p_two.append(
+            links.send(rows.at[:, pl.ds(0, 32)], self.p_two_in.at[n], dy=(1, -1)[n])
+        )
+
+    def second(self, k):
+        links, keep = self.links, self.keep
+        self.q_two[k] = []
+        for n, d in enumerate((1, -1)):
+            self.q_one[k][n].wait_recv()
+            rows = self.q_rows(d, 16 * n, 16)
+            keep[k, rows, :] = keep[k, rows, :] + self.q_one_in[k, n]
+            self.q_two[k].append(
+                links.send(keep.at[k, self.q_rows(d)], self.q_two_in.at[k, n], dz=d)
             )
 
     def q_sum(self, k):
-        z = self.links.here[2]
-        for copy in self.q_one[k]:
-            copy.wait_recv()
-        part = self.keep[k, at(z * HOME + 32, 32), :].astype(F32)
-        for n in range(3):
-            part = part + self.q_one_in[k, n].astype(F32)
+        arrived(self.q_two[k])
+        part = self.keep[k, self.q_rows(0), :].astype(F32)
+        for n in range(2):
+            part = part + self.q_two_in[k, n].astype(F32)
         return part
 
-    def q_send(self, k, buffer):
+    def third(self, k, buffer):
         buffer[k] = self.q_sum(k).astype(BF)
-        self.q_two.append(
-            self.links.send(buffer.at[k], self.q_two_in.at[k], dy=(2, 1, -1)[k])
+        self.q_three.append(
+            self.links.send(buffer.at[k], self.q_three_in.at[k], dy=(2, 1, -1)[k])
         )
 
     def p_send(self):
@@ -567,9 +702,9 @@
     def home(self):
         z = self.links.here[2]
         second = self.q_sum(3)
-        arrived(self.q_two)
+        arrived(self.q_three)
         for n in range(3):
-            second = second + self.q_two_in[n].astype(F32)
+            second = second + self.q_three_in[n].astype(F32)
         arrived(self.p_three)
         first = self.keep[3, at(z * HOME, 32), :].astype(F32)
         for n in range(3):
@@ -577,7 +712,7 @@
         return first, second
 
 
-TOKEN_SUM_COPIES = 4 + 12 + 2 + 2 + 3 + 3
+TOKEN_SUM_COPIES = 4 + 8 + 8 + 2 + 2 + 3 + 3
 
 
 def spread_home(links, array, home_ref):
@@ -586,12 +721,13 @@
 
 
 def experts(
-    x_all, g_all, picked_all, w_in_hbm, w_out_hbm, weights, hidden_ref,
-    gated_out, grad_out, grad_near_out, low_all, hidden_grad_out, gain_out,
+    x_all, g_all, picked_all, own_grad, w_in_hbm, w_out_hbm, weights, others, hidden_ref,
+    grad_out, grad_near_out, low_all, hidden_grad_out, gain_out, layer_out,
     w_in, w_out, gain_ref, x_ref, g_ref, picked_ref, gates_ref, gate_grad_ref, back_ref, pre_ref,
-    gated_ref, give, keep, grad_ref, q_buffer, home_ref,
-    core_in, p_one_in, p_two_in, p_three_in, q_one_in, q_two_in,
-    send_sems, recv_sems, local_sems,
+    gated_ref, give, keep, keep_layer, grad_far, grad_stage, q_buffer, q_layer, home_ref,
+    core_in, p_one_in, p_two_in, p_three_in, q_one_in, q_two_in, q_three_in,
+    core_layer, p_one_layer, p_two_layer, p_three_layer, q_one_layer, q_two_layer, q_three_layer,
+    credits, send_sems, recv_sems, local_sems,
 ):
     links = Links(send_sems, recv_sems)
     x, y, z, c = links.here
@@ -607,21 +743,34 @@
 
     first = [load(g_all.at[order[0]], g_ref.at[0]), load(w_out_hbm, w_out)]
     first += [load(picked_all.at[place], picked_ref.at[k]) for k, place in enumerate(order)]
-    first.append(load(weights.at[:, :, pl.ds(0, 256), pl.ds(768, 128)], w_in.at[:, :, :, pl.ds(1024, 128)]))
+    first.append(load(others.at[:, :, :, pl.ds(0, 128)], w_in.at[:, :, :, pl.ds(1024, 128)]))
     first.append(load(weights.at[:, :, pl.ds(256, 16), pl.ds(0, 256)], gain_ref))
     first.append(load(x_all.at[order[0]], x_ref.at[0]))
     first += [
         load(w_in_hbm.at[e], w_in.at[:, :, :, pl.ds(e * 256, 256)]) for e in range(4)
     ]
     rest = [
-        [load(g_all.at[order[k]], g_ref.at[k]), load(x_all.at[order[k]], x_ref.at[k])]
+        [
+            load(g_all.at[order[k]] if k < 3 else own_grad, g_ref.at[k]),
+            load(x_all.at[order[k]], x_ref.at[k]),
+        ]
         for k in range(1, 4)
     ]
     links.greet(STEPS_X + STEPS_Y + STEPS_Z + STEPS_C)
     for copy in first:
         copy.wait()
 
-    sums = TokenSum(links, give, keep, (core_in, p_one_in, p_two_in, p_three_in, q_one_in, q_two_in))
+    sums = TokenSum(
+        links, give.at[0], keep,
+        (core_in, p_one_in, p_two_in, p_three_in, q_one_in, q_two_in, q_three_in), credits.at[0],
+    )
+    layer_sums = TokenSum(
+        links, give.at[1], keep_layer,
+        (
+            core_layer, p_one_layer, p_two_layer, p_three_layer, q_one_layer, q_two_layer, q_three_layer,
+        ),
+        credits.at[1],
+    )
     lanes = lax.broadcasted_iota(jnp.int32, (ROWS, 128), 1)
     own_rows = at(c * HALF, HALF)
     other_rows = at((1 - c) * HALF, HALF)
@@ -634,14 +783,20 @@
             for copy in rest[k - 1]:
                 copy.wait()
         logits = dot(x_ref[k], in_block(1024, 128))
-        logits = jnp.where(picked_ref[k].astype(F32) > 0.5, logits, MASKED_SCORE)
+        marks = jnp.concatenate([picked_ref[k].astype(F32), jnp.zeros((112, ROWS), F32)], axis=0)
+        logits = jnp.where(marks.T > 0.5, logits, MASKED_SCORE)
         exponents = jnp.exp(logits - jnp.max(logits, axis=-1, keepdims=True))
         gates_ref[...] = exponents / jnp.sum(exponents, axis=-1, keepdims=True)
         gate_grad_ref[...] = jnp.zeros_like(gate_grad_ref)
         back_ref[...] = dot_nt(g_ref[k], w_out[...].reshape(512, WIDTH))
 
-        def one_expert(e, carry, k=k):
-            joined = dot(x_ref[k], in_block(pl.multiple_of(e * 256, 256), 256))
+        def two_experts(pair, carry, k=k):
+            joined = dot(x_ref[k], in_block(pl.multiple_of(pair * 512, 512), 512))
+            for n in range(2):
+                one_expert(pair * 2 + n, joined[:, n * 256 : n * 256 + 256])
+            return carry
+
+        def one_expert(e, joined, k=k):
             gate_pre, up_pre = joined[:, :128], joined[:, 128:]
             logistic = 1.0 / (1.0 + jnp.exp(-gate_pre))
             silu_gate = gate_pre * logistic
@@ -660,49 +815,60 @@
                 act_grad * silu_gate
             ).astype(BF)
             gated_ref[k, :, at(e * 128, 128)] = (act * gate).astype(BF)
-            return carry
-
-        lax.fori_loop(0, 4, one_expert, 0)
+
+        lax.fori_loop(0, 2, two_experts, 0)
         gates, gate_grad = gates_ref[...], gate_grad_ref[...]
         logit_grad = gates * (gate_grad - jnp.sum(gates * gate_grad, axis=-1, keepdims=True))
         pre_ref[k, :, 1024:1152] = logit_grad.astype(BF)
 
         def back_rows(rows, target, k=k):
-            def one_block(s, carry):
-                block = w_in[s // 2, lax.rem(s, 2)]
-                target[k, :, at(s * 256, 256)] = dot_nt(pre_ref[k, rows, :], block).astype(BF)
-                return carry
-
-            lax.fori_loop(0, 8, one_block, 0)
-
-        back_rows(other_rows, give)
+            for s in range(0, 4, 2):
+                block = w_in[s : s + 2].reshape(1024, 1152)
+                target[:, s * 512 : s * 512 + 1024] = dot_nt(pre_ref[k, rows, :], block).astype(BF)
+
+        def layer_rows(rows, target, k=k):
+            for s in range(0, WIDTH, 1024):
+                block = w_out[:, :, s : s + 1024].reshape(512, 1024)
+                target[:, s : s + 1024] = dot(gated_ref[k, rows, :], block).astype(BF)
+
+        sums.free(k)
+        back_rows(other_rows, give.at[0])
         sums.give_core(k)
-        back_rows(own_rows, keep)
-        if k:
-            sums.q_send(k - 1, q_buffer)
+        layer_sums.free(k)
+        layer_rows(other_rows, give.at[1])
+        layer_sums.give_core(k)
+        back_rows(own_rows, keep.at[k])
+        layer_rows(own_rows, keep_layer.at[k])
         sums.add(k)
+        if k in (1, 2):
+            sums.p_step(k)
+        layer_sums.add(k)
+        if k > 0:
+            sums.second(k - 1)
+            layer_sums.second(k - 1)
+        if k > 1:
+            layer_sums.p_step(k - 1)
+            sums.third(k - 2, q_buffer)
+            layer_sums.third(k - 2, q_layer)
+    sums.second(3)
+    sums.third(2, q_buffer)
     sums.p_send()
-    keep_gated = pltpu.make_async_copy(gated_ref, gated_out, local_sems.at[len(loads)])
-    keep_gated.start()
-
-    def weight_grad(slot):
+
+    def weight_grad(slot, target):
         columns = at(slot * 256, 256)
         rows = x_ref[:, :, columns].reshape(4 * ROWS, 256)
-        grad_ref[slot, :, 0:1152] = dot_tn(rows, pre_ref[...].reshape(4 * ROWS, 1152)).astype(BF)
+        target[:, 0:1152] = dot_tn(rows, pre_ref[...].reshape(4 * ROWS, 1152)).astype(BF)
         rows = g_ref[:, :, columns].reshape(4 * ROWS, 256)
-        grad_ref[slot, :, 1152:MCOLS] = dot_tn(rows, gated_ref[...].reshape(4 * ROWS, 512)).astype(BF)
-
-    def weight_grads(place):
-        def one_slot(i, carry):
-            weight_grad(place * 2 + i)
-            return carry
-
-        lax.fori_loop(0, 2, one_slot, 0)
-
-    weight_grads(x_far)
+        target[:, 1152:MCOLS] = dot_tn(rows, gated_ref[...].reshape(4 * ROWS, 512)).astype(BF)
+
+    def far_slot(i, carry):
+        weight_grad(x_far * 2 + i, grad_far.at[i])
+        return carry
+
+    lax.fori_loop(0, 2, far_slot, 0)
     near = [
-        links.send(grad_ref.at[x_far * 2], grad_near_out.at[0], dx=1),
-        links.send(grad_ref.at[x_far * 2 + 1], grad_near_out.at[1], dx=-1),
+        links.send(grad_far.at[0], grad_near_out.at[0], dx=1),
+        links.send(grad_far.at[1], grad_near_out.at[1], dx=-1),
     ]
 
     moe_gains = jnp.concatenate(
@@ -716,44 +882,62 @@
     hidden_grad_out[...] = hidden_grad
     gain_out[...] = jnp.broadcast_to(jnp.sum(gain_rows, axis=0, keepdims=True), (8, WIDTH))
     home_ref[...] = hidden_grad.astype(BF)
-    place_home = pltpu.make_async_copy(home_ref, low_all.at[c, z], local_sems.at[len(loads) + 1])
-    place_home.start()
+    place_home = load(home_ref, low_all.at[c, z])
     low_near = spread_home(links, low_all, home_ref)
+    layer_sums.second(3)
+    layer_sums.third(2, q_layer)
+    layer_sums.p_send()
+
+    first_sem = len(loads)
+
+    def stage(i, n):
+        slot = lax.rem(x_far * 2 + 2 + 2 * i + n, 8)
+        return pltpu.make_async_copy(
+            grad_stage.at[n], grad_out.at[slot], local_sems.at[first_sem + n]
+        )
 
     def other_grads(i, carry):
-        weight_grad(lax.rem(x_far * 2 + 2 + i, 8))
+        for n in range(2):
+
+            @pl.when(i > 0)
+            def _():
+                stage(i - 1, n).wait()
+
+            weight_grad(lax.rem(x_far * 2 + 2 + 2 * i + n, 8), grad_stage.at[n])
+            stage(i, n).start()
         return carry
 
-    lax.fori_loop(0, 6, other_grads, 0)
+    lax.fori_loop(0, 2, other_grads, 0)
     arrived(low_near)
     place_home.wait()
     sibling = links.send(low_all.at[c], low_all.at[c], dc=1)
-    keep_grad = pltpu.make_async_copy(grad_ref, grad_out, local_sems.at[len(loads) + 2])
-    keep_grad.start()
+    layer_grad = jnp.concatenate(layer_sums.home(), axis=0)
+    layer_out[...] = (hidden_ref[...] + layer_grad).astype(BF)
+    other_grads(2, 0)
+    for n in range(2):
+        stage(2, n).wait()
     arrived(near)
     sibling.wait_recv()
-    keep_gated.wait()
-    keep_grad.wait()
     links.finish()
 
 
-EXPERT_COPIES = TOKEN_SUM_COPIES + 2 + 3 + 1
-
-
-def run_experts(moe_in_all, grad_all, picked_all, experts_in, experts_out, weights, hidden):
+EXPERT_COPIES = 2 * TOKEN_SUM_COPIES + 2 + 3 + 1
+
+
+def run_experts(moe_in_all, *rest):
     shape = jax.ShapeDtypeStruct
     outs = (
-        (shape((4, ROWS, 512), BF), ANY),
         (shape((8, 256, MCOLS), BF), ANY),
         (shape((2, 256, MCOLS), BF), ANY),
         (shape((2, 4, HOME, WIDTH), BF), ANY),
         (shape((HOME, WIDTH), F32), VMEM),
         (shape((8, WIDTH), F32), VMEM),
+        (shape((HOME, WIDTH), BF), VMEM),
     )
     return pl.pallas_call(
         experts,
         out_shape=[o for o, _ in outs],
-        in_specs=[ANY] * 6 + [VMEM],
+        in_specs=[ANY] * 8 + [VMEM],
         out_specs=[spec for _, spec in outs],
         scratch_shapes=[
             pltpu.VMEM((4, 2, 256, 1152), BF),
@@ -761,18 +945,23 @@
             pltpu.VMEM((4, 2, 16, 256), BF),
             pltpu.VMEM((4, ROWS, WIDTH), BF),
             pltpu.VMEM((4, ROWS, WIDTH), BF),
-            pltpu.VMEM((4, ROWS, 128), BF),
+            pltpu.VMEM((4, 16, ROWS), BF),
             pltpu.VMEM((ROWS, 128), F32),
             pltpu.VMEM((ROWS, 128), F32),
             pltpu.VMEM((ROWS, 512), F32),
             pltpu.VMEM((4, ROWS, 1152), BF),
             pltpu.VMEM((4, ROWS, 512), BF),
+            pltpu.VMEM((2, HALF, WIDTH), BF),
             pltpu.VMEM((4, HALF, WIDTH), BF),
             pltpu.VMEM((4, HALF, WIDTH), BF),
-            pltpu.VMEM((8, 256, MCOLS), BF),
+            pltpu.VMEM((2, 256, MCOLS), BF),
+            pltpu.VMEM((2, 256, MCOLS), BF),
+            pltpu.VMEM((3, 32, WIDTH), BF),
             pltpu.VMEM((3, 32, WIDTH), BF),
             pltpu.VMEM((HOME, WIDTH), BF),
             *scatter_buffers(),
+            *scatter_buffers(),
+            pltpu.SemaphoreType.REGULAR((2,)),
             pltpu.SemaphoreType.DMA((EXPERT_COPIES,)),
             pltpu.SemaphoreType.DMA((EXPERT_COPIES,)),
             pltpu.SemaphoreType.DMA((24,)),
@@ -783,12 +972,7 @@
         name="experts",
     )(
         moe_in_all.reshape(4, ROWS, WIDTH),
-        grad_all,
-        picked_all,
-        experts_in,
-        experts_out,
-        weights,
-        hidden,
+        *rest,
     )
 
 
@@ -796,17 +980,16 @@
 
 
 def back(
-    grad_moe, grad_near, low_hbm, weights, mixed_hbm, rot_hbm, kv_hbm, kv_far_hbm, lse_hbm, pre_hbm,
-    normed_hbm, gated_hbm, w_out_hbm, tok_hbm,
-    hidden_ref, hidden_grad_ref, home_scale_ref, gain_ref, cosine_ref, sine_ref, segment_rows, segment_row,
+    grad_moe, grad_near, low_hbm, weights, others, mixed_hbm, rot_hbm, kv_hbm, kv_far_hbm, lse_hbm, pre_hbm,
+    normed_hbm, tok_hbm,
+    layer_ref, hidden_grad_ref, home_scale_ref, gain_ref, cosine_ref, sine_ref, segment_row,
     layer_all, input_all, groups_in, groups_out, moe_in,
     grad_q, grad_k, grad_v, grad_o, small_out, heads_out,
-    w_ref, w_gains, low, mixed, rot, kv, kv_far, lse, pre, gated, w_out, home_tok,
+    w_ref, w_gains, low, mixed, rot, kv, kv_far, lse, pre, home_tok,
     bias, mixed_grad, dq, dkv, kv_give, kv_got, stacked,
     moe_after, moe_before, moe_near, pay_in, pay_out,
     attn_grad, attn_one, attn_two, attn_give, attn_keep, attn_y_one, attn_y_two,
-    part, part_core, part_z, home_in, home_layer,
-    give, keep, q_buffer, core_in, p_one_in, p_two_in, p_three_in, q_one_in, q_two_in,
+    part, part_core, part_z, home_in,
     sums_ref, sums_x, sums_y, pair_ref, small_ref, small_z, small_c, routed,
     send_sems, recv_sems, local_sems,
 ):
@@ -834,22 +1017,18 @@
     every = pl.ds(0, 256)
     out_loads = [
         load(low_hbm, low),
-        load(weights.at[:, :, every, pl.ds(896, 256)], w_ref.at[:, :, :, pl.ds(768, 256)]),
+        load(others.at[:, :, :, pl.ds(128, 256)], w_ref.at[:, :, :, pl.ds(768, 256)]),
         load(mixed_hbm, mixed),
         load(rot_hbm, rot),
         load(kv_hbm, kv),
         load(kv_far_hbm, kv_far),
-        load(lse_hbm.at[pl.ds(0, 2)], lse),
+        load(lse_hbm, lse),
     ]
     next_loads = [
         load(pre_hbm, pre),
         load(weights.at[:, :, every, pl.ds(0, 768)], w_ref.at[:, :, :, pl.ds(0, 768)]),
         load(weights.at[:, :, pl.ds(256, 16), every], w_gains),
         load(tok_hbm.at[at(c * HALF + z * HOME, HOME)], home_tok),
-    ]
-    last_loads = [
-        load(gated_hbm, gated),
-        load(w_out_hbm, w_out),
     ]
     links.greet(STEPS_X + [(2, 0, 0, 0)] + STEPS_Y + STEPS_Z + STEPS_C)
 
@@ -861,6 +1040,9 @@
     moe_two.append(links.send(moe_before, moe_in.at[1], dx=-1))
     moe_own = moe_near
     own_load = load(pair_of(grad_moe, x), moe_own)
+
+    place_layer = load(layer_ref, layer_all.at[c, z])
+    layer_near = spread_home(links, layer_all, layer_ref)
 
     own_first = at(ctx * ROWS, ROWS)
     for copy in out_loads:
@@ -896,7 +1078,7 @@
 
     @pl.when(ctx == 1)
     def _():
-        bias[...] = earlier_mask(segment_rows, segment_row, own_first)
+        bias[...] = earlier_mask(segment_row, ctx * ROWS)
         for h in range(2):
             query_part, key_part, value_part = scores_back(h, kv_far)
             dq[:, h * 128 : h * 128 + 128] = query_part
@@ -908,7 +1090,7 @@
     def _():
         dq[...] = jnp.zeros_like(dq)
 
-    bias[...] = own_mask(segment_rows, segment_row, own_first)
+    bias[...] = own_mask(segment_row, ctx * ROWS)
     for h in range(2):
         query_part, key_part, value_part = scores_back(h, kv)
         dq[:, h * 128 : h * 128 + 128] += query_part
@@ -989,29 +1171,9 @@
         return carry
 
     lax.fori_loop(0, 6, other_blocks, 0)
-
-    for copy in last_loads:
-        copy.wait()
-    sums = TokenSum(links, give, keep, (core_in, p_one_in, p_two_in, p_three_in, q_one_in, q_two_in))
-
-    def expert_rows(k, rows, target):
-        def one_block(s, carry):
-            block = w_out[:, :, at(s * 256, 256)].reshape(512, 256)
-            target[:, at(s * 256, 256)] = dot(gated[k, rows, :], block).astype(BF)
-            return carry
-
-        lax.fori_loop(0, 8, one_block, 0)
-
-    def expert_chunk(k):
-        expert_rows(k, other_rows, give.at[sums.give_slot(k)])
-        sums.give_core(k)
-        expert_rows(k, own_rows, keep.at[k])
-        if k:
-            sums.q_send(k - 1, q_buffer)
-        sums.add(k)
-
-    expert_chunk(0)
-    expert_chunk(1)
+    arrived(layer_near)
+    place_layer.wait()
+    siblings = [links.send(layer_all.at[c], layer_all.at[c], dc=1)]
 
     arrived(z_sum)
     normed_grad = part[0, at(z * HOME, HOME), :].astype(F32)
@@ -1036,9 +1198,6 @@
         links.send(sums_ref.at[lax.rem(x + d + 4, 4)], sums_x.at[k], dx=d)
         for k, d in enumerate((1, -1, 2))
     ]
-    expert_chunk(2)
-    expert_chunk(3)
-    sums.p_send()
 
     arrived(moe_two)
     arrivals = []
@@ -1069,13 +1228,9 @@
     attn_grad[slot] = (attn_grad[slot].astype(F32) + attn_one[1].astype(F32)).astype(BF)
     attn_next.append(links.send(pair_of(attn_grad, x_before), attn_two.at[1], dx=-1))
 
-    first, second = sums.home()
-    home_layer[...] = (hidden_ref[...] + jnp.concatenate([first, second], axis=0)).astype(BF)
-    place_layer = load(home_layer, layer_all.at[c, z])
-    layer_near = spread_home(links, layer_all, home_layer)
     arrived(input_near)
     place_in.wait()
-    siblings = [links.send(input_all.at[c], input_all.at[c], dc=1)]
+    siblings.append(links.send(input_all.at[c], input_all.at[c], dc=1))
 
     arrived(sum_x)
     pair_ref[...] = sums_ref[x] + sums_x[0] + sums_x[1] + sums_x[2]
@@ -1083,9 +1238,6 @@
         links.send(pair_ref.at[low_place], sums_y.at[k], dy=d)
         for k, (d, low_place) in enumerate(((1, 1 - y_low), (-1, 1 - y_low), (2, y_low)))
     ]
-    arrived(layer_near)
-    place_layer.wait()
-    siblings.append(links.send(layer_all.at[c], layer_all.at[c], dc=1))
     arrived(groups)
     for copy in place_groups:
         copy.wait()
@@ -1144,7 +1296,7 @@
         earlier.wait_send()
 
 
-BACK_COPIES = 2 + 1 + 1 + 3 + 2 + TOKEN_SUM_COPIES + 3 + 3 + 6 + 2 + 3 + 2 + 3 + 3 + 1 + 3
+BACK_COPIES = 2 + 1 + 1 + 3 + 2 + 3 + 3 + 6 + 2 + 3 + 2 + 3 + 3 + 1 + 3
 
 
 def run_back(hbm, vmem):
@@ -1181,8 +1333,6 @@
             buffer(ROWS, 512),
             buffer(2, ROWS, 128, kind=F32),
             buffer(ROWS, 512, kind=F32),
-            buffer(4, ROWS, 512),
-            buffer(4, 128, WIDTH),
             buffer(HOME, WIDTH),
             buffer(ROWS, ROWS, kind=F32),
             buffer(ROWS, 256),
@@ -1207,11 +1357,6 @@
             buffer(HALF, WIDTH),
             buffer(3, HOME, WIDTH),
             buffer(HOME, WIDTH),
-            buffer(HOME, WIDTH),
-            buffer(2, HALF, WIDTH),
-            buffer(4, HALF, WIDTH),
-            buffer(3, 32, WIDTH),
-            *scatter_buffers(),
             buffer(4, 2, 16, 256, kind=F32),
             buffer(3, 2, 16, 256, kind=F32),
             buffer(3, 16, 256, kind=F32),
@@ -1263,47 +1408,33 @@
     experts_count = gate_weight.shape[0]
     shard = lax.axis_index("shard")
 
-    lanes = jnp.zeros((4, 128), BF)
-    head_gains = jnp.concatenate([query_gain, key_gain], axis=0)
-    lanes = lax.dynamic_update_slice_in_dim(lanes, head_gains, shard * 16, 1)
-    gain_rows = jnp.zeros((16, WCOLS), BF)
-    gain_rows = gain_rows.at[0, :256].set(attn_gain).at[1, :256].set(moe_gain)
-    gain_rows = gain_rows.at[2:6, :128].set(lanes)
-    router_pad = jnp.pad(router_weight, ((0, 0), (0, 128 - experts_count)))
-    own_weights = jnp.concatenate(
-        [
-            jnp.concatenate([query_weight, key_weight, value_weight, router_pad, out_weight], axis=1),
-            gain_rows,
-        ],
-        axis=0,
-    )
     own_grad = out_grad.reshape(rows, width)
-    route_rows = routes.reshape(rows, -1)
-    own_picked = jnp.any(
-        route_rows[:, :, None] == jnp.arange(128, dtype=jnp.int32)[None, None, :], axis=1
-    ).astype(BF)
+    own_tokens = tokens.reshape(rows, width)
+    tables = [jnp.asarray(table) for table in turn_tables()]
     (
-        weights, experts_in, experts_out, grad_all, picked_all, moe_in_all,
+        weights, others, experts_in, experts_out, grad_all, picked_all, moe_in_all,
         normed, pre, rot, key_value, key_value_far, mixed, lse, hidden, home_scale,
     ) = run_front(
-        tokens.reshape(rows, width), own_weights, turn_tables(), segments,
-        gate_weight, up_weight, down_weight, own_grad, own_picked,
-    )
-    gated, grad_moe, grad_near, hidden_low, hidden_grad, gain_sum = run_experts(
-        moe_in_all, grad_all, picked_all, experts_in, experts_out, weights, hidden
-    )
-    tables = turn_tables()
+        [
+            own_tokens, router_weight, jnp.stack([attn_gain, moe_gain]), query_gain, key_gain, *tables,
+            segments, routes.reshape(rows, -1),
+        ],
+        [
+            query_weight, key_weight, value_weight, out_weight, gate_weight, up_weight, down_weight,
+            own_grad,
+        ],
+    )
+    grad_moe, grad_near, hidden_low, hidden_grad, gain_sum, layer_rows = run_experts(
+        moe_in_all, grad_all, picked_all, own_grad, experts_in, experts_out, weights, others, hidden
+    )
     (
         layer_all, input_all, groups_in, groups_out, _, grad_q, grad_k, grad_v, grad_o, small, heads,
     ) = run_back(
         [
-            grad_moe, grad_near, hidden_low.reshape(rows, width), weights, mixed, rot, key_value,
-            key_value_far, lse, pre, normed, gated, experts_out, tokens.reshape(rows, width),
+            grad_moe, grad_near, hidden_low.reshape(rows, width), weights, others, mixed, rot, key_value,
+            key_value_far, lse, pre, normed, own_tokens,
         ],
-        [
-            hidden, hidden_grad, home_scale, gain_sum, jnp.asarray(tables[0]), jnp.asarray(tables[1]),
-            segments.reshape(-1, 1), segments,
-        ],
+        [layer_rows, hidden_grad, home_scale, gain_sum, *tables, segments],
     )
     head_grads = lax.dynamic_slice_in_dim(heads[:4], shard * 16, 16, 1)
 

time: 400 us -> 356 us (0.89)
  the two profiles are of different devices: /device:TPU:14 before, /device:TPU:16 now
where the time goes in v5:
time: 356 us; the launch traced here: 350 us
  Pallas kernels  330 us (93%)
  local copies, waits for them, and re-layouts  14.4 us (4%)
  other arithmetic  4.83 us (1%)
    pallas_call x1, Pallas kernels, run_back(): pl.pallas_call(back, out_shape=[o for o, _ in outs], in_specs=[ANY] * len...  116 us
    pallas_call x1, Pallas kernels, run_front(): pl.pallas_call(front, out_shape=[o for o, _ in outs], in_specs=[VMEM] * l...  114 us
    pallas_call x1, Pallas kernels, run_experts(): pl.pallas_call(experts, out_shape=[o for o, _ in outs], in_specs=[ANY] *...  99.2 us
    unnamed x27, local copies, waits for them, and re-layouts  10.2 us

profile of v5, /device:TPU:16, one launch (start us, length us, event | category | flops | bytes accessed | tf_op | source)
XLA Modules:
  0.0 349.9 jit_solution(17713949146060483473)
XLA Ops:
  0.6 1.6 copy.32
  2.2 1.4 copy.33.router
  3.6 0.7 stack.10
  4.3 0.7 stack.9
  4.9 0.6 pad_maximum_fusion.gain_pair
  5.5 114.3 %front.1 = (bf16[4,2,272,768]{3,2,1,0:T(8,128)(2,1)}, bf16[4,2,256,384]{3,2,1,0:T(8,128)(2,1)}, bf16[4,4,2,256,256]{4,3,2,1,0:T(8,128)(2,1)}, bf16[4,128,2048]{2...) custom-call(bf16[512,2048]{1,0:T(8,128)(2,1)} %bitcast.21, ...), custom_call_target="tpu_custom_call" | custom-call | tf_op jit(solution)/shard_map/front/pallas_call | solution.py:559
  119.8 99.2 %experts.1 = (bf16[8,256,1664]{2,1,0:T(8,128)(2,1)}, bf16[2,256,1664]{2,1,0:T(8,128)(2,1)}, bf16[2,4,64,2048]{3,2,1,0:T(8,128)(2,1)}, f32[64,2048]{1,0:T(8,128)}...) custom-call(bf16[4,512,2048]{2,1,0:T(8,128)(2,1)} %bitcast.20, bf16[4,512,2048]{2,1,0:T(8,128)(2,1)} %get-tuple-element.47.g_all, ...), custom_call_target="tpu_custom_call" | custom-call | tf_op jit(solution)/shard_map/experts/pallas_call | solution.py:937
  219.1 116.1 %back.1 = (bf16[2,4,64,2048]{3,2,1,0:T(8,128)(2,1)}, bf16[2,4,64,2048]{3,2,1,0:T(8,128)(2,1)}, bf16[4,9,256,128]{3,2,1,0:T(8,128)(2,1)}, bf16[4,4,128,256]{3,2,1...) custom-call(bf16[8,256,1664]{2,1,0:T(8,128)(2,1)} %get-tuple-element, ...), custom_call_target="tpu_custom_call" | custom-call | tf_op jit(solution)/shard_map/back/pallas_call | solution.py:1321
  335.2 1.7 fusion
  336.9 0.0 copy-start.7
  336.9 0.0 copy-start.2
  336.9 2.6 bitcast_convert_fusion.1
  339.6 0.0 copy-start.8
  339.6 0.0 copy-start.1
  339.6 0.0 copy-done.7
  339.6 0.6 slice_bitcast_fusion
  340.2 0.0 copy-done.2
  340.2 1.6 bitcast_convert_fusion
  341.8 0.7 copy.34
  342.5 0.0 copy-done.8
  342.5 0.1 constant_dynamic-slice_fusion
  342.6 0.6 fusion.1
  343.1 0.0 copy-done.1
  343.2 0.0 copy-start
  343.2 1.3 copy.41
  344.5 1.0 copy-done
  345.5 0.0 copy-start.6
  345.5 0.0 copy-start.5
  345.5 0.0 copy-start.4
  345.5 0.0 copy-start.3
  345.5 1.3 copy.42
  346.8 0.0 copy-done.6
  346.8 0.7 copy.43
  347.5 0.0 copy-done.5
  347.5 0.7 copy.44
  348.2 0.0 copy-done.4
  348.2 0.7 copy.45
  349.0 0.0 copy-done.3
  349.0 0.7 copy.46
  (4 shorter events, 0.0 us)
Async XLA Ops:
  336.9 2.7 copy-start.7
  336.9 3.3 copy-start.2
  339.6 2.9 copy-start.8
  339.6 3.6 %copy-start.1 = (bf16[2,4,64,2048]{3,2,1,0:T(8,128)(2,1)S(1)}, bf16[2,4,64,2048]{3,2,1,0:T(8,128)(2,1)}, u32[]{:S(2)}) copy-start(bf16[2,4,64,2048]{3,2,1,0:T(8,128)(2,1)} %get-tuple-element.68) | copy-start | bytes 6291460
  343.2 2.3 copy-start
  345.5 1.3 copy-start.6
  345.5 2.0 copy-start.5
  345.5 2.7 copy-start.4
  345.5 3.4 copy-start.3
